TPU v7x, 512 devices: a whole 4x4x16 slice. The times are simulated.
512 devices in a mesh: row: 128 (over y, z, core), col: 4 (over x).
Axes of the slice: x: 4, y: 4, z: 16, core: 2. Of those that a mesh axis runs over, the one named last changes fastest.
Arguments:
- edge: bfloat16 [32768, 1536], P('row', 'col'), may hold values from -6 to 6
- corner: bfloat16 [1536, 1536], P(None, 'col'), may hold values from -0.15625 to 0.15625
- tri_inv: bfloat16 [1536, 1536], P(None, 'col'), as said below
- vector: float32 [32768, 1536], P('row', 'col'), may hold values from -6 to 6
Outputs:
- next_vector: float32 [32768, 1536], P('row', 'col')
- coeffs: float32 [2], replicated
Inputs may be any that keep to these rules, and one draw needn't show every extreme that they name: tri_inv is upper triangular; its diagonal lies between 1 and 2.
All inputs are finite; a program needn't handle non-finite values.
Results may differ from a plain program's by a relative error of at most 0.0075.
Values may be sent and summed in bfloat16 or wider, within the bound.
No kernel may reach another device: no remote copies, remote signals or barrier semaphores. Data moves between devices by JAX's collectives and lax.ppermute only.
A program may use at most 64 MiB of HBM per device.

v0:
```python
import jax
import jax.numpy as jnp
from jax import lax
from jax.sharding import PartitionSpec as P


def widen(block):
    return lax.all_gather(block, "col", axis=1, tiled=True)


def turn(block):
    return lax.all_to_all(block, "col", split_axis=0, concat_axis=0, tiled=True)


def tally(values):
    return lax.psum(values, ("row", "col"))


def rowwise(wide, stacked):
    width = stacked.shape[1]
    blocks = stacked.shape[0] // width
    left = wide.reshape(wide.shape[0], blocks, width)
    right = stacked.reshape(blocks, width, width)
    return jnp.einsum("rbk,bjk->rj", left, right, preferred_element_type=jnp.float32)


def on_device(edge, corner, tri_inv, vector):
    col_pos = lax.axis_index("col")
    width = corner.shape[1]
    bond = corner.shape[0]
    blocks = bond // width
    row_count = lax.axis_size("row")
    rows_total = vector.shape[0] * row_count
    half = jnp.dot(widen(edge), corner, preferred_element_type=jnp.float32).astype(jnp.bfloat16)
    proj = jnp.dot(widen(half), tri_inv, preferred_element_type=jnp.float32).astype(jnp.bfloat16)
    proj_wide = widen(proj)
    vec_low = vector.astype(jnp.bfloat16)
    partial_gram = lax.dot_general(
        proj_wide, vec_low, (((0,), (0,)), ((), ())), preferred_element_type=jnp.float32
    )
    gram = lax.psum(partial_gram, "row") / rows_total
    gram_low = gram.astype(jnp.bfloat16)
    mirror = turn(gram_low)
    flipped = mirror.reshape(blocks, width, width).transpose(0, 2, 1).reshape(bond, width)
    rows_index = lax.broadcasted_iota(jnp.int32, (bond, width), 0)
    cols_index = lax.broadcasted_iota(jnp.int32, (bond, width), 1) + col_pos * width
    sym = jnp.where(rows_index >= cols_index, gram_low, flipped)
    corrected = (vector - jnp.dot(proj_wide, sym, preferred_element_type=jnp.float32)).astype(
        jnp.bfloat16
    )
    dhalf = rowwise(widen(corrected), turn(tri_inv)).astype(jnp.bfloat16)
    dedge = rowwise(widen(dhalf), turn(corner))
    image = vector - dedge
    count = float(rows_total * bond)
    along = tally(jnp.sum(vector * image)) / count
    resid = image - along * vector
    spread = tally(jnp.sum(resid * resid)) / count
    scale = jnp.sqrt(spread + 1e-06)
    return (resid / scale, jnp.stack([along, scale]))


def solution(mesh):
    in_specs = (P("row", "col"), P(None, "col"), P(None, "col"), P("row", "col"))
    out_specs = (P("row", "col"), P())
    return jax.shard_map(
        on_device, mesh=mesh, in_specs=in_specs, out_specs=out_specs, check_vma=False
    )
```

profile of v0, /device:TPU:1, one launch (start us, length us, event | category | flops | bytes accessed | tf_op | source)
XLA Modules:
  0.0 692.4 jit_solution(12492011397853342699)
XLA Ops:
  7.2 0.0 all-reduce.2.cloned.1.call-start
  7.2 13.1 %all_gather.15 = bf16[256,1536]{1,0:T(8,128)(2,1)S(1)} all-gather(bf16[256,384]{1,0:T(8,128)(2,1)} %param.4), channel_id=1, replica_groups=mesh['row'=128,'col'=4] {'col'}, dimensions={1}, use_global_device_ids=true | all-gather | bytes 983040 | tf_op jit(solution)/shard_map/all_gather | solution.py:8
  20.4 1.8 convolution_convert_fusion.1
  22.2 12.0 %all_gather.16 = bf16[256,1536]{1,0:T(8,128)(2,1)S(1)} all-gather(bf16[256,384]{1,0:T(8,128)(2,1)S(1)} %convolution_convert_fusion.1), channel_id=1, replica_groups=mesh['row'=128,'col'=4] {'col'}, dimensions={1}, use_global_device_ids=true | all-gather | bytes 983040 | tf_op jit(solution)/shard_map/all_gather | solution.py:8
  34.3 1.9 convolution_convert_fusion
  36.1 10.8 %all_gather.17 = bf16[256,1536]{1,0:T(8,128)(2,1)S(1)} all-gather(bf16[256,384]{1,0:T(8,128)(2,1)S(1)} %convolution_convert_fusion), channel_id=1, replica_groups=mesh['row'=128,'col'=4] {'col'}, dimensions={1}, use_global_device_ids=true | all-gather | bytes 983040 | tf_op jit(solution)/shard_map/all_gather | solution.py:8
  46.9 2.0 fusion.12
  48.9 3.5 all-to-all-start.1
  52.5 357.4 %all-reduce.2.cloned.1.call-done = f32[1536,384]{1,0:T(8,128)} async-done(((f32[1536,384]{1,0:T(8,128)}), f32[1536,384]{1,0:T(8,128)}) %all-reduce.2.cloned.1.call-update) | async-done | bytes 2359312 | tf_op jit(solution)/shard_map/psum | solution.py:41
  409.9 1.9 multiply_convert_fusion
  411.7 1.5 copy.6
  413.2 4.3 all-to-all-start
  417.5 16.0 %all-to-all-done = bf16[4,384,384]{1,2,0:T(8,128)(2,1)} async-done(((bf16[4,384,384]{1,2,0:T(8,128)(2,1)}), bf16[4,384,384]{1,2,0:T(8,128)(2,1)}, u32[]{:S(2)}, u32[]{:S(2)}) %all-to-all-start) | async-done | bytes 1179680 | tf_op jit(solution)/shard_map/all_to_all | solution.py:12
  433.5 4.3 all-to-all-start.2
  437.7 1.9 fusion.4
  439.6 20.9 %all_gather.18 = bf16[256,1536]{1,0:T(8,128)(2,1)S(1)} all-gather(bf16[256,384]{1,0:T(8,128)(2,1)S(1)} %fusion.4), channel_id=1, replica_groups=mesh['row'=128,'col'=4] {'col'}, dimensions={1}, use_global_device_ids=true | all-gather | bytes 983040 | tf_op jit(solution)/shard_map/all_gather | solution.py:8
  460.5 0.6 fusion.7
  461.1 12.0 %all_gather.19 = bf16[256,1536]{1,0:T(8,128)(2,1)S(1)} all-gather(bf16[256,384]{1,0:T(8,128)(2,1)S(1)} %fusion.7), channel_id=1, replica_groups=mesh['row'=128,'col'=4] {'col'}, dimensions={1}, use_global_device_ids=true | all-gather | bytes 983040 | tf_op jit(solution)/shard_map/all_gather | solution.py:8
  473.1 2.5 multiply_reduce_fusion.1
  475.6 107.4 %psum.22 = f32[]{:T(128)} all-reduce(f32[]{:T(128)} %get-tuple-element.2), channel_id=1, replica_groups=mesh['row'=128,'col'=4] {'row','col'}, use_global_device_ids=true, to_apply=%region_2.3 | all-reduce | flops 1 | bytes 8 | tf_op jit(solution)/shard_map/psum | solution.py:16
  583.7 0.7 multiply_reduce_fusion
  584.4 99.1 %psum.23 = f32[]{:T(128)} all-reduce(f32[]{:T(128)} %multiply_reduce_fusion), channel_id=1, replica_groups=mesh['row'=128,'col'=4] {'row','col'}, use_global_device_ids=true, to_apply=%region_4.5 | all-reduce | flops 1 | bytes 8 | tf_op jit(solution)/shard_map/psum | solution.py:16
  684.2 0.8 broadcast_divide_fusion
  685.0 0.6 pad_maximum_fusion
  (6 shorter events, 0.0 us)
Async XLA Ops:
  7.2 402.7 %all-reduce.2.cloned.1.call-start = ((), (), s32[]{:S(2)}) async-start(), calls=%async_computation.3 | async-start | bytes 4718592 | tf_op jit(solution)/shard_map/psum | solution.py:41
  34.2 12.7 %copy-start = (f32[256,384]{1,0:T(8,128)S(1)}, f32[256,384]{1,0:T(8,128)}, u32[]{:S(2)}) copy-start(f32[256,384]{1,0:T(8,128)} %param.7) | copy-start | bytes 1179652
  48.9 364.3 %all-to-all-start.1 = ((bf16[4,384,384]{2,1,0:T(8,128)(2,1)}), bf16[4,384,384]{2,1,0:T(8,128)(2,1)S(1)}, u32[]{:S(2)}, u32[]{:S(2)}) async-start(bf16[4,384,384]{2,1,0:T(8,128)(2,1)} %bitcast.3), calls=%async_computation.1 | async-start | bytes 2359296 | tf_op jit(solution)/shard_map/all_to_all | solution.py:12
  413.2 20.3 %all-to-all-start = ((bf16[4,384,384]{1,2,0:T(8,128)(2,1)}), bf16[4,384,384]{1,2,0:T(8,128)(2,1)}, u32[]{:S(2)}, u32[]{:S(2)}) async-start(bf16[4,384,384]{1,2,0:T(8,128)(2,1)} %copy.6), calls=%async_computation | async-start | bytes 2359296 | tf_op jit(solution)/shard_map/all_to_all | solution.py:12
  433.5 39.6 %all-to-all-start.2 = ((bf16[4,384,384]{2,1,0:T(8,128)(2,1)}), bf16[4,384,384]{2,1,0:T(8,128)(2,1)}, u32[]{:S(2)}, u32[]{:S(2)}) async-start(bf16[4,384,384]{2,1,0:T(8,128)(2,1)} %bitcast.5), calls=%async_computation.2 | async-start | bytes 2359296 | tf_op jit(solution)/shard_map/all_to_all | solution.py:12
Sparse Core Ops, SparseCore 0:
  49.1 360.7 all-reduce.1
where the time goes:
time: 693 us; the launch traced here: 692 us
  waiting for transfers between devices  373 us (54%)
  blocking collectives  275 us (40%)
  between operations  15.4 us (2%)
  starting transfers between devices  12.1 us (2%)
  matrix products  10.7 us (2%)
    psum x1, waiting for transfers between devices, on_device(): gram = lax.psum(partial_gram, 'row') / rows_total  357 us
    psum x2, blocking collectives, tally(): return lax.psum(values, ('row', 'col'))  207 us
    all_gather x5, blocking collectives, widen(): return lax.all_gather(block, 'col', axis=1, tiled=True)  68.8 us
    all_to_all x3, waiting for transfers between devices, turn(): return lax.all_to_all(block, 'col', split_axis=0, concat_axis=0, tiled=True)  16 us
  transfers between devices with their start and end apart: 4, of which 2 were waited for; matrix products, arithmetic and copies ran while one was open for 1% of the time, Pallas kernels for 0%

commit v1 on v0

v1 whole, which is shorter than its diff:
```python
import jax
import jax.numpy as jnp
from jax import lax
from jax.sharding import Mesh, PartitionSpec as P

BF16 = jnp.bfloat16
F32 = jnp.float32
ROW = ("y", "zh", "zl", "core")


def swap(pieces, axis):
    return lax.all_to_all(pieces, axis, split_axis=0, concat_axis=0, tiled=True)


def spread(block, axis):
    members = lax.axis_size(axis)
    return swap(jnp.broadcast_to(block[None], (members, *block.shape)), axis)


def total(pieces):
    return jnp.sum(pieces.astype(F32), axis=0)


def scatter_sum(block, axis):
    members = lax.axis_size(axis)
    pieces = block.reshape(members, block.shape[0] // members, block.shape[1])
    return total(swap(pieces, axis))


def join_rows(blocks, axis):
    stacked = spread(blocks, axis)
    members, count, rows, width = stacked.shape
    return stacked.transpose(1, 0, 2, 3).reshape(count, members * rows, width)


def whole_map(corner, tri_inv):
    bond, width = corner.shape
    blocks = bond // width
    half = bond // 2
    start = lax.axis_index("core") * half
    both = jnp.stack(
        [
            lax.dynamic_slice_in_dim(corner, start, half, 0),
            lax.dynamic_slice_in_dim(tri_inv, start, half, 0),
        ]
    )
    wide = spread(both, "x")
    corner_half = wide[:, 0]
    tri = spread(wide[:, 1], "core")
    tri = tri.transpose(1, 0, 2, 3).reshape(blocks, bond, width)
    corner_half = corner_half.transpose(1, 0, 2).reshape(half, bond)
    columns = [
        jnp.dot(
            corner_half[:, : (b + 1) * width],
            tri[b, : (b + 1) * width],
            preferred_element_type=F32,
        ).astype(BF16)
        for b in range(blocks)
    ]
    mine = jnp.concatenate(columns, axis=1)
    return spread(mine, "core").reshape(bond, bond)


def on_device(edge, corner, tri_inv, vector):
    bond, width = corner.shape
    blocks = bond // width
    place = lax.axis_index("x")
    row_devices = lax.axis_size(ROW)
    rows_total = vector.shape[0] * row_devices

    edge_wide = lax.all_gather(edge, "x", axis=1, tiled=True)
    vec_low = vector.astype(BF16)
    cross = lax.dot_general(
        vec_low, edge_wide, (((0,), (0,)), ((), ())), preferred_element_type=F32
    )
    for axis in ("core", "y", "zl"):
        cross = scatter_sum(cross.astype(BF16), axis)
    cross = total(spread(cross.astype(BF16), "zh")) / rows_total

    full_map = whole_map(corner, tri_inv)
    proj_wide = jnp.dot(edge_wide, full_map, preferred_element_type=F32).astype(BF16)

    gram_t = jnp.dot(cross.astype(BF16), full_map, preferred_element_type=F32)
    own = gram_t.astype(BF16).reshape(-1, blocks, width).transpose(1, 0, 2)
    other = swap(own, "x")
    block_id = lax.broadcasted_iota(jnp.int32, own.shape, 0)
    chosen = jnp.where(block_id < place, other, own)
    for axis in ("zl", "y", "core"):
        chosen = join_rows(chosen, axis)
    block_id = lax.broadcasted_iota(jnp.int32, chosen.shape, 0)
    first = lax.broadcasted_iota(jnp.int32, chosen.shape, 1)
    second = lax.broadcasted_iota(jnp.int32, chosen.shape, 2)
    diagonal = block_id == place
    zero = jnp.zeros_like(chosen)
    straight = jnp.where((block_id < place) | (diagonal & (first <= second)), chosen, zero)
    turned = jnp.where((block_id > place) | (diagonal & (first < second)), chosen, zero)
    product = jnp.dot(
        proj_wide, straight.reshape(bond, width), preferred_element_type=F32
    ) + jnp.einsum(
        "rbk,bjk->rj",
        proj_wide.reshape(-1, blocks, width),
        turned,
        preferred_element_type=F32,
    )
    corrected = (vector - product).astype(BF16)
    corrected_wide = lax.all_gather(corrected, "x", axis=1, tiled=True)
    map_rows = lax.dynamic_slice_in_dim(full_map, place * width, width, 0)
    dedge = lax.dot_general(
        corrected_wide, map_rows, (((1,), (1,)), ((), ())), preferred_element_type=F32
    )

    sums = jnp.stack(
        [jnp.sum(vector * vector), jnp.sum(vector * dedge), jnp.sum(dedge * dedge)]
    )
    for axis in ("core", "x", "y", "zl", "zh"):
        sums = lax.psum(sums, axis)
    count = float(rows_total * bond)
    along = (sums[0] - sums[1]) / count
    keep = 1.0 - along
    spread_sq = (keep * keep * sums[0] - 2.0 * keep * sums[1] + sums[2]) / count
    scale = jnp.sqrt(jnp.maximum(spread_sq, 0.0) + 1e-06)
    return ((keep * vector - dedge) / scale, jnp.stack([along, scale]))


def solution(mesh):
    fine = Mesh(mesh.devices.reshape(4, 4, -1, 2, mesh.shape["col"]), ROW + ("x",))
    in_specs = (P(ROW, "x"), P(None, "x"), P(None, "x"), P(ROW, "x"))
    out_specs = (P(ROW, "x"), P())
    return jax.shard_map(
        on_device, mesh=fine, in_specs=in_specs, out_specs=out_specs, check_vma=False
    )
```

time: 693 us -> 281 us (0.41)
  the two profiles are of different devices: /device:TPU:1 before, /device:TPU:2 now
where the time goes in v1:
time: 281 us; the launch traced here: 280 us
  blocking collectives  127 us (45%)
  waiting for transfers between devices  75.9 us (27%)
  starting transfers between devices  28.6 us (10%)
  local copies, waits for them, and re-layouts  24.1 us (9%)
  matrix products  13.7 us (5%)
  other arithmetic  6.05 us (2%)
  between operations  4 us (1%)
    all_to_all x5, waiting for transfers between devices, swap(): return lax.all_to_all(pieces, axis, split_axis=0, concat_axis=0, tiled=True)  75.9 us
    all_to_all x6, blocking collectives, swap(): return lax.all_to_all(pieces, axis, split_axis=0, concat_axis=0, tiled=True)  50 us
    psum x5, blocking collectives, on_device(): sums = lax.psum(sums, axis)  46.2 us
    all_to_all x5, starting transfers between devices, swap(): return lax.all_to_all(pieces, axis, split_axis=0, concat_axis=0, tiled=True)  28.6 us
    all_gather x1, blocking collectives, on_device(): edge_wide = lax.all_gather(edge, 'x', axis=1, tiled=True)  16.9 us
    all_gather x1, blocking collectives, on_device(): corrected_wide = lax.all_gather(corrected, 'x', axis=1, tiled=True)  14.1 us
    broadcast_in_dim x10, local copies, waits for them, and re-layouts, spread(): return swap(jnp.broadcast_to(block[None], (members, *block.shape)), axis)  13.4 us
  transfers between devices with their start and end apart: 5, of which 5 were waited for; matrix products, arithmetic and copies ran while one was open for 2% of the time, Pallas kernels for 0%

profile of v1, /device:TPU:2, one launch (start us, length us, event | category | flops | bytes accessed | tf_op | source)
XLA Modules:
  0.0 279.6 jit_solution(7348774244752112228)
XLA Ops:
  0.6 16.9 %all_gather.6 = bf16[256,1536]{1,0:T(8,128)(2,1)S(1)} all-gather(bf16[256,384]{1,0:T(8,128)(2,1)} %param.4), channel_id=1, replica_groups=mesh['y'=4,'zh'=4,'zl'=4,'core'=2,'x'=4] {'x'}, dimensions={1}, use_global_device_ids=true | all-gather | bytes 983040 | tf_op jit(solution)/shard_map/all_gather | solution.py:71
  19.1 4.7 %all_to_all.55 = bf16[2,192,1536]{2,1,0:T(8,128)(2,1)S(1)} all-to-all(bf16[2,192,1536]{2,1,0:T(8,128)(2,1)S(1)} %bitcast.77), channel_id=1, replica_groups=mesh['y'=4,'zh'=4,'zl'=4,'core'=2,'x'=4] {'core'}, dimensions={0} | all-to-all | bytes 2359296 | tf_op jit(solution)/shard_map/all_to_all | solution.py:12
  24.0 13.1 %all_to_all.56 = bf16[4,48,1536]{2,1,0:T(8,128)(2,1)S(1)} all-to-all(bf16[4,48,1536]{2,1,0:T(8,128)(2,1)S(1)} %bitcast.79), channel_id=1, replica_groups=mesh['y'=4,'zh'=4,'zl'=4,'core'=2,'x'=4] {'y'}, dimensions={0} | all-to-all | bytes 1179648 | tf_op jit(solution)/shard_map/all_to_all | solution.py:12
  37.3 12.4 %all_to_all.57 = bf16[4,12,1536]{2,1,0:T(8,128)(2,1)S(1)} all-to-all(bf16[4,12,1536]{2,1,0:T(8,128)(2,1)S(1)} %reshape.54), channel_id=1, replica_groups=mesh['y'=4,'zh'=4,'zl'=4,'core'=2,'x'=4] {'zl'}, dimensions={0} | all-to-all | bytes 294912 | tf_op jit(solution)/shard_map/all_to_all | solution.py:12
  50.5 12.4 %all-to-all-start.6 = ((bf16[4,12,1536]{2,1,0:T(8,128)(2,1)}), bf16[4,12,1536]{2,1,0:T(8,128)(2,1)S(1)}, u32[]{:S(2)}, u32[]{:S(2)}) async-start(bf16[4,12,1536]{2,1,0:T(8,128)(2,1)} %broadcast_in_dim.54), calls=%async_computation.6 | async-start | bytes 393216 | tf_op jit(solution)/shard_map/all_to_all | solution.py:12
  65.0 13.7 %all-to-all-done.6 = bf16[4,12,1536]{2,1,0:T(8,128)(2,1)S(1)} async-done(((bf16[4,12,1536]{2,1,0:T(8,128)(2,1)}), bf16[4,12,1536]{2,1,0:T(8,128)(2,1)S(1)}, u32[]{:S(2)}, u32[]{:S(2)}) %all-to-all-start.6) | async-done | bytes 147488 | tf_op jit(solution)/shard_map/all_to_all | solution.py:12
  81.2 5.0 %all-to-all-start = ((bf16[4,2,768,384]{2,3,1,0:T(8,128)(2,1)}), bf16[4,2,768,384]{2,3,1,0:T(8,128)(2,1)}, u32[]{:S(2)}, u32[]{:S(2)}) async-start(bf16[4,2,768,384]{2,3,1,0:T(8,128)(2,1)} %broadcast_in_dim.24), calls=%async_computation | async-start | bytes 9437184 | tf_op jit(solution)/shard_map/all_to_all | solution.py:12
  86.2 47.8 %all-to-all-done = bf16[4,2,768,384]{2,3,1,0:T(8,128)(2,1)} async-done(((bf16[4,2,768,384]{2,3,1,0:T(8,128)(2,1)}), bf16[4,2,768,384]{2,3,1,0:T(8,128)(2,1)}, u32[]{:S(2)}, u32[]{:S(2)}) %all-to-all-start) | async-done | bytes 4718624 | tf_op jit(solution)/shard_map/all_to_all | solution.py:12
  134.0 4.8 %slice_bitcast_fusion = (bf16[4,768,384]{1,2,0:T(8,128)(2,1)}, bf16[4,1,768,384]{2,3,1,0:T(8,128)(2,1)}) fusion(bf16[4,2,768,384]{2,3,1,0:T(8,128)(2,1)} %all-to-all-done), kind=kLoop, calls=%fused_computation.2 | loop fusion | bytes 9437184 | tf_op jit(solution)/shard_map/broadcast_in_dim | solution.py:17
  142.3 7.5 %all_to_all.58 = bf16[2,4,768,384]{3,2,1,0:T(8,128)(2,1)S(1)} all-to-all(bf16[2,4,768,384]{3,2,1,0:T(8,128)(2,1)S(1)} %broadcast_in_dim.52), channel_id=1, replica_groups=mesh['y'=4,'zh'=4,'zl'=4,'core'=2,'x'=4] {'core'}, dimensions={0} | all-to-all | bytes 9437184 | tf_op jit(solution)/shard_map/all_to_all | solution.py:12
  159.7 7.5 %all_to_all.59 = bf16[2,768,1536]{2,1,0:T(8,128)(2,1)S(1)} all-to-all(bf16[2,768,1536]{2,1,0:T(8,128)(2,1)S(1)} %broadcast_in_dim.53), channel_id=1, replica_groups=mesh['y'=4,'zh'=4,'zl'=4,'core'=2,'x'=4] {'core'}, dimensions={0} | all-to-all | bytes 9437184 | tf_op jit(solution)/shard_map/all_to_all | solution.py:12
  170.7 4.4 %all-to-all-start.7 = ((bf16[4,12,384]{2,1,0:T(8,128)(2,1)}), bf16[4,12,384]{2,1,0:T(8,128)(2,1)S(1)}, u32[]{:S(2)}, u32[]{:S(2)}) async-start(bf16[4,12,384]{2,1,0:T(8,128)(2,1)} %bitcast.68), calls=%async_computation.7 | async-start | bytes 98304 | tf_op jit(solution)/shard_map/all_to_all | solution.py:12
  175.2 4.1 %all-to-all-done.7 = bf16[4,12,384]{2,1,0:T(8,128)(2,1)S(1)} async-done(((bf16[4,12,384]{2,1,0:T(8,128)(2,1)}), bf16[4,12,384]{2,1,0:T(8,128)(2,1)S(1)}, u32[]{:S(2)}, u32[]{:S(2)}) %all-to-all-start.7) | async-done | bytes 36896 | tf_op jit(solution)/shard_map/all_to_all | solution.py:12
  180.0 3.3 %all-to-all-start.8 = ((bf16[4,4,12,384]{3,1,2,0:T(4,128)(2,1)}), bf16[4,4,12,384]{3,1,2,0:T(4,128)(2,1)S(1)}, u32[]{:S(2)}, u32[]{:S(2)}) async-start(bf16[4,4,12,384]{3,1,2,0:T(4,128)(2,1)} %broadcast_in_dim.55), calls=%async_computation.8 | async-start | bytes 294912 | tf_op jit(solution)/shard_map/all_to_all | solution.py:12
  183.6 5.7 %all-to-all-done.8 = bf16[4,4,12,384]{3,1,2,0:T(4,128)(2,1)S(1)} async-done(((bf16[4,4,12,384]{3,1,2,0:T(4,128)(2,1)}), bf16[4,4,12,384]{3,1,2,0:T(4,128)(2,1)S(1)}, u32[]{:S(2)}, u32[]{:S(2)}) %all-to-all-start.8) | async-done | bytes 147488 | tf_op jit(solution)/shard_map/all_to_all | solution.py:12
  190.2 3.5 %all-to-all-start.9 = ((bf16[4,4,48,384]{3,2,1,0:T(8,128)(2,1)}), bf16[4,4,48,384]{3,2,1,0:T(8,128)(2,1)S(1)}, u32[]{:S(2)}, u32[]{:S(2)}) async-start(bf16[4,4,48,384]{3,2,1,0:T(8,128)(2,1)} %broadcast_in_dim.57), calls=%async_computation.9 | async-start | bytes 1179648 | tf_op jit(solution)/shard_map/all_to_all | solution.py:12
  193.7 3.8 %convolution_convert_fusion.1 = bf16[1536,256]{1,0:T(8,128)(2,1)S(1)} fusion(bf16[1536,1536]{1,0:T(8,128)(2,1)} %bitcast.70, bf16[256,1536]{1,0:T(8,128)(2,1)S(1)} %all_gather.6), kind=kOutput, calls=%fused_computation.1 | convolution fusion | flops 1208352768 | bytes 6291456 | tf_op jit(solution)/shard_map/dot_general | solution.py:81
  197.5 4.7 %all-to-all-done.9 = bf16[4,4,48,384]{3,2,1,0:T(8,128)(2,1)S(1)} async-done(((bf16[4,4,48,384]{3,2,1,0:T(8,128)(2,1)}), bf16[4,4,48,384]{3,2,1,0:T(8,128)(2,1)S(1)}, u32[]{:S(2)}, u32[]{:S(2)}) %all-to-all-start.9) | async-done | bytes 589856 | tf_op jit(solution)/shard_map/all_to_all | solution.py:12
  202.3 4.7 %all_to_all.60 = bf16[2,4,192,384]{3,2,1,0:T(8,128)(2,1)S(1)} all-to-all(bf16[2,4,192,384]{3,2,1,0:T(8,128)(2,1)S(1)} %broadcast_in_dim.59), channel_id=1, replica_groups=mesh['y'=4,'zh'=4,'zl'=4,'core'=2,'x'=4] {'core'}, dimensions={0} | all-to-all | bytes 2359296 | tf_op jit(solution)/shard_map/all_to_all | solution.py:12
  209.8 14.1 %all_gather.7 = bf16[256,1536]{1,0:T(8,128)(2,1)S(1)} all-gather(bf16[256,384]{1,0:T(8,128)(2,1)S(1)} %fusion.19), channel_id=1, replica_groups=mesh['y'=4,'zh'=4,'zl'=4,'core'=2,'x'=4] {'x'}, dimensions={1}, use_global_device_ids=true | all-gather | bytes 983040 | tf_op jit(solution)/shard_map/all_gather | solution.py:106
  230.7 10.2 %psum.36 = f32[3]{0:T(128)S(1)} all-reduce(f32[3]{0:T(128)S(1)} %psum.35), channel_id=1, replica_groups=mesh['y'=4,'zh'=4,'zl'=4,'core'=2,'x'=4] {'x'}, use_global_device_ids=true, to_apply=%region_8.9 | all-reduce | flops 3 | bytes 24 | tf_op jit(solution)/shard_map/psum | solution.py:116
  240.9 8.9 %psum.37 = f32[3]{0:T(128)S(1)} all-reduce(f32[3]{0:T(128)S(1)} %psum.36), channel_id=1, replica_groups=mesh['y'=4,'zh'=4,'zl'=4,'core'=2,'x'=4] {'y'}, use_global_device_ids=true, to_apply=%region_9.10 | all-reduce | flops 3 | bytes 24 | tf_op jit(solution)/shard_map/psum | solution.py:116
  249.8 10.2 %psum.38 = f32[3]{0:T(128)S(1)} all-reduce(f32[3]{0:T(128)S(1)} %psum.37), channel_id=1, replica_groups=mesh['y'=4,'zh'=4,'zl'=4,'core'=2,'x'=4] {'zl'}, use_global_device_ids=true, to_apply=%region_10.11 | all-reduce | flops 3 | bytes 24 | tf_op jit(solution)/shard_map/psum | solution.py:116
  260.0 14.5 %psum.39 = f32[3]{0:T(128)S(1)} all-reduce(f32[3]{0:T(128)S(1)} %psum.38), channel_id=1, replica_groups=mesh['y'=4,'zh'=4,'zl'=4,'core'=2,'x'=4] {'zh'}, use_global_device_ids=true, to_apply=%region_11.12 | all-reduce | flops 3 | bytes 24 | tf_op jit(solution)/shard_map/psum | solution.py:116
  (57 shorter events, 37.7 us)
Async XLA Ops:
  50.5 28.2 %all-to-all-start.6 = ((bf16[4,12,1536]{2,1,0:T(8,128)(2,1)}), bf16[4,12,1536]{2,1,0:T(8,128)(2,1)S(1)}, u32[]{:S(2)}, u32[]{:S(2)}) async-start(bf16[4,12,1536]{2,1,0:T(8,128)(2,1)} %broadcast_in_dim.54), calls=%async_computation.6 | async-start | bytes 393216 | tf_op jit(solution)/shard_map/all_to_all | solution.py:12
  81.2 52.8 %all-to-all-start = ((bf16[4,2,768,384]{2,3,1,0:T(8,128)(2,1)}), bf16[4,2,768,384]{2,3,1,0:T(8,128)(2,1)}, u32[]{:S(2)}, u32[]{:S(2)}) async-start(bf16[4,2,768,384]{2,3,1,0:T(8,128)(2,1)} %broadcast_in_dim.24), calls=%async_computation | async-start | bytes 9437184 | tf_op jit(solution)/shard_map/all_to_all | solution.py:12
  149.8 1.7 copy-start.2
  167.2 2.1 copy-start
  170.7 8.5 %all-to-all-start.7 = ((bf16[4,12,384]{2,1,0:T(8,128)(2,1)}), bf16[4,12,384]{2,1,0:T(8,128)(2,1)S(1)}, u32[]{:S(2)}, u32[]{:S(2)}) async-start(bf16[4,12,384]{2,1,0:T(8,128)(2,1)} %bitcast.68), calls=%async_computation.7 | async-start | bytes 98304 | tf_op jit(solution)/shard_map/all_to_all | solution.py:12
  180.0 9.3 %all-to-all-start.8 = ((bf16[4,4,12,384]{3,1,2,0:T(4,128)(2,1)}), bf16[4,4,12,384]{3,1,2,0:T(4,128)(2,1)S(1)}, u32[]{:S(2)}, u32[]{:S(2)}) async-start(bf16[4,4,12,384]{3,1,2,0:T(4,128)(2,1)} %broadcast_in_dim.55), calls=%async_computation.8 | async-start | bytes 294912 | tf_op jit(solution)/shard_map/all_to_all | solution.py:12
  190.2 11.9 %all-to-all-start.9 = ((bf16[4,4,48,384]{3,2,1,0:T(8,128)(2,1)}), bf16[4,4,48,384]{3,2,1,0:T(8,128)(2,1)S(1)}, u32[]{:S(2)}, u32[]{:S(2)}) async-start(bf16[4,4,48,384]{3,2,1,0:T(8,128)(2,1)} %broadcast_in_dim.57), calls=%async_computation.9 | async-start | bytes 1179648 | tf_op jit(solution)/shard_map/all_to_all | solution.py:12
  207.6 1.0 copy-start.1

commit v2 on v1

v2 whole, which is shorter than its diff:
```python
import jax
import jax.numpy as jnp
from jax import lax
from jax.sharding import Mesh, PartitionSpec as P

BF16 = jnp.bfloat16
F32 = jnp.float32
ROW = ("y", "zh", "zl", "core")


def swap(pieces, axis):
    return lax.all_to_all(pieces, axis, split_axis=0, concat_axis=0, tiled=True)


def spread(block, axis):
    members = lax.axis_size(axis)
    return swap(jnp.broadcast_to(block[None], (members, *block.shape)), axis)


def total(pieces):
    return jnp.sum(pieces.astype(F32), axis=0)


def scatter_sum(block, axis):
    members = lax.axis_size(axis)
    pieces = block.reshape(members, block.shape[0] // members, block.shape[1])
    return total(swap(pieces, axis))


def join_rows(blocks, axis):
    stacked = spread(blocks, axis)
    members, count, rows, width = stacked.shape
    return stacked.transpose(1, 0, 2, 3).reshape(count, members * rows, width)


def on_device(edge, corner, tri_inv, vector):
    bond, width = corner.shape
    blocks = bond // width
    place = lax.axis_index("x")
    row_devices = lax.axis_size(ROW)
    rows_total = vector.shape[0] * row_devices

    edge_wide = lax.all_gather(edge, "x", axis=1, tiled=True)
    edge_wide, corner = lax.optimization_barrier((edge_wide, corner))
    corner_wide = lax.all_gather(corner, "x", axis=1, tiled=True)
    vec_low = vector.astype(BF16)
    cross = lax.dot_general(
        vec_low, edge_wide, (((0,), (0,)), ((), ())), preferred_element_type=F32
    )
    for axis in ("core", "y", "zl"):
        cross = scatter_sum(cross.astype(BF16), axis)
    cross = total(spread(cross.astype(BF16), "zh")) / rows_total
    cross_all = spread(cross.astype(BF16), "x").reshape(-1, bond)

    own_map = jnp.dot(corner_wide, tri_inv, preferred_element_type=F32).astype(BF16)
    proj = jnp.dot(edge_wide, own_map, preferred_element_type=F32).astype(BF16)

    other = jnp.dot(cross_all, own_map, preferred_element_type=F32).astype(BF16)
    other = other.reshape(blocks, -1, width)
    own = swap(other, "x")
    block_id = lax.broadcasted_iota(jnp.int32, own.shape, 0)
    chosen = jnp.where(block_id < place, other, own)
    late = jnp.concatenate(
        [
            jnp.broadcast_to(proj[None], (blocks, *proj.shape)),
            own_map.reshape(blocks, width, width),
        ],
        axis=1,
    )
    late, chosen = lax.optimization_barrier((late, chosen))
    late = swap(late, "x")
    proj_blocks, map_blocks = late[:, : proj.shape[0]], late[:, proj.shape[0] :]
    for axis in ("zl", "y", "core"):
        chosen = join_rows(chosen, axis)
    block_id = lax.broadcasted_iota(jnp.int32, chosen.shape, 0)
    first = lax.broadcasted_iota(jnp.int32, chosen.shape, 1)
    second = lax.broadcasted_iota(jnp.int32, chosen.shape, 2)
    diagonal = block_id == place
    zero = jnp.zeros_like(chosen)
    straight = jnp.where((block_id < place) | (diagonal & (first <= second)), chosen, zero)
    turned = jnp.where((block_id > place) | (diagonal & (first < second)), chosen, zero)
    product = sum(
        jnp.dot(proj_blocks[k], straight[k], preferred_element_type=F32)
        + lax.dot_general(
            proj_blocks[k], turned[k], (((1,), (1,)), ((), ())), preferred_element_type=F32
        )
        for k in range(blocks)
    )
    corrected = (vector - product).astype(BF16)
    corrected_wide = lax.all_gather(corrected, "x", axis=1, tiled=True)
    dedge = sum(
        lax.dot_general(
            corrected_wide[:, k * width : (k + 1) * width],
            map_blocks[k],
            (((1,), (1,)), ((), ())),
            preferred_element_type=F32,
        )
        for k in range(blocks)
    )

    sums = jnp.stack(
        [jnp.sum(vector * vector), jnp.sum(vector * dedge), jnp.sum(dedge * dedge)]
    )
    for axis in ("core", "x", "y", "zl", "zh"):
        sums = lax.psum(sums, axis)
    count = float(rows_total * bond)
    along = (sums[0] - sums[1]) / count
    keep = 1.0 - along
    spread_sq = (keep * keep * sums[0] - 2.0 * keep * sums[1] + sums[2]) / count
    scale = jnp.sqrt(jnp.maximum(spread_sq, 0.0) + 1e-06)
    return ((keep * vector - dedge) / scale, jnp.stack([along, scale]))


def solution(mesh):
    fine = Mesh(mesh.devices.reshape(4, 4, -1, 2, mesh.shape["col"]), ROW + ("x",))
    in_specs = (P(ROW, "x"), P(None, "x"), P(None, "x"), P(ROW, "x"))
    out_specs = (P(ROW, "x"), P())
    return jax.shard_map(
        on_device, mesh=fine, in_specs=in_specs, out_specs=out_specs, check_vma=False
    )
```

time: 281 us -> 251 us (0.89)
  waiting for transfers between devices: 75.9 us -> 42.8 us
  local copies, waits for them, and re-layouts: 24.1 us -> 6.08 us
  between operations: 4 us -> 17.3 us
  other arithmetic: 6.05 us -> 10.2 us
  blocking collectives: 127 us -> 131 us
    all_to_all x5 -> x4, waiting for transfers between devices: 75.9 us -> 42.8 us  [swap(): return lax.all_to_all(pieces, axis, split_axis=0, concat_axis=0, tiled=True)]
    broadcast_in_dim x10 -> x6, local copies, waits for them, and re-layouts: 13.4 us -> 1.6 us  [spread(): return swap(jnp.broadcast_to(block[None], (members, *block.shape)), axis)]
    all_to_all x6, blocking collectives: 50 us -> 55.8 us  [swap(): return lax.all_to_all(pieces, axis, split_axis=0, concat_axis=0, tiled=True)]
    unnamed x6 -> x8, local copies, waits for them, and re-layouts: 3.54 us -> 0.02 us
    dot_general x9 -> x15, matrix products: 12.2 us -> 15.3 us  [the longest x4 5 us: on_device(): jnp.dot(proj_blocks[k], straight[k], preferred_element_type=F32)]
    concatenate x1 -> x0, local copies, waits for them, and re-layouts: 2.83 us -> none  [whole_map(): mine = jnp.concatenate(columns, axis=1)]
    all_to_all x5 -> x4, starting transfers between devices: 28.6 us -> 26.4 us  [swap(): return lax.all_to_all(pieces, axis, split_axis=0, concat_axis=0, tiled=True)]
  transfers between devices with their start and end apart: 5 -> 5, of which waited for: 5 -> 4; matrix products, arithmetic and copies ran while one was open for 2% -> 4% of each run, Pallas kernels for 0% -> 0%
where the time goes in v2:
time: 251 us; the launch traced here: 250 us
  blocking collectives  131 us (52%)
  waiting for transfers between devices  42.8 us (17%)
  starting transfers between devices  26.5 us (11%)
  between operations  17.3 us (7%)
  matrix products  15.8 us (6%)
  other arithmetic  10.2 us (4%)
  local copies, waits for them, and re-layouts  6.08 us (2%)
    all_to_all x6, blocking collectives, swap(): return lax.all_to_all(pieces, axis, split_axis=0, concat_axis=0, tiled=True)  55.8 us
    psum x5, blocking collectives, on_device(): sums = lax.psum(sums, axis)  44.2 us
    all_to_all x4, waiting for transfers between devices, swap(): return lax.all_to_all(pieces, axis, split_axis=0, concat_axis=0, tiled=True)  42.8 us
    all_to_all x4, starting transfers between devices, swap(): return lax.all_to_all(pieces, axis, split_axis=0, concat_axis=0, tiled=True)  26.4 us
    all_gather x1, blocking collectives, on_device(): edge_wide = lax.all_gather(edge, 'x', axis=1, tiled=True)  17.1 us
    all_gather x1, blocking collectives, on_device(): corrected_wide = lax.all_gather(corrected, 'x', axis=1, tiled=True)  13.9 us
  transfers between devices with their start and end apart: 5, of which 4 were waited for; matrix products, arithmetic and copies ran while one was open for 4% of the time, Pallas kernels for 0%

profile of v2, /device:TPU:2, one launch (start us, length us, event | category | flops | bytes accessed | tf_op | source)
XLA Modules:
  0.0 249.7 jit_solution(6232296085085142809)
XLA Ops:
  7.2 17.1 %all_gather.9 = bf16[256,1536]{1,0:T(8,128)(2,1)S(1)} all-gather(bf16[256,384]{1,0:T(8,128)(2,1)} %param.4), channel_id=1, replica_groups=mesh['y'=4,'zh'=4,'zl'=4,'core'=2,'x'=4] {'x'}, dimensions={1}, use_global_device_ids=true | all-gather | bytes 983040 | tf_op jit(solution)/shard_map/all_gather | solution.py:43
  24.9 4.7 %all_to_all.50 = bf16[2,192,1536]{2,1,0:T(8,128)(2,1)S(1)} all-to-all(bf16[2,192,1536]{2,1,0:T(8,128)(2,1)S(1)} %bitcast.85), channel_id=1, replica_groups=mesh['y'=4,'zh'=4,'zl'=4,'core'=2,'x'=4] {'core'}, dimensions={0} | all-to-all | bytes 2359296 | tf_op jit(solution)/shard_map/all_to_all | solution.py:12
  30.7 14.2 %all_to_all.51 = bf16[4,48,1536]{2,1,0:T(8,128)(2,1)S(1)} all-to-all(bf16[4,48,1536]{2,1,0:T(8,128)(2,1)} %bitcast.88), channel_id=1, replica_groups=mesh['y'=4,'zh'=4,'zl'=4,'core'=2,'x'=4] {'y'}, dimensions={0} | all-to-all | bytes 1179648 | tf_op jit(solution)/shard_map/all_to_all | solution.py:12
  45.1 11.6 %all_to_all.52 = bf16[4,12,1536]{2,1,0:T(8,128)(2,1)S(1)} all-to-all(bf16[4,12,1536]{2,1,0:T(8,128)(2,1)S(1)} %reshape.37), channel_id=1, replica_groups=mesh['y'=4,'zh'=4,'zl'=4,'core'=2,'x'=4] {'zl'}, dimensions={0} | all-to-all | bytes 294912 | tf_op jit(solution)/shard_map/all_to_all | solution.py:12
  57.4 12.4 %all-to-all-start.3 = ((bf16[4,12,1536]{2,1,0:T(8,128)(2,1)}), bf16[4,12,1536]{2,1,0:T(8,128)(2,1)S(1)}, u32[]{:S(2)}, u32[]{:S(2)}) async-start(bf16[4,12,1536]{2,1,0:T(8,128)(2,1)} %broadcast_in_dim.19), calls=%async_computation.3 | async-start | bytes 393216 | tf_op jit(solution)/shard_map/all_to_all | solution.py:12
  69.8 15.8 %all-to-all-done.3 = bf16[4,12,1536]{2,1,0:T(8,128)(2,1)S(1)} async-done(((bf16[4,12,1536]{2,1,0:T(8,128)(2,1)}), bf16[4,12,1536]{2,1,0:T(8,128)(2,1)S(1)}, u32[]{:S(2)}, u32[]{:S(2)}) %all-to-all-start.3) | async-done | bytes 147488 | tf_op jit(solution)/shard_map/all_to_all | solution.py:12
  86.3 4.3 %all-to-all-start.4 = ((bf16[4,12,1536]{2,1,0:T(8,128)(2,1)}), bf16[4,12,1536]{2,1,0:T(8,128)(2,1)S(1)}, u32[]{:S(2)}, u32[]{:S(2)}) async-start(bf16[4,12,1536]{2,1,0:T(8,128)(2,1)} %broadcast_in_dim.20), calls=%async_computation.4 | async-start | bytes 393216 | tf_op jit(solution)/shard_map/all_to_all | solution.py:12
  90.6 4.9 %all-to-all-done.4 = bf16[4,12,1536]{2,1,0:T(8,128)(2,1)S(1)} async-done(((bf16[4,12,1536]{2,1,0:T(8,128)(2,1)}), bf16[4,12,1536]{2,1,0:T(8,128)(2,1)S(1)}, u32[]{:S(2)}, u32[]{:S(2)}) %all-to-all-start.4) | async-done | bytes 147488 | tf_op jit(solution)/shard_map/all_to_all | solution.py:12
  96.2 4.9 %convolution_convert_fusion = bf16[1536,384]{1,0:T(8,128)(2,1)S(1)} fusion(bf16[1536,1536]{1,0:T(8,128)(2,1)} %all-gather.2.cloned.1.call-done, bf16[1536,384]{1,0:T(8,128)(2,1)S(1)} %copy-done), kind=kOutput, calls=%fused_computation | convolution fusion | flops 1812529152 | bytes 7077888 | tf_op jit(solution)/shard_map/dot_general | solution.py:55
  103.4 4.7 %all-to-all-start.5 = ((bf16[4,12,384]{2,1,0:T(8,128)(2,1)}), bf16[4,12,384]{2,1,0:T(8,128)(2,1)S(1)}, u32[]{:S(2)}, u32[]{:S(2)}) async-start(bf16[4,12,384]{2,1,0:T(8,128)(2,1)} %reshape.39), calls=%async_computation.5 | async-start | bytes 98304 | tf_op jit(solution)/shard_map/all_to_all | solution.py:12
  113.1 9.0 %all_to_all.53 = bf16[4,4,12,384]{3,1,2,0:T(4,128)(2,1)S(1)} all-to-all(bf16[4,4,12,384]{3,1,2,0:T(4,128)(2,1)S(1)} %broadcast_in_dim.21), channel_id=1, replica_groups=mesh['y'=4,'zh'=4,'zl'=4,'core'=2,'x'=4] {'zl'}, dimensions={0} | all-to-all | bytes 294912 | tf_op jit(solution)/shard_map/all_to_all | solution.py:12
  122.2 10.8 %all_to_all.54 = bf16[4,4,48,384]{3,2,1,0:T(8,128)(2,1)S(1)} all-to-all(bf16[4,4,48,384]{3,2,1,0:T(8,128)(2,1)S(1)} %broadcast_in_dim.46), channel_id=1, replica_groups=mesh['y'=4,'zh'=4,'zl'=4,'core'=2,'x'=4] {'y'}, dimensions={0} | all-to-all | bytes 1179648 | tf_op jit(solution)/shard_map/all_to_all | solution.py:12
  133.2 5.5 %all_to_all.55 = bf16[2,4,192,384]{3,2,1,0:T(8,128)(2,1)} all-to-all(bf16[2,4,192,384]{3,2,1,0:T(8,128)(2,1)S(1)} %broadcast_in_dim.48), channel_id=1, replica_groups=mesh['y'=4,'zh'=4,'zl'=4,'core'=2,'x'=4] {'core'}, dimensions={0} | all-to-all | bytes 2359296 | tf_op jit(solution)/shard_map/all_to_all | solution.py:12
  138.7 5.0 %all-to-all-start.6 = ((bf16[4,640,384]{2,1,0:T(8,128)(2,1)}), bf16[4,640,384]{2,1,0:T(8,128)(2,1)S(1)}, u32[]{:S(2)}, u32[]{:S(2)}) async-start(bf16[4,640,384]{2,1,0:T(8,128)(2,1)} %pad_maximum_fusion), calls=%async_computation.6 | async-start | bytes 3932160 | tf_op jit(solution)/shard_map/all_to_all | solution.py:12
  145.1 2.1 fusion.5
  147.2 20.6 %all-to-all-done.6 = bf16[4,640,384]{2,1,0:T(8,128)(2,1)S(1)} async-done(((bf16[4,640,384]{2,1,0:T(8,128)(2,1)}), bf16[4,640,384]{2,1,0:T(8,128)(2,1)S(1)}, u32[]{:S(2)}, u32[]{:S(2)}) %all-to-all-start.6) | async-done | bytes 1966112 | tf_op jit(solution)/shard_map/all_to_all | solution.py:12
  174.0 13.9 %all_gather.11 = bf16[256,1536]{1,0:T(8,128)(2,1)S(1)} all-gather(bf16[256,384]{1,0:T(8,128)(2,1)S(1)} %fusion.10), channel_id=1, replica_groups=mesh['y'=4,'zh'=4,'zl'=4,'core'=2,'x'=4] {'x'}, dimensions={1}, use_global_device_ids=true | all-gather | bytes 983040 | tf_op jit(solution)/shard_map/all_gather | solution.py:90
  190.6 2.0 pad_maximum_fusion.1
  192.6 2.4 psum.35
  195.0 9.9 %psum.36 = f32[3]{0:T(128)S(1)} all-reduce(f32[3]{0:T(128)S(1)} %psum.35), channel_id=1, replica_groups=mesh['y'=4,'zh'=4,'zl'=4,'core'=2,'x'=4] {'x'}, use_global_device_ids=true, to_apply=%region_8.9 | all-reduce | flops 3 | bytes 24 | tf_op jit(solution)/shard_map/psum | solution.py:105
  205.0 8.9 %psum.37 = f32[3]{0:T(128)S(1)} all-reduce(f32[3]{0:T(128)S(1)} %psum.36), channel_id=1, replica_groups=mesh['y'=4,'zh'=4,'zl'=4,'core'=2,'x'=4] {'y'}, use_global_device_ids=true, to_apply=%region_9.10 | all-reduce | flops 3 | bytes 24 | tf_op jit(solution)/shard_map/psum | solution.py:105
  213.8 9.2 %psum.38 = f32[3]{0:T(128)S(1)} all-reduce(f32[3]{0:T(128)S(1)} %psum.37), channel_id=1, replica_groups=mesh['y'=4,'zh'=4,'zl'=4,'core'=2,'x'=4] {'zl'}, use_global_device_ids=true, to_apply=%region_10.11 | all-reduce | flops 3 | bytes 24 | tf_op jit(solution)/shard_map/psum | solution.py:105
  223.0 13.8 %psum.39 = f32[3]{0:T(128)S(1)} all-reduce(f32[3]{0:T(128)S(1)} %psum.38), channel_id=1, replica_groups=mesh['y'=4,'zh'=4,'zl'=4,'core'=2,'x'=4] {'zh'}, use_global_device_ids=true, to_apply=%region_11.12 | all-reduce | flops 3 | bytes 24 | tf_op jit(solution)/shard_map/psum | solution.py:105
  240.5 1.8 subtract_divide_fusion
  (51 shorter events, 22.9 us)
Async XLA Ops:
  7.2 89.1 %copy-start = (bf16[1536,384]{1,0:T(8,128)(2,1)S(1)}, bf16[1536,384]{1,0:T(8,128)(2,1)}, u32[]{:S(2)}) copy-start(bf16[1536,384]{1,0:T(8,128)(2,1)} %param.6) | copy-start | bytes 3538948
  7.2 17.2 %copy-start.1 = (f32[256,384]{1,0:T(8,128)S(1)}, f32[256,384]{1,0:T(8,128)}, u32[]{:S(2)}) copy-start(f32[256,384]{1,0:T(8,128)} %param.7) | copy-start | bytes 1179652
  7.2 89.0 %all-gather.2.cloned.1.call-start = ((), (), s32[]{:S(2)}) async-start(), calls=%async_computation.10 | async-start | bytes 5898240 | tf_op jit(solution)/shard_map/all_gather | solution.py:45
  57.4 28.2 %all-to-all-start.3 = ((bf16[4,12,1536]{2,1,0:T(8,128)(2,1)}), bf16[4,12,1536]{2,1,0:T(8,128)(2,1)S(1)}, u32[]{:S(2)}, u32[]{:S(2)}) async-start(bf16[4,12,1536]{2,1,0:T(8,128)(2,1)} %broadcast_in_dim.19), calls=%async_computation.3 | async-start | bytes 393216 | tf_op jit(solution)/shard_map/all_to_all | solution.py:12
  86.3 9.2 %all-to-all-start.4 = ((bf16[4,12,1536]{2,1,0:T(8,128)(2,1)}), bf16[4,12,1536]{2,1,0:T(8,128)(2,1)S(1)}, u32[]{:S(2)}, u32[]{:S(2)}) async-start(bf16[4,12,1536]{2,1,0:T(8,128)(2,1)} %broadcast_in_dim.20), calls=%async_computation.4 | async-start | bytes 393216 | tf_op jit(solution)/shard_map/all_to_all | solution.py:12
  101.2 1.3 copy-start.3
  103.4 8.8 %all-to-all-start.5 = ((bf16[4,12,384]{2,1,0:T(8,128)(2,1)}), bf16[4,12,384]{2,1,0:T(8,128)(2,1)S(1)}, u32[]{:S(2)}, u32[]{:S(2)}) async-start(bf16[4,12,384]{2,1,0:T(8,128)(2,1)} %reshape.39), calls=%async_computation.5 | async-start | bytes 98304 | tf_op jit(solution)/shard_map/all_to_all | solution.py:12
  138.7 29.1 %all-to-all-start.6 = ((bf16[4,640,384]{2,1,0:T(8,128)(2,1)}), bf16[4,640,384]{2,1,0:T(8,128)(2,1)S(1)}, u32[]{:S(2)}, u32[]{:S(2)}) async-start(bf16[4,640,384]{2,1,0:T(8,128)(2,1)} %pad_maximum_fusion), calls=%async_computation.6 | async-start | bytes 3932160 | tf_op jit(solution)/shard_map/all_to_all | solution.py:12
  167.8 5.0 %copy-start.2 = (bf16[4,384,384]{2,1,0:T(8,128)(2,1)S(1)}, bf16[4,384,384]{2,1,0:T(8,128)(2,1)}, u32[]{:S(2)}) copy-start(bf16[4,384,384]{2,1,0:T(8,128)(2,1)} %get-tuple-element.13) | copy-start | bytes 3538948
Sparse Core Ops, SparseCore 0:
  24.5 62.0 all-gather.1

commit v3 on v2

v3 whole, which is shorter than its diff:
```python
import functools

import jax
import jax.numpy as jnp
from jax import lax
from jax.experimental import pallas as pl
from jax.experimental.pallas import tpu as pltpu
from jax.sharding import Mesh, PartitionSpec as P

BF16 = jnp.bfloat16
F32 = jnp.float32
ROW = ("y", "zh", "zl", "core")
VMEM = pl.BlockSpec(memory_space=pltpu.VMEM)
SMEM = pl.BlockSpec(memory_space=pltpu.SMEM)
PARAMS = pltpu.CompilerParams(vmem_limit_bytes=48 * 1024 * 1024)


def swap(pieces, axis):
    return lax.all_to_all(pieces, axis, split_axis=0, concat_axis=0, tiled=True)


def spread(block, axis):
    members = lax.axis_size(axis)
    return swap(jnp.broadcast_to(block[None], (members, *block.shape)), axis)


def total(pieces):
    return jnp.sum(pieces.astype(F32), axis=0)


def scatter_sum(block, axis):
    members = lax.axis_size(axis)
    pieces = block.reshape(members, block.shape[0] // members, block.shape[1])
    return total(swap(pieces, axis))


def join_rows(blocks, axis):
    stacked = spread(blocks, axis)
    members, count, rows, width = stacked.shape
    return stacked.transpose(1, 0, 2, 3).reshape(count, members * rows, width)


def dot(a, b):
    return jnp.dot(a, b, preferred_element_type=F32)


def dot_turned(a, b):
    return lax.dot_general(a, b, (((1,), (1,)), ((), ())), preferred_element_type=F32)


def correct_kernel(place, vec, proj, *refs):
    *late, sym, out = refs
    rows = vec.shape[0]
    diag = sym[0]
    first = lax.broadcasted_iota(jnp.int32, diag.shape, 0)
    second = lax.broadcasted_iota(jnp.int32, diag.shape, 1)
    zero = jnp.zeros_like(diag)
    acc = dot(proj[...], jnp.where(first <= second, diag, zero))
    acc += dot_turned(proj[...], jnp.where(first < second, diag, zero))
    for s, piece in enumerate(late, 1):
        part = piece[:rows]
        straight = jnp.broadcast_to(s <= place[0], diag.shape)
        acc += dot(part, jnp.where(straight, sym[s], zero))
        acc += dot_turned(part, jnp.where(straight, zero, sym[s]))
    out[...] = (vec[...] - acc).astype(out.dtype)


def fold(values):
    line = jnp.sum(values, axis=0, keepdims=True)
    return sum(line[:, i : i + 128] for i in range(0, values.shape[1], 128))


def edge_kernel(place, vec, wide, own_rows, *refs):
    *late, dedge, sums = refs
    rows, width = vec.shape
    blocks = len(late) + 1
    acc = jnp.zeros((rows, width), F32)
    for s in range(blocks):
        k = lax.rem(place[0] + blocks - s, blocks)
        part = wide[:, pl.ds(pl.multiple_of(k * width, 128), width)]
        acc += dot_turned(part, own_rows[...] if s == 0 else late[s - 1][rows:])
    v = vec[...]
    dedge[...] = acc
    sums[...] = jnp.concatenate(
        [fold(v * v), fold(v * acc), fold(acc * acc), jnp.zeros((5, 128), F32)], axis=0
    )


def finish_kernel(count, sums, vec, dedge, out, coeffs):
    vv, vd, dd = (jnp.sum(sums[i : i + 1], axis=1, keepdims=True) for i in range(3))
    along = (vv - vd) / count
    keep = 1.0 - along
    square = (keep * keep * vv - 2.0 * keep * vd + dd) / count
    scale = jnp.sqrt(jnp.maximum(square, 0.0) + 1e-06)
    inverse = 1.0 / scale
    out[...] = (keep * vec[...] - dedge[...]) * inverse
    coeffs[0] = along[0, 0]
    coeffs[1] = scale[0, 0]


def on_device(edge, corner, tri_inv, vector):
    bond, width = corner.shape
    rows = vector.shape[0]
    blocks = bond // width
    place = lax.axis_index("x")
    here = place[None]
    rows_total = rows * lax.axis_size(ROW)

    edge_wide = lax.all_gather(edge, "x", axis=1, tiled=True)
    edge_wide, corner = lax.optimization_barrier((edge_wide, corner))
    corner_wide = lax.all_gather(corner, "x", axis=1, tiled=True)
    vec_low = vector.astype(BF16)
    cross = lax.dot_general(
        vec_low, edge_wide, (((0,), (0,)), ((), ())), preferred_element_type=F32
    )
    for axis in ("core", "y", "zl"):
        cross = scatter_sum(cross.astype(BF16), axis)
    cross = lax.psum(cross, "zh") / rows_total
    cross_all = spread(cross.astype(BF16), "x").reshape(-1, bond)

    other = dot(dot(cross_all, corner_wide).astype(BF16), tri_inv).astype(BF16)
    other = other.reshape(blocks, -1, width)
    own = swap(other, "x")

    own_map = dot(corner_wide, tri_inv).astype(BF16)
    proj = dot(edge_wide, own_map).astype(BF16)

    def block_of(s):
        k = lax.rem(place + blocks - s, blocks)
        source = own if s == 0 else jnp.where(s <= place, other, own)
        return lax.dynamic_index_in_dim(source, k, 0, keepdims=False)

    chosen = jnp.stack([block_of(s) for s in range(blocks)])

    def piece_for(s):
        k = lax.rem(place + s, blocks)
        return lax.dynamic_slice_in_dim(own_map, k * width, width, 0)

    pieces = [jnp.concatenate([proj, piece_for(s)]) for s in range(1, blocks)]
    pieces, chosen = lax.optimization_barrier((pieces, chosen))
    late = [
        lax.ppermute(piece, "x", [(i, (i + s) % blocks) for i in range(blocks)])
        for s, piece in enumerate(pieces, 1)
    ]
    for axis in ("zl", "y", "core"):
        chosen = join_rows(chosen, axis)

    corrected = pl.pallas_call(
        correct_kernel,
        out_shape=jax.ShapeDtypeStruct((rows, width), BF16),
        in_specs=[SMEM] + [VMEM] * (blocks + 2),
        out_specs=VMEM,
        compiler_params=PARAMS,
    )(here, vector, proj, *late, chosen)
    corrected_wide = lax.all_gather(corrected, "x", axis=1, tiled=True)
    dedge, sums = pl.pallas_call(
        edge_kernel,
        out_shape=(
            jax.ShapeDtypeStruct((rows, width), F32),
            jax.ShapeDtypeStruct((8, 128), F32),
        ),
        in_specs=[SMEM] + [VMEM] * (blocks + 2),
        out_specs=(VMEM, VMEM),
        compiler_params=PARAMS,
    )(here, vector, corrected_wide, piece_for(0), *late)
    for axis in ("core", "x", "y", "zl", "zh"):
        sums = lax.psum(sums, axis)
    return pl.pallas_call(
        functools.partial(finish_kernel, float(rows_total * bond)),
        out_shape=(
            jax.ShapeDtypeStruct((rows, width), F32),
            jax.ShapeDtypeStruct((2,), F32),
        ),
        in_specs=[VMEM] * 3,
        out_specs=(VMEM, SMEM),
        compiler_params=PARAMS,
    )(sums, vector, dedge)


def solution(mesh):
    fine = Mesh(mesh.devices.reshape(4, 4, -1, 2, mesh.shape["col"]), ROW + ("x",))
    in_specs = (P(ROW, "x"), P(None, "x"), P(None, "x"), P(ROW, "x"))
    out_specs = (P(ROW, "x"), P())
    return jax.shard_map(
        on_device, mesh=fine, in_specs=in_specs, out_specs=out_specs, check_vma=False
    )
```

time: 251 us -> 262 us (1.044)
  waiting for transfers between devices: 42.8 us -> 71.4 us
  matrix products: 15.8 us -> 9.46 us
  other arithmetic: 10.2 us -> 4.81 us
  blocking collectives: 131 us -> 128 us
  Pallas kernels: 0 us -> 2.77 us
    psum x0 -> x1, waiting for transfers between devices: none -> 65.9 us  [on_device(): cross = lax.psum(cross, 'zh') / rows_total]
    all_to_all x4 -> x3, waiting for transfers between devices: 42.8 us -> 4.87 us  [swap(): return lax.all_to_all(pieces, axis, split_axis=0, concat_axis=0, tiled=True)]
    all_to_all x4 -> x3, starting transfers between devices: 26.4 us -> 13.6 us  [swap(): return lax.all_to_all(pieces, axis, split_axis=0, concat_axis=0, tiled=True)]
    ppermute x0 -> x3, starting transfers between devices: none -> 10.4 us  [on_device(): lax.ppermute(piece, 'x', [(i, (i + s) % blocks) for i in range(blocks)])]
    all_to_all x6 -> x5, blocking collectives: 55.8 us -> 47.6 us  [swap(): return lax.all_to_all(pieces, axis, split_axis=0, concat_axis=0, tiled=True)]
    dot_general x15 -> x3, matrix products: 15.3 us -> 8.96 us  [dot(): return jnp.dot(a, b, preferred_element_type=F32)]
    psum x5, blocking collectives: 44.2 us -> 49.1 us  [on_device(): sums = lax.psum(sums, axis)]
    pallas_call x0 -> x3, Pallas kernels: none -> 2.77 us  [the longest x1 1.14 us: on_device(): pl.pallas_call(correct_kernel, out_shape=jax.ShapeDtypeStruct((rows, widt...]
  transfers between devices with their start and end apart: 5 -> 8, of which waited for: 4 -> 2; matrix products, arithmetic and copies ran while one was open for 4% -> 4% of each run, Pallas kernels for 0% -> 0%
where the time goes in v3:
time: 262 us; the launch traced here: 261 us
  blocking collectives  128 us (49%)
  waiting for transfers between devices  71.4 us (27%)
  starting transfers between devices  24 us (9%)
  between operations  15.7 us (6%)
  matrix products  9.46 us (4%)
  local copies, waits for them, and re-layouts  5.27 us (2%)
  other arithmetic  4.81 us (2%)
  Pallas kernels  2.77 us (1%)
    psum x1, waiting for transfers between devices, on_device(): cross = lax.psum(cross, 'zh') / rows_total  65.9 us
    psum x5, blocking collectives, on_device(): sums = lax.psum(sums, axis)  49.1 us
    all_to_all x5, blocking collectives, swap(): return lax.all_to_all(pieces, axis, split_axis=0, concat_axis=0, tiled=True)  47.6 us
    all_gather x1, blocking collectives, on_device(): edge_wide = lax.all_gather(edge, 'x', axis=1, tiled=True)  17.1 us
    all_gather x1, blocking collectives, on_device(): corrected_wide = lax.all_gather(corrected, 'x', axis=1, tiled=True)  14 us
    all_to_all x3, starting transfers between devices, swap(): return lax.all_to_all(pieces, axis, split_axis=0, concat_axis=0, tiled=True)  13.6 us
    ppermute x3, starting transfers between devices, on_device(): lax.ppermute(piece, 'x', [(i, (i + s) % blocks) for i in range(blocks)])  10.4 us
    dot_general x3, matrix products, dot(): return jnp.dot(a, b, preferred_element_type=F32)  8.96 us
  transfers between devices with their start and end apart: 8, of which 2 were waited for; matrix products, arithmetic and copies ran while one was open for 4% of the time, Pallas kernels for 0%

profile of v3, /device:TPU:2, one launch (start us, length us, event | category | flops | bytes accessed | tf_op | source)
XLA Modules:
  0.0 261.2 jit_solution(12584031880705457088)
XLA Ops:
  8.1 17.1 %all_gather.9 = bf16[256,1536]{1,0:T(8,128)(2,1)S(1)} all-gather(bf16[256,384]{1,0:T(8,128)(2,1)} %param.4), channel_id=1, replica_groups=mesh['y'=4,'zh'=4,'zl'=4,'core'=2,'x'=4] {'x'}, dimensions={1}, use_global_device_ids=true | all-gather | bytes 983040 | tf_op jit(solution)/shard_map/all_gather | solution.py:109
  25.7 4.7 %all_to_all.40 = bf16[2,192,1536]{2,1,0:T(8,128)(2,1)S(1)} all-to-all(bf16[2,192,1536]{2,1,0:T(8,128)(2,1)S(1)} %bitcast.23), channel_id=1, replica_groups=mesh['y'=4,'zh'=4,'zl'=4,'core'=2,'x'=4] {'core'}, dimensions={0} | all-to-all | bytes 2359296 | tf_op jit(solution)/shard_map/all_to_all | solution.py:19
  30.3 1.2 reduce_sum.33
  31.5 14.2 %all_to_all.41 = bf16[4,48,1536]{2,1,0:T(8,128)(2,1)S(1)} all-to-all(bf16[4,48,1536]{2,1,0:T(8,128)(2,1)} %bitcast.25), channel_id=1, replica_groups=mesh['y'=4,'zh'=4,'zl'=4,'core'=2,'x'=4] {'y'}, dimensions={0} | all-to-all | bytes 1179648 | tf_op jit(solution)/shard_map/all_to_all | solution.py:19
  45.8 11.6 %all_to_all.42 = bf16[4,12,1536]{2,1,0:T(8,128)(2,1)S(1)} all-to-all(bf16[4,12,1536]{2,1,0:T(8,128)(2,1)S(1)} %reshape.28), channel_id=1, replica_groups=mesh['y'=4,'zh'=4,'zl'=4,'core'=2,'x'=4] {'zl'}, dimensions={0} | all-to-all | bytes 294912 | tf_op jit(solution)/shard_map/all_to_all | solution.py:19
  58.7 65.9 %all-reduce.2.cloned.1.call-done = f32[12,1536]{1,0:T(8,128)} async-done(((f32[12,1536]{1,0:T(8,128)}), f32[12,1536]{1,0:T(8,128)}) %all-reduce.2.cloned.1.call-update) | async-done | bytes 73744 | tf_op jit(solution)/shard_map/psum | solution.py:118
  126.2 4.8 %all-to-all-start.3 = ((bf16[4,12,1536]{2,1,0:T(8,128)(2,1)}), bf16[4,12,1536]{2,1,0:T(8,128)(2,1)S(1)}, u32[]{:S(2)}, u32[]{:S(2)}) async-start(bf16[4,12,1536]{2,1,0:T(8,128)(2,1)} %broadcast_in_dim.30), calls=%async_computation.3 | async-start | bytes 393216 | tf_op jit(solution)/shard_map/all_to_all | solution.py:19
  131.0 4.9 %all-to-all-done.3 = bf16[4,12,1536]{2,1,0:T(8,128)(2,1)S(1)} async-done(((bf16[4,12,1536]{2,1,0:T(8,128)(2,1)}), bf16[4,12,1536]{2,1,0:T(8,128)(2,1)S(1)}, u32[]{:S(2)}, u32[]{:S(2)}) %all-to-all-start.3) | async-done | bytes 147488 | tf_op jit(solution)/shard_map/all_to_all | solution.py:19
  136.0 3.4 %fusion.1 = bf16[48,384]{1,0:T(8,128)(2,1)S(1)} fusion(bf16[1536,384]{1,0:T(8,128)(2,1)S(1)} %copy-done, bf16[48,1536]{1,0:T(8,128)(2,1)S(1)} %reshape.29, bf16[1536,1536]{1,0:T(8,128)(2,1)} %all-gather.2.cloned.1.call-done), kind=kOutput, calls=%fused_computation.5 | convolution fusion | flops 283207680 | bytes 6082560 | tf_op jit(solution)/shard_map/dot_general | solution.py:44
  140.0 4.7 %all-to-all-start.4 = ((bf16[4,12,384]{2,1,0:T(8,128)(2,1)}), bf16[4,12,384]{2,1,0:T(8,128)(2,1)S(1)}, u32[]{:S(2)}, u32[]{:S(2)}) async-start(bf16[4,12,384]{2,1,0:T(8,128)(2,1)} %reshape.30), calls=%async_computation.4 | async-start | bytes 98304 | tf_op jit(solution)/shard_map/all_to_all | solution.py:19
  144.7 4.9 %convolution_convert_fusion = bf16[1536,384]{1,0:T(8,128)(2,1)S(1)} fusion(bf16[1536,1536]{1,0:T(8,128)(2,1)} %all-gather.2.cloned.1.call-done, bf16[1536,384]{1,0:T(8,128)(2,1)S(1)} %copy-done), kind=kOutput, calls=%fused_computation | convolution fusion | flops 1812529152 | bytes 7077888 | tf_op jit(solution)/shard_map/dot_general | solution.py:44
  150.4 1.2 pad_maximum_fusion
  153.1 4.0 %all-to-all-start.5 = ((bf16[4,4,12,384]{3,1,2,0:T(4,128)(2,1)}), bf16[4,4,12,384]{3,1,2,0:T(4,128)(2,1)}, u32[]{:S(2)}, u32[]{:S(2)}) async-start(bf16[4,4,12,384]{3,1,2,0:T(4,128)(2,1)} %broadcast_in_dim.31), calls=%async_computation.5 | async-start | bytes 294912 | tf_op jit(solution)/shard_map/all_to_all | solution.py:19
  157.2 3.4 %collective-permute-start = (bf16[640,384]{1,0:T(8,128)(2,1)}, bf16[640,384]{1,0:T(8,128)(2,1)S(1)}, u32[]{:S(2)}, u32[]{:S(2)}) collective-permute-start(bf16[640,384]{1,0:T(8,128)(2,1)} %get-tuple-element.12), channel_id=1, source_target_pairs={{0,1},{1,2},{2,3},{3,0},{4,5},{5,6},{6,7},{7,4},{8,9},{9,10},{10,1... | collective-permute-start | bytes 1474568 | tf_op jit(solution)/shard_map/ppermute | solution.py:142
  160.6 2.6 collective-permute-start.1
  163.1 4.5 %collective-permute-start.2 = (bf16[640,384]{1,0:T(8,128)(2,1)}, bf16[640,384]{1,0:T(8,128)(2,1)S(1)}, u32[]{:S(2)}, u32[]{:S(2)}) collective-permute-start(bf16[640,384]{1,0:T(8,128)(2,1)} %get-tuple-element.14), channel_id=1, source_target_pairs={{0,3},{1,0},{2,1},{3,2},{4,7},{5,4},{6,5},{7,6},{8,11},{9,8},{10,9... | collective-permute-start | bytes 1474568 | tf_op jit(solution)/shard_map/ppermute | solution.py:142
  168.6 12.5 %all_to_all.43 = bf16[4,4,48,384]{3,2,1,0:T(8,128)(2,1)S(1)} all-to-all(bf16[4,4,48,384]{3,2,1,0:T(8,128)(2,1)S(1)} %broadcast_in_dim.33), channel_id=1, replica_groups=mesh['y'=4,'zh'=4,'zl'=4,'core'=2,'x'=4] {'y'}, dimensions={0} | all-to-all | bytes 1179648 | tf_op jit(solution)/shard_map/all_to_all | solution.py:19
  181.3 4.7 %all_to_all.44 = bf16[2,4,192,384]{3,2,1,0:T(8,128)(2,1)S(1)} all-to-all(bf16[2,4,192,384]{3,2,1,0:T(8,128)(2,1)S(1)} %broadcast_in_dim.35), channel_id=1, replica_groups=mesh['y'=4,'zh'=4,'zl'=4,'core'=2,'x'=4] {'core'}, dimensions={0} | all-to-all | bytes 2359296 | tf_op jit(solution)/shard_map/all_to_all | solution.py:19
  187.3 14.0 %all_gather.11.wide = bf16[256,1536]{1,0:T(8,128)(2,1)S(1)} all-gather(bf16[256,384]{1,0:T(8,128)(2,1)S(1)} %shard_map.59), channel_id=1, replica_groups=mesh['y'=4,'zh'=4,'zl'=4,'core'=2,'x'=4] {'x'}, dimensions={1}, use_global_device_ids=true | all-gather | bytes 983040 | tf_op jit(solution)/shard_map/all_gather | solution.py:155
  202.8 2.4 psum.43
  205.2 10.3 %psum.44 = f32[8,128]{1,0:T(8,128)S(1)} all-reduce(f32[8,128]{1,0:T(8,128)S(1)} %psum.43), channel_id=1, replica_groups=mesh['y'=4,'zh'=4,'zl'=4,'core'=2,'x'=4] {'x'}, use_global_device_ids=true, to_apply=%region_5.6 | all-reduce | flops 1024 | bytes 8192 | tf_op jit(solution)/shard_map/psum | solution.py:167
  215.5 8.9 %psum.45 = f32[8,128]{1,0:T(8,128)S(1)} all-reduce(f32[8,128]{1,0:T(8,128)S(1)} %psum.44), channel_id=1, replica_groups=mesh['y'=4,'zh'=4,'zl'=4,'core'=2,'x'=4] {'y'}, use_global_device_ids=true, to_apply=%region_6.7 | all-reduce | flops 1024 | bytes 8192 | tf_op jit(solution)/shard_map/psum | solution.py:167
  224.4 12.2 %psum.46 = f32[8,128]{1,0:T(8,128)S(1)} all-reduce(f32[8,128]{1,0:T(8,128)S(1)} %psum.45), channel_id=1, replica_groups=mesh['y'=4,'zh'=4,'zl'=4,'core'=2,'x'=4] {'zl'}, use_global_device_ids=true, to_apply=%region_7.8 | all-reduce | flops 1024 | bytes 8192 | tf_op jit(solution)/shard_map/psum | solution.py:167
  236.6 15.3 %psum.47.sums = f32[8,128]{1,0:T(8,128)S(1)} all-reduce(f32[8,128]{1,0:T(8,128)S(1)} %psum.46), channel_id=1, replica_groups=mesh['y'=4,'zh'=4,'zl'=4,'core'=2,'x'=4] {'zh'}, use_global_device_ids=true, to_apply=%region_8.9 | all-reduce | flops 1024 | bytes 8192 | tf_op jit(solution)/shard_map/psum | solution.py:167
  (40 shorter events, 12.2 us)
Async XLA Ops:
  8.0 127.9 %copy-start = (bf16[1536,384]{1,0:T(8,128)(2,1)S(1)}, bf16[1536,384]{1,0:T(8,128)(2,1)}, u32[]{:S(2)}) copy-start(bf16[1536,384]{1,0:T(8,128)(2,1)} %param.6) | copy-start | bytes 3538948
  8.0 17.1 %copy-start.1 = (f32[256,384]{1,0:T(8,128)S(1)}, f32[256,384]{1,0:T(8,128)}, u32[]{:S(2)}) copy-start(f32[256,384]{1,0:T(8,128)} %vec.5) | copy-start | bytes 1179652
  8.0 116.6 %all-reduce.2.cloned.1.call-start = ((), (), s32[]{:S(2)}) async-start(), calls=%async_computation.9 | async-start | bytes 196608 | tf_op jit(solution)/shard_map/psum | solution.py:118
  58.1 77.8 %all-gather.2.cloned.1.call-start = ((), (), s32[]{:S(2)}) async-start(), calls=%async_computation.8 | async-start | bytes 5898240 | tf_op jit(solution)/shard_map/all_gather | solution.py:111
  126.2 9.7 %all-to-all-start.3 = ((bf16[4,12,1536]{2,1,0:T(8,128)(2,1)}), bf16[4,12,1536]{2,1,0:T(8,128)(2,1)S(1)}, u32[]{:S(2)}, u32[]{:S(2)}) async-start(bf16[4,12,1536]{2,1,0:T(8,128)(2,1)} %broadcast_in_dim.30), calls=%async_computation.3 | async-start | bytes 393216 | tf_op jit(solution)/shard_map/all_to_all | solution.py:19
  140.0 11.6 %all-to-all-start.4 = ((bf16[4,12,384]{2,1,0:T(8,128)(2,1)}), bf16[4,12,384]{2,1,0:T(8,128)(2,1)S(1)}, u32[]{:S(2)}, u32[]{:S(2)}) async-start(bf16[4,12,384]{2,1,0:T(8,128)(2,1)} %reshape.30), calls=%async_computation.4 | async-start | bytes 98304 | tf_op jit(solution)/shard_map/all_to_all | solution.py:19
  153.1 14.5 %all-to-all-start.5 = ((bf16[4,4,12,384]{3,1,2,0:T(4,128)(2,1)}), bf16[4,4,12,384]{3,1,2,0:T(4,128)(2,1)}, u32[]{:S(2)}, u32[]{:S(2)}) async-start(bf16[4,4,12,384]{3,1,2,0:T(4,128)(2,1)} %broadcast_in_dim.31), calls=%async_computation.5 | async-start | bytes 294912 | tf_op jit(solution)/shard_map/all_to_all | solution.py:19
  157.2 28.9 %collective-permute-start = (bf16[640,384]{1,0:T(8,128)(2,1)}, bf16[640,384]{1,0:T(8,128)(2,1)S(1)}, u32[]{:S(2)}, u32[]{:S(2)}) collective-permute-start(bf16[640,384]{1,0:T(8,128)(2,1)} %get-tuple-element.12), channel_id=1, source_target_pairs={{0,1},{1,2},{2,3},{3,0},{4,5},{5,6},{6,7},{7,4},{8,9},{9,10},{10,1... | collective-permute-start | bytes 1474568 | tf_op jit(solution)/shard_map/ppermute | solution.py:142
  160.6 25.6 %collective-permute-start.1 = (bf16[640,384]{1,0:T(8,128)(2,1)}, bf16[640,384]{1,0:T(8,128)(2,1)S(1)}, u32[]{:S(2)}, u32[]{:S(2)}) collective-permute-start(bf16[640,384]{1,0:T(8,128)(2,1)} %get-tuple-element.13), channel_id=1, source_target_pairs={{0,2},{1,3},{2,0},{3,1},{4,6},{5,7},{6,4},{7,5},{8,10},{9,11},{10,... | collective-permute-start | bytes 1474568 | tf_op jit(solution)/shard_map/ppermute | solution.py:142
  163.1 23.0 %collective-permute-start.2 = (bf16[640,384]{1,0:T(8,128)(2,1)}, bf16[640,384]{1,0:T(8,128)(2,1)S(1)}, u32[]{:S(2)}, u32[]{:S(2)}) collective-permute-start(bf16[640,384]{1,0:T(8,128)(2,1)} %get-tuple-element.14), channel_id=1, source_target_pairs={{0,3},{1,0},{2,1},{3,2},{4,7},{5,4},{6,5},{7,6},{8,11},{9,8},{10,9... | collective-permute-start | bytes 1474568 | tf_op jit(solution)/shard_map/ppermute | solution.py:142
  202.0 0.8 copy-start.2
  251.9 1.0 copy-start.3
Sparse Core Ops, SparseCore 0:
  58.2 66.3 all-reduce.1
Sparse Core Ops, SparseCore 1:
  60.7 58.8 all-gather.1

commit v4 on v3

--- a/solution.py
+++ b/solution.py
@@ -48,21 +48,22 @@
     return lax.dot_general(a, b, (((1,), (1,)), ((), ())), preferred_element_type=F32)
 
 
-def correct_kernel(place, vec, proj, *refs):
-    *late, sym, out = refs
-    rows = vec.shape[0]
-    diag = sym[0]
-    first = lax.broadcasted_iota(jnp.int32, diag.shape, 0)
-    second = lax.broadcasted_iota(jnp.int32, diag.shape, 1)
-    zero = jnp.zeros_like(diag)
-    acc = dot(proj[...], jnp.where(first <= second, diag, zero))
-    acc += dot_turned(proj[...], jnp.where(first < second, diag, zero))
-    for s, piece in enumerate(late, 1):
-        part = piece[:rows]
-        straight = jnp.broadcast_to(s <= place[0], diag.shape)
-        acc += dot(part, jnp.where(straight, sym[s], zero))
-        acc += dot_turned(part, jnp.where(straight, zero, sym[s]))
-    out[...] = (vec[...] - acc).astype(out.dtype)
+def partial_kernel(place, vec, proj, sym, own_map, out):
+    rows, width = vec.shape
+    blocks = sym.shape[0]
+    first = lax.broadcasted_iota(jnp.int32, (width, width), 0)
+    second = lax.broadcasted_iota(jnp.int32, (width, width), 1)
+    zero = jnp.zeros((width, width), BF16)
+    acc = jnp.zeros((rows, width), F32)
+    for k in range(blocks):
+        shift = (place[0] - k) * width
+        part = proj[k, :rows]
+        acc += dot(part, jnp.where(first <= second + shift, sym[k], zero))
+        acc += dot_turned(part, jnp.where(first < second - shift, sym[k], zero))
+    corrected = (vec[...] - acc).astype(BF16)
+    for k in range(blocks):
+        share = dot_turned(corrected, own_map[k * width : (k + 1) * width])
+        out[k] = share.astype(BF16)
 
 
 def fold(values):
@@ -70,15 +71,8 @@
     return sum(line[:, i : i + 128] for i in range(0, values.shape[1], 128))
 
 
-def edge_kernel(place, vec, wide, own_rows, *refs):
-    *late, dedge, sums = refs
-    rows, width = vec.shape
-    blocks = len(late) + 1
-    acc = jnp.zeros((rows, width), F32)
-    for s in range(blocks):
-        k = lax.rem(place[0] + blocks - s, blocks)
-        part = wide[:, pl.ds(pl.multiple_of(k * width, 128), width)]
-        acc += dot_turned(part, own_rows[...] if s == 0 else late[s - 1][rows:])
+def edge_kernel(vec, shares, dedge, sums):
+    acc = sum(shares[k].astype(F32) for k in range(shares.shape[0]))
     v = vec[...]
     dedge[...] = acc
     sums[...] = jnp.concatenate(
@@ -106,6 +100,8 @@
     here = place[None]
     rows_total = rows * lax.axis_size(ROW)
 
+    before = lax.broadcasted_iota(jnp.int32, (blocks, 1, 1), 0) < place
+    edge, here, before = lax.optimization_barrier((edge, here, before))
     edge_wide = lax.all_gather(edge, "x", axis=1, tiled=True)
     edge_wide, corner = lax.optimization_barrier((edge_wide, corner))
     corner_wide = lax.all_gather(corner, "x", axis=1, tiled=True)
@@ -113,9 +109,10 @@
     cross = lax.dot_general(
         vec_low, edge_wide, (((0,), (0,)), ((), ())), preferred_element_type=F32
     )
+    cross = cross * (1.0 / rows_total)
     for axis in ("core", "y", "zl"):
         cross = scatter_sum(cross.astype(BF16), axis)
-    cross = lax.psum(cross, "zh") / rows_total
+    cross = total(spread(cross.astype(BF16), "zh"))
     cross_all = spread(cross.astype(BF16), "x").reshape(-1, bond)
 
     other = dot(dot(cross_all, corner_wide).astype(BF16), tri_inv).astype(BF16)
@@ -124,45 +121,31 @@
 
     own_map = dot(corner_wide, tri_inv).astype(BF16)
     proj = dot(edge_wide, own_map).astype(BF16)
+    proj = jnp.concatenate([proj, own_map[: width - rows]])
+    proj_blocks = lax.all_gather(proj, "x", axis=0)
 
-    def block_of(s):
-        k = lax.rem(place + blocks - s, blocks)
-        source = own if s == 0 else jnp.where(s <= place, other, own)
-        return lax.dynamic_index_in_dim(source, k, 0, keepdims=False)
-
-    chosen = jnp.stack([block_of(s) for s in range(blocks)])
-
-    def piece_for(s):
-        k = lax.rem(place + s, blocks)
-        return lax.dynamic_slice_in_dim(own_map, k * width, width, 0)
-
-    pieces = [jnp.concatenate([proj, piece_for(s)]) for s in range(1, blocks)]
-    pieces, chosen = lax.optimization_barrier((pieces, chosen))
-    late = [
-        lax.ppermute(piece, "x", [(i, (i + s) % blocks) for i in range(blocks)])
-        for s, piece in enumerate(pieces, 1)
-    ]
+    chosen = jnp.where(before, other, own)
     for axis in ("zl", "y", "core"):
         chosen = join_rows(chosen, axis)
 
-    corrected = pl.pallas_call(
-        correct_kernel,
-        out_shape=jax.ShapeDtypeStruct((rows, width), BF16),
-        in_specs=[SMEM] + [VMEM] * (blocks + 2),
+    shares = pl.pallas_call(
+        partial_kernel,
+        out_shape=jax.ShapeDtypeStruct((blocks, rows, width), BF16),
+        in_specs=[SMEM] + [VMEM] * 4,
         out_specs=VMEM,
         compiler_params=PARAMS,
-    )(here, vector, proj, *late, chosen)
-    corrected_wide = lax.all_gather(corrected, "x", axis=1, tiled=True)
+    )(here, vector, proj_blocks, chosen, own_map)
+    shares = swap(shares, "x")
     dedge, sums = pl.pallas_call(
         edge_kernel,
         out_shape=(
             jax.ShapeDtypeStruct((rows, width), F32),
             jax.ShapeDtypeStruct((8, 128), F32),
         ),
-        in_specs=[SMEM] + [VMEM] * (blocks + 2),
+        in_specs=[VMEM, VMEM],
         out_specs=(VMEM, VMEM),
         compiler_params=PARAMS,
-    )(here, vector, corrected_wide, piece_for(0), *late)
+    )(vector, shares)
     for axis in ("core", "x", "y", "zl", "zh"):
         sums = lax.psum(sums, axis)
     return pl.pallas_call(

time: 262 us -> 217 us (0.83)
  waiting for transfers between devices: 71.4 us -> 16.8 us
  blocking collectives: 128 us -> 154 us
  starting transfers between devices: 24 us -> 12.4 us
    psum x1 -> x0, waiting for transfers between devices: 65.9 us -> none  [on_device(): cross = lax.psum(cross, 'zh') / rows_total]
    all_to_all x5 -> x9, blocking collectives: 47.6 us -> 91.3 us  [swap(): return lax.all_to_all(pieces, axis, split_axis=0, concat_axis=0, tiled=True)]
    all_gather x1, waiting for transfers between devices: 0.03 us -> 16.7 us  [on_device(): corner_wide = lax.all_gather(corner, 'x', axis=1, tiled=True)]
    all_gather x1 -> x0, blocking collectives: 14 us -> none  [on_device(): corrected_wide = lax.all_gather(corrected, 'x', axis=1, tiled=True)]
    ppermute x3 -> x0, starting transfers between devices: 10.4 us -> none  [on_device(): lax.ppermute(piece, 'x', [(i, (i + s) % blocks) for i in range(blocks)])]
    all_to_all x3 -> x1, waiting for transfers between devices: 4.87 us -> 0.01 us  [swap(): return lax.all_to_all(pieces, axis, split_axis=0, concat_axis=0, tiled=True)]
    psum x5, blocking collectives: 49.1 us -> 45.9 us  [on_device(): sums = lax.psum(sums, axis)]
    all_to_all x3 -> x1, starting transfers between devices: 13.6 us -> 12.4 us  [swap(): return lax.all_to_all(pieces, axis, split_axis=0, concat_axis=0, tiled=True)]
  transfers between devices with their start and end apart: 8 -> 3, of which waited for: 2 -> 1; matrix products, arithmetic and copies ran while one was open for 4% -> 6% of each run, Pallas kernels for 0% -> 0%
where the time goes in v4:
time: 217 us
  blocking collectives  154 us (71%)
  waiting for transfers between devices  16.8 us (8%)
  between operations  14.2 us (7%)
  starting transfers between devices  12.4 us (6%)
  matrix products  9.48 us (4%)
  local copies, waits for them, and re-layouts  4.19 us (2%)
  Pallas kernels  3.14 us (1%)
  other arithmetic  2.19 us (1%)
    all_to_all x9, blocking collectives, swap(): return lax.all_to_all(pieces, axis, split_axis=0, concat_axis=0, tiled=True)  91.3 us
    psum x5, blocking collectives, on_device(): sums = lax.psum(sums, axis)  45.9 us
    all_gather x1, blocking collectives, on_device(): edge_wide = lax.all_gather(edge, 'x', axis=1, tiled=True)  17.1 us
    all_gather x1, waiting for transfers between devices, on_device(): corner_wide = lax.all_gather(corner, 'x', axis=1, tiled=True)  16.7 us
    all_to_all x1, starting transfers between devices, swap(): return lax.all_to_all(pieces, axis, split_axis=0, concat_axis=0, tiled=True)  12.4 us
    dot_general x3, matrix products, dot(): return jnp.dot(a, b, preferred_element_type=F32)  8.97 us
  transfers between devices with their start and end apart: 3, of which 1 were waited for; matrix products, arithmetic and copies ran while one was open for 6% of the time, Pallas kernels for 0%

profile of v4, /device:TPU:2, one launch (start us, length us, event | category | flops | bytes accessed | tf_op | source)
XLA Modules:
  0.0 216.7 jit_solution(9003223820388774657)
XLA Ops:
  7.3 17.1 %all_gather.12 = bf16[256,1536]{1,0:T(8,128)(2,1)S(1)} all-gather(bf16[256,384]{1,0:T(8,128)(2,1)} %param.4), channel_id=1, replica_groups=mesh['y'=4,'zh'=4,'zl'=4,'core'=2,'x'=4] {'x'}, dimensions={1}, use_global_device_ids=true | all-gather | bytes 983040 | tf_op jit(solution)/shard_map/all_gather | solution.py:105
  24.9 4.7 %all_to_all.50 = bf16[2,192,1536]{2,1,0:T(8,128)(2,1)S(1)} all-to-all(bf16[2,192,1536]{2,1,0:T(8,128)(2,1)S(1)} %bitcast.26), channel_id=1, replica_groups=mesh['y'=4,'zh'=4,'zl'=4,'core'=2,'x'=4] {'core'}, dimensions={0} | all-to-all | bytes 2359296 | tf_op jit(solution)/shard_map/all_to_all | solution.py:19
  29.6 1.2 reduce_sum.48
  30.7 14.2 %all_to_all.51 = bf16[4,48,1536]{2,1,0:T(8,128)(2,1)S(1)} all-to-all(bf16[4,48,1536]{2,1,0:T(8,128)(2,1)} %bitcast.28), channel_id=1, replica_groups=mesh['y'=4,'zh'=4,'zl'=4,'core'=2,'x'=4] {'y'}, dimensions={0} | all-to-all | bytes 1179648 | tf_op jit(solution)/shard_map/all_to_all | solution.py:19
  45.1 11.6 %all_to_all.52 = bf16[4,12,1536]{2,1,0:T(8,128)(2,1)S(1)} all-to-all(bf16[4,12,1536]{2,1,0:T(8,128)(2,1)S(1)} %reshape.37), channel_id=1, replica_groups=mesh['y'=4,'zh'=4,'zl'=4,'core'=2,'x'=4] {'zl'}, dimensions={0} | all-to-all | bytes 294912 | tf_op jit(solution)/shard_map/all_to_all | solution.py:19
  57.4 12.4 %all-to-all-start.3 = ((bf16[4,12,1536]{2,1,0:T(8,128)(2,1)}), bf16[4,12,1536]{2,1,0:T(8,128)(2,1)S(1)}, u32[]{:S(2)}, u32[]{:S(2)}) async-start(bf16[4,12,1536]{2,1,0:T(8,128)(2,1)} %broadcast_in_dim.48), calls=%async_computation.3 | async-start | bytes 393216 | tf_op jit(solution)/shard_map/all_to_all | solution.py:19
  69.8 16.7 %all-gather.4.cloned.1.call-done = bf16[1536,1536]{1,0:T(8,128)(2,1)} async-done(((bf16[1536,384]{1,0:T(8,128)(2,1)}), bf16[1536,1536]{1,0:T(8,128)(2,1)}) %all-gather.4.cloned.1.call-update) | async-done | bytes 4718608 | tf_op jit(solution)/shard_map/all_gather | solution.py:107
  86.5 5.0 %convolution_convert_fusion.own_map = bf16[1536,384]{1,0:T(8,128)(2,1)S(1)} fusion(bf16[1536,1536]{1,0:T(8,128)(2,1)} %all-gather.4.cloned.1.call-done, bf16[1536,384]{1,0:T(8,128)(2,1)S(1)} %copy-done), kind=kOutput, calls=%fused_computation.2 | convolution fusion | flops 1812529152 | bytes 7077888 | tf_op jit(solution)/shard_map/dot_general | solution.py:44
  93.4 9.2 %all_to_all.53 = bf16[4,12,1536]{2,1,0:T(8,128)(2,1)S(1)} all-to-all(bf16[4,12,1536]{2,1,0:T(8,128)(2,1)S(1)} %broadcast_in_dim.49), channel_id=1, replica_groups=mesh['y'=4,'zh'=4,'zl'=4,'core'=2,'x'=4] {'x'}, dimensions={0} | all-to-all | bytes 294912 | tf_op jit(solution)/shard_map/all_to_all | solution.py:19
  102.6 3.4 %fusion.2 = bf16[48,384]{1,0:T(8,128)(2,1)S(1)} fusion(bf16[1536,384]{1,0:T(8,128)(2,1)S(1)} %copy-done, bf16[48,1536]{1,0:T(8,128)(2,1)S(1)} %reshape.38, bf16[1536,1536]{1,0:T(8,128)(2,1)} %all-gather.4.cloned.1.call-done), kind=kOutput, calls=%fused_computation.6 | convolution fusion | flops 283207680 | bytes 6082560 | tf_op jit(solution)/shard_map/dot_general | solution.py:44
  106.1 7.9 %all_to_all.54 = bf16[4,12,384]{2,1,0:T(8,128)(2,1)S(1)} all-to-all(bf16[4,12,384]{2,1,0:T(8,128)(2,1)S(1)} %reshape.39), channel_id=1, replica_groups=mesh['y'=4,'zh'=4,'zl'=4,'core'=2,'x'=4] {'x'}, dimensions={0} | all-to-all | bytes 73728 | tf_op jit(solution)/shard_map/all_to_all | solution.py:19
  114.1 11.3 %all_to_all.55 = bf16[4,4,12,384]{3,1,2,0:T(4,128)(2,1)S(1)} all-to-all(bf16[4,4,12,384]{3,1,2,0:T(4,128)(2,1)S(1)} %broadcast_in_dim.50), channel_id=1, replica_groups=mesh['y'=4,'zh'=4,'zl'=4,'core'=2,'x'=4] {'zl'}, dimensions={0} | all-to-all | bytes 294912 | tf_op jit(solution)/shard_map/all_to_all | solution.py:19
  125.5 12.5 %all_to_all.56 = bf16[4,4,48,384]{3,2,1,0:T(8,128)(2,1)S(1)} all-to-all(bf16[4,4,48,384]{3,2,1,0:T(8,128)(2,1)S(1)} %broadcast_in_dim.52), channel_id=1, replica_groups=mesh['y'=4,'zh'=4,'zl'=4,'core'=2,'x'=4] {'y'}, dimensions={0} | all-to-all | bytes 1179648 | tf_op jit(solution)/shard_map/all_to_all | solution.py:19
  138.2 4.7 %all_to_all.57 = bf16[2,4,192,384]{3,2,1,0:T(8,128)(2,1)S(1)} all-to-all(bf16[2,4,192,384]{3,2,1,0:T(8,128)(2,1)S(1)} %broadcast_in_dim.54), channel_id=1, replica_groups=mesh['y'=4,'zh'=4,'zl'=4,'core'=2,'x'=4] {'core'}, dimensions={0} | all-to-all | bytes 2359296 | tf_op jit(solution)/shard_map/all_to_all | solution.py:19
  143.0 1.3 copy-done.3
  144.3 1.3 copy-done.4
  145.5 2.0 shard_map.59
  147.6 15.3 %all_to_all.58.shares = bf16[4,256,384]{2,1,0:T(8,128)(2,1)S(1)} all-to-all(bf16[4,256,384]{2,1,0:T(8,128)(2,1)S(1)} %shard_map.59), channel_id=1, replica_groups=mesh['y'=4,'zh'=4,'zl'=4,'core'=2,'x'=4] {'x'}, dimensions={0} | all-to-all | bytes 1572864 | tf_op jit(solution)/shard_map/all_to_all | solution.py:19
  163.0 2.5 %psum.35 = f32[8,128]{1,0:T(8,128)S(1)} all-reduce(f32[8,128]{1,0:T(8,128)S(1)} %get-tuple-element.14), channel_id=1, replica_groups=mesh['y'=4,'zh'=4,'zl'=4,'core'=2,'x'=4] {'core'}, use_global_device_ids=true, to_apply=%region_4.5 | all-reduce | flops 1024 | bytes 8192 | tf_op jit(solution)/shard_map/psum | solution.py:150
  165.5 9.2 %psum.36 = f32[8,128]{1,0:T(8,128)S(1)} all-reduce(f32[8,128]{1,0:T(8,128)S(1)} %psum.35), channel_id=1, replica_groups=mesh['y'=4,'zh'=4,'zl'=4,'core'=2,'x'=4] {'x'}, use_global_device_ids=true, to_apply=%region_5.6 | all-reduce | flops 1024 | bytes 8192 | tf_op jit(solution)/shard_map/psum | solution.py:150
  174.7 8.9 %psum.37 = f32[8,128]{1,0:T(8,128)S(1)} all-reduce(f32[8,128]{1,0:T(8,128)S(1)} %psum.36), channel_id=1, replica_groups=mesh['y'=4,'zh'=4,'zl'=4,'core'=2,'x'=4] {'y'}, use_global_device_ids=true, to_apply=%region_6.7 | all-reduce | flops 1024 | bytes 8192 | tf_op jit(solution)/shard_map/psum | solution.py:150
  183.6 9.2 %psum.38 = f32[8,128]{1,0:T(8,128)S(1)} all-reduce(f32[8,128]{1,0:T(8,128)S(1)} %psum.37), channel_id=1, replica_groups=mesh['y'=4,'zh'=4,'zl'=4,'core'=2,'x'=4] {'zl'}, use_global_device_ids=true, to_apply=%region_7.8 | all-reduce | flops 1024 | bytes 8192 | tf_op jit(solution)/shard_map/psum | solution.py:150
  192.7 16.2 %psum.39.sums = f32[8,128]{1,0:T(8,128)S(1)} all-reduce(f32[8,128]{1,0:T(8,128)S(1)} %psum.38), channel_id=1, replica_groups=mesh['y'=4,'zh'=4,'zl'=4,'core'=2,'x'=4] {'zh'}, use_global_device_ids=true, to_apply=%region_8.9 | all-reduce | flops 1024 | bytes 8192 | tf_op jit(solution)/shard_map/psum | solution.py:150
  208.9 0.9 shard_map.61
  (36 shorter events, 4.0 us)
Async XLA Ops:
  7.2 79.4 %copy-start = (bf16[1536,384]{1,0:T(8,128)(2,1)S(1)}, bf16[1536,384]{1,0:T(8,128)(2,1)}, u32[]{:S(2)}) copy-start(bf16[1536,384]{1,0:T(8,128)(2,1)} %param.6) | copy-start | bytes 3538948
  7.2 17.2 %copy-start.1 = (f32[256,384]{1,0:T(8,128)S(1)}, f32[256,384]{1,0:T(8,128)}, u32[]{:S(2)}) copy-start(f32[256,384]{1,0:T(8,128)} %vec.5) | copy-start | bytes 1179652
  7.2 79.3 %all-gather.4.cloned.1.call-start = ((), (), s32[]{:S(2)}) async-start(), calls=%async_computation.10 | async-start | bytes 5898240 | tf_op jit(solution)/shard_map/all_gather | solution.py:107
  57.4 35.9 %all-to-all-start.3 = ((bf16[4,12,1536]{2,1,0:T(8,128)(2,1)}), bf16[4,12,1536]{2,1,0:T(8,128)(2,1)S(1)}, u32[]{:S(2)}, u32[]{:S(2)}) async-start(bf16[4,12,1536]{2,1,0:T(8,128)(2,1)} %broadcast_in_dim.48), calls=%async_computation.3 | async-start | bytes 393216 | tf_op jit(solution)/shard_map/all_to_all | solution.py:19
  69.8 73.2 %all-gather.6.cloned.1.call-start = ((), (), s32[]{:S(2)}) async-start(), calls=%async_computation.11 | async-start | bytes 1474560 | tf_op jit(solution)/shard_map/all_gather | solution.py:125
  91.5 1.0 copy-start.2
  143.0 1.3 copy-start.3
  144.3 1.3 copy-start.4
Sparse Core Ops, SparseCore 0:
  24.5 62.0 all-gather.3
  93.4 32.0 all-gather.5

commit v5 on v4

--- a/solution.py
+++ b/solution.py
@@ -103,8 +103,11 @@
     before = lax.broadcasted_iota(jnp.int32, (blocks, 1, 1), 0) < place
     edge, here, before = lax.optimization_barrier((edge, here, before))
     edge_wide = lax.all_gather(edge, "x", axis=1, tiled=True)
-    edge_wide, corner = lax.optimization_barrier((edge_wide, corner))
-    corner_wide = lax.all_gather(corner, "x", axis=1, tiled=True)
+    half = bond // 2
+    core = lax.axis_index("core")
+    corner_rows = lax.dynamic_slice_in_dim(corner, core * half, half, 0)
+    edge_wide, corner_rows = lax.optimization_barrier((edge_wide, corner_rows))
+    corner_wide = lax.all_gather(corner_rows, "x", axis=1, tiled=True)
     vec_low = vector.astype(BF16)
     cross = lax.dot_general(
         vec_low, edge_wide, (((0,), (0,)), ((), ())), preferred_element_type=F32
@@ -115,12 +118,16 @@
     cross = total(spread(cross.astype(BF16), "zh"))
     cross_all = spread(cross.astype(BF16), "x").reshape(-1, bond)
 
-    other = dot(dot(cross_all, corner_wide).astype(BF16), tri_inv).astype(BF16)
-    other = other.reshape(blocks, -1, width)
+    mine = dot(corner_wide, tri_inv).astype(BF16)
+    theirs = lax.ppermute(mine, "core", [(0, 1), (1, 0)])
+    own_map = jnp.concatenate(
+        [jnp.where(core == 0, mine, theirs), jnp.where(core == 0, theirs, mine)]
+    )
+    proj = dot(edge_wide, own_map).astype(BF16)
+
+    other = dot(cross_all, own_map).astype(BF16).reshape(blocks, -1, width)
     own = swap(other, "x")
 
-    own_map = dot(corner_wide, tri_inv).astype(BF16)
-    proj = dot(edge_wide, own_map).astype(BF16)
     proj = jnp.concatenate([proj, own_map[: width - rows]])
     proj_blocks = lax.all_gather(proj, "x", axis=0)
 

time: 217 us -> 237 us (1.092)
  waiting for transfers between devices: 16.8 us -> 60.9 us
  blocking collectives: 154 us -> 112 us
  starting transfers between devices: 12.4 us -> 25.5 us
  local copies, waits for them, and re-layouts: 4.19 us -> 9.18 us
  matrix products: 9.48 us -> 4.73 us
  other arithmetic: 2.19 us -> 6.32 us
    all_to_all x9 -> x6, blocking collectives: 91.3 us -> 53.2 us  [swap(): return lax.all_to_all(pieces, axis, split_axis=0, concat_axis=0, tiled=True)]
    all_to_all x1 -> x4, waiting for transfers between devices: 0.01 us -> 28.5 us  [swap(): return lax.all_to_all(pieces, axis, split_axis=0, concat_axis=0, tiled=True)]
    all_gather x1, waiting for transfers between devices: 16.7 us -> 32.4 us  [on_device(): corner_wide = lax.all_gather(corner_rows, 'x', axis=1, tiled=True)]
    all_to_all x1 -> x4, starting transfers between devices: 12.4 us -> 23.5 us  [swap(): return lax.all_to_all(pieces, axis, split_axis=0, concat_axis=0, tiled=True)]
    dot_general x3, matrix products: 8.97 us -> 4.23 us  [dot(): return jnp.dot(a, b, preferred_element_type=F32)]
    psum x5, blocking collectives: 45.9 us -> 41.8 us  [on_device(): sums = lax.psum(sums, axis)]
  transfers between devices with their start and end apart: 3 -> 7, of which waited for: 1 -> 4; matrix products, arithmetic and copies ran while one was open for 6% -> 7% of each run, Pallas kernels for 0% -> 0%
where the time goes in v5:
time: 237 us; the launch traced here: 236 us
  blocking collectives  112 us (47%)
  waiting for transfers between devices  60.9 us (26%)
  starting transfers between devices  25.5 us (11%)
  between operations  14.3 us (6%)
  local copies, waits for them, and re-layouts  9.18 us (4%)
  other arithmetic  6.32 us (3%)
  matrix products  4.73 us (2%)
  Pallas kernels  3.14 us (1%)
    all_to_all x6, blocking collectives, swap(): return lax.all_to_all(pieces, axis, split_axis=0, concat_axis=0, tiled=True)  53.2 us
    psum x5, blocking collectives, on_device(): sums = lax.psum(sums, axis)  41.8 us
    all_gather x1, waiting for transfers between devices, on_device(): corner_wide = lax.all_gather(corner_rows, 'x', axis=1, tiled=True)  32.4 us
    all_to_all x4, waiting for transfers between devices, swap(): return lax.all_to_all(pieces, axis, split_axis=0, concat_axis=0, tiled=True)  28.5 us
    all_to_all x4, starting transfers between devices, swap(): return lax.all_to_all(pieces, axis, split_axis=0, concat_axis=0, tiled=True)  23.5 us
    all_gather x1, blocking collectives, on_device(): edge_wide = lax.all_gather(edge, 'x', axis=1, tiled=True)  17.1 us
  transfers between devices with their start and end apart: 7, of which 4 were waited for; matrix products, arithmetic and copies ran while one was open for 7% of the time, Pallas kernels for 0%

profile of v5, /device:TPU:2, one launch (start us, length us, event | category | flops | bytes accessed | tf_op | source)
XLA Modules:
  0.0 236.1 jit_solution(13518189296049741134)
XLA Ops:
  7.3 17.1 %all_gather.12 = bf16[256,1536]{1,0:T(8,128)(2,1)S(1)} all-gather(bf16[256,384]{1,0:T(8,128)(2,1)} %param.4), channel_id=1, replica_groups=mesh['y'=4,'zh'=4,'zl'=4,'core'=2,'x'=4] {'x'}, dimensions={1}, use_global_device_ids=true | all-gather | bytes 983040 | tf_op jit(solution)/shard_map/all_gather | solution.py:105
  25.8 4.7 %all_to_all.50 = bf16[2,192,1536]{2,1,0:T(8,128)(2,1)S(1)} all-to-all(bf16[2,192,1536]{2,1,0:T(8,128)(2,1)S(1)} %bitcast.23), channel_id=1, replica_groups=mesh['y'=4,'zh'=4,'zl'=4,'core'=2,'x'=4] {'core'}, dimensions={0} | all-to-all | bytes 2359296 | tf_op jit(solution)/shard_map/all_to_all | solution.py:19
  31.6 3.5 %all-to-all-start.1 = ((bf16[4,48,1536]{2,1,0:T(8,128)(2,1)}), bf16[4,48,1536]{2,1,0:T(8,128)(2,1)S(1)}, u32[]{:S(2)}, u32[]{:S(2)}) async-start(bf16[4,48,1536]{2,1,0:T(8,128)(2,1)} %bitcast.25), calls=%async_computation.1 | async-start | bytes 1179648 | tf_op jit(solution)/shard_map/all_to_all | solution.py:19
  35.1 32.4 %all-gather.4.cloned.1.call-done = bf16[768,1536]{1,0:T(8,128)(2,1)} async-done(((bf16[768,384]{1,0:T(8,128)(2,1)}), bf16[768,1536]{1,0:T(8,128)(2,1)}) %all-gather.4.cloned.1.call-update) | async-done | bytes 2359312 | tf_op jit(solution)/shard_map/all_gather | solution.py:110
  67.5 3.4 %convolution_convert_fusion = bf16[768,384]{1,0:T(8,128)(2,1)S(1)} fusion(bf16[768,1536]{1,0:T(8,128)(2,1)} %all-gather.4.cloned.1.call-done, bf16[1536,384]{1,0:T(8,128)(2,1)} %param.6), kind=kOutput, calls=%fused_computation.2 | convolution fusion | flops 906264576 | bytes 4128768 | tf_op jit(solution)/shard_map/dot_general | solution.py:44
  70.8 1.9 collective-permute-start
  73.5 1.6 reshape.37
  75.2 4.8 %all-to-all-start.2 = ((bf16[4,12,1536]{2,1,0:T(8,128)(2,1)}), bf16[4,12,1536]{2,1,0:T(8,128)(2,1)S(1)}, u32[]{:S(2)}, u32[]{:S(2)}) async-start(bf16[4,12,1536]{2,1,0:T(8,128)(2,1)} %reshape.37), calls=%async_computation.2 | async-start | bytes 393216 | tf_op jit(solution)/shard_map/all_to_all | solution.py:19
  80.0 8.1 %all-to-all-done.2 = bf16[4,12,1536]{2,1,0:T(8,128)(2,1)S(1)} async-done(((bf16[4,12,1536]{2,1,0:T(8,128)(2,1)}), bf16[4,12,1536]{2,1,0:T(8,128)(2,1)S(1)}, u32[]{:S(2)}, u32[]{:S(2)}) %all-to-all-start.2) | async-done | bytes 147488 | tf_op jit(solution)/shard_map/all_to_all | solution.py:19
  88.8 11.0 %all-to-all-start.3 = ((bf16[4,12,1536]{2,1,0:T(8,128)(2,1)}), bf16[4,12,1536]{2,1,0:T(8,128)(2,1)}, u32[]{:S(2)}, u32[]{:S(2)}) async-start(bf16[4,12,1536]{2,1,0:T(8,128)(2,1)} %broadcast_in_dim.48), calls=%async_computation.3 | async-start | bytes 393216 | tf_op jit(solution)/shard_map/all_to_all | solution.py:19
  102.6 13.0 %all-to-all-done.3 = bf16[4,12,1536]{2,1,0:T(8,128)(2,1)} async-done(((bf16[4,12,1536]{2,1,0:T(8,128)(2,1)}), bf16[4,12,1536]{2,1,0:T(8,128)(2,1)}, u32[]{:S(2)}, u32[]{:S(2)}) %all-to-all-start.3) | async-done | bytes 147488 | tf_op jit(solution)/shard_map/all_to_all | solution.py:19
  116.6 11.1 %all_to_all.51 = bf16[4,12,1536]{2,1,0:T(8,128)(2,1)S(1)} all-to-all(bf16[4,12,1536]{2,1,0:T(8,128)(2,1)S(1)} %broadcast_in_dim.49), channel_id=1, replica_groups=mesh['y'=4,'zh'=4,'zl'=4,'core'=2,'x'=4] {'x'}, dimensions={0} | all-to-all | bytes 294912 | tf_op jit(solution)/shard_map/all_to_all | solution.py:19
  128.1 8.5 %all_to_all.52 = bf16[4,12,384]{2,1,0:T(8,128)(2,1)S(1)} all-to-all(bf16[4,12,384]{2,1,0:T(8,128)(2,1)S(1)} %reshape.39), channel_id=1, replica_groups=mesh['y'=4,'zh'=4,'zl'=4,'core'=2,'x'=4] {'x'}, dimensions={0} | all-to-all | bytes 73728 | tf_op jit(solution)/shard_map/all_to_all | solution.py:19
  136.7 9.0 %all_to_all.53 = bf16[4,4,12,384]{3,1,2,0:T(4,128)(2,1)S(1)} all-to-all(bf16[4,4,12,384]{3,1,2,0:T(4,128)(2,1)S(1)} %broadcast_in_dim.50), channel_id=1, replica_groups=mesh['y'=4,'zh'=4,'zl'=4,'core'=2,'x'=4] {'zl'}, dimensions={0} | all-to-all | bytes 294912 | tf_op jit(solution)/shard_map/all_to_all | solution.py:19
  146.7 4.3 %all-to-all-start.7 = ((bf16[4,4,48,384]{3,2,1,0:T(8,128)(2,1)}), bf16[4,4,48,384]{3,2,1,0:T(8,128)(2,1)}, u32[]{:S(2)}, u32[]{:S(2)}) async-start(bf16[4,4,48,384]{3,2,1,0:T(8,128)(2,1)} %broadcast_in_dim.52), calls=%async_computation.7 | async-start | bytes 1179648 | tf_op jit(solution)/shard_map/all_to_all | solution.py:19
  152.1 7.4 %all-to-all-done.7 = bf16[4,4,48,384]{3,2,1,0:T(8,128)(2,1)} async-done(((bf16[4,4,48,384]{3,2,1,0:T(8,128)(2,1)}), bf16[4,4,48,384]{3,2,1,0:T(8,128)(2,1)}, u32[]{:S(2)}, u32[]{:S(2)}) %all-to-all-start.7) | async-done | bytes 589856 | tf_op jit(solution)/shard_map/all_to_all | solution.py:19
  160.7 4.7 %all_to_all.54 = bf16[2,4,192,384]{3,2,1,0:T(8,128)(2,1)S(1)} all-to-all(bf16[2,4,192,384]{3,2,1,0:T(8,128)(2,1)S(1)} %broadcast_in_dim.54), channel_id=1, replica_groups=mesh['y'=4,'zh'=4,'zl'=4,'core'=2,'x'=4] {'core'}, dimensions={0} | all-to-all | bytes 2359296 | tf_op jit(solution)/shard_map/all_to_all | solution.py:19
  169.1 2.0 shard_map.59
  171.1 15.2 %all_to_all.55.shares = bf16[4,256,384]{2,1,0:T(8,128)(2,1)S(1)} all-to-all(bf16[4,256,384]{2,1,0:T(8,128)(2,1)S(1)} %shard_map.59), channel_id=1, replica_groups=mesh['y'=4,'zh'=4,'zl'=4,'core'=2,'x'=4] {'x'}, dimensions={0} | all-to-all | bytes 1572864 | tf_op jit(solution)/shard_map/all_to_all | solution.py:19
  186.5 2.5 %psum.35 = f32[8,128]{1,0:T(8,128)S(1)} all-reduce(f32[8,128]{1,0:T(8,128)S(1)} %get-tuple-element.14), channel_id=1, replica_groups=mesh['y'=4,'zh'=4,'zl'=4,'core'=2,'x'=4] {'core'}, use_global_device_ids=true, to_apply=%region_4.5 | all-reduce | flops 1024 | bytes 8192 | tf_op jit(solution)/shard_map/psum | solution.py:157
  189.0 9.2 %psum.36 = f32[8,128]{1,0:T(8,128)S(1)} all-reduce(f32[8,128]{1,0:T(8,128)S(1)} %psum.35), channel_id=1, replica_groups=mesh['y'=4,'zh'=4,'zl'=4,'core'=2,'x'=4] {'x'}, use_global_device_ids=true, to_apply=%region_5.6 | all-reduce | flops 1024 | bytes 8192 | tf_op jit(solution)/shard_map/psum | solution.py:157
  198.1 8.9 %psum.37 = f32[8,128]{1,0:T(8,128)S(1)} all-reduce(f32[8,128]{1,0:T(8,128)S(1)} %psum.36), channel_id=1, replica_groups=mesh['y'=4,'zh'=4,'zl'=4,'core'=2,'x'=4] {'y'}, use_global_device_ids=true, to_apply=%region_6.7 | all-reduce | flops 1024 | bytes 8192 | tf_op jit(solution)/shard_map/psum | solution.py:157
  207.0 9.2 %psum.38 = f32[8,128]{1,0:T(8,128)S(1)} all-reduce(f32[8,128]{1,0:T(8,128)S(1)} %psum.37), channel_id=1, replica_groups=mesh['y'=4,'zh'=4,'zl'=4,'core'=2,'x'=4] {'zl'}, use_global_device_ids=true, to_apply=%region_7.8 | all-reduce | flops 1024 | bytes 8192 | tf_op jit(solution)/shard_map/psum | solution.py:157
  216.2 12.0 %psum.39.sums = f32[8,128]{1,0:T(8,128)S(1)} all-reduce(f32[8,128]{1,0:T(8,128)S(1)} %psum.38), channel_id=1, replica_groups=mesh['y'=4,'zh'=4,'zl'=4,'core'=2,'x'=4] {'zh'}, use_global_device_ids=true, to_apply=%region_8.9 | all-reduce | flops 1024 | bytes 8192 | tf_op jit(solution)/shard_map/psum | solution.py:157
  (50 shorter events, 16.4 us)
Async XLA Ops:
  7.2 17.2 %copy-start = (bf16[1536,384]{1,0:T(8,128)(2,1)S(1)}, bf16[1536,384]{1,0:T(8,128)(2,1)}, u32[]{:S(2)}) copy-start(bf16[1536,384]{1,0:T(8,128)(2,1)} %param.5) | copy-start | bytes 3538948
  7.2 60.3 %all-gather.4.cloned.1.call-start = ((), (), s32[]{:S(2)}) async-start(), calls=%async_computation.10 | async-start | bytes 2949120 | tf_op jit(solution)/shard_map/all_gather | solution.py:110
  7.2 18.0 %copy-start.1 = (f32[256,384]{1,0:T(8,128)S(1)}, f32[256,384]{1,0:T(8,128)}, u32[]{:S(2)}) copy-start(f32[256,384]{1,0:T(8,128)} %vec.5) | copy-start | bytes 1179652
  31.6 41.1 %all-to-all-start.1 = ((bf16[4,48,1536]{2,1,0:T(8,128)(2,1)}), bf16[4,48,1536]{2,1,0:T(8,128)(2,1)S(1)}, u32[]{:S(2)}, u32[]{:S(2)}) async-start(bf16[4,48,1536]{2,1,0:T(8,128)(2,1)} %bitcast.25), calls=%async_computation.1 | async-start | bytes 1179648 | tf_op jit(solution)/shard_map/all_to_all | solution.py:19
  70.8 18.0 %copy-start.7 = (bf16[768,384]{1,0:T(8,128)(2,1)}, bf16[768,384]{1,0:T(8,128)(2,1)S(1)}, u32[]{:S(2)}) copy-start(bf16[768,384]{1,0:T(8,128)(2,1)S(1)} %convolution_convert_fusion) | copy-start | bytes 1769476
  70.8 29.0 %collective-permute-start = (bf16[768,384]{1,0:T(8,128)(2,1)S(1)}, bf16[768,384]{1,0:T(8,128)(2,1)}, u32[]{:S(2)}, u32[]{:S(2)}) collective-permute-start(bf16[768,384]{1,0:T(8,128)(2,1)S(1)} %convolution_convert_fusion), channel_id=1, source_target_pairs={{0,4},{4,0},{1,5},{5,1},{2,6},{6,2},{3,7},{7,3},{8,12},{12,8},{9,1... | collective-permute-start | bytes 1769480 | tf_op jit(solution)/shard_map/ppermute | solution.py:122
  75.2 12.9 %all-to-all-start.2 = ((bf16[4,12,1536]{2,1,0:T(8,128)(2,1)}), bf16[4,12,1536]{2,1,0:T(8,128)(2,1)S(1)}, u32[]{:S(2)}, u32[]{:S(2)}) async-start(bf16[4,12,1536]{2,1,0:T(8,128)(2,1)} %reshape.37), calls=%async_computation.2 | async-start | bytes 393216 | tf_op jit(solution)/shard_map/all_to_all | solution.py:19
  88.8 26.7 %all-to-all-start.3 = ((bf16[4,12,1536]{2,1,0:T(8,128)(2,1)}), bf16[4,12,1536]{2,1,0:T(8,128)(2,1)}, u32[]{:S(2)}, u32[]{:S(2)}) async-start(bf16[4,12,1536]{2,1,0:T(8,128)(2,1)} %broadcast_in_dim.48), calls=%async_computation.3 | async-start | bytes 393216 | tf_op jit(solution)/shard_map/all_to_all | solution.py:19
  99.8 66.7 %all-gather.6.cloned.1.call-start = ((), (), s32[]{:S(2)}) async-start(), calls=%async_computation.11 | async-start | bytes 1474560 | tf_op jit(solution)/shard_map/all_gather | solution.py:132
  101.2 26.5 %copy-start.4 = (bf16[768,384]{1,0:T(8,128)(2,1)}, bf16[768,384]{1,0:T(8,128)(2,1)S(1)}, u32[]{:S(2)}) copy-start(bf16[768,384]{1,0:T(8,128)(2,1)S(1)} %get-tuple-element.17) | copy-start | bytes 1769476
  101.2 26.5 %copy-start.6 = (bf16[768,384]{1,0:T(8,128)(2,1)}, bf16[768,384]{1,0:T(8,128)(2,1)S(1)}, u32[]{:S(2)}) copy-start(bf16[768,384]{1,0:T(8,128)(2,1)S(1)} %get-tuple-element.16) | copy-start | bytes 1769476
  145.8 5.2 %copy-start.5 = (bf16[768,384]{1,0:T(8,128)(2,1)S(1)}, bf16[768,384]{1,0:T(8,128)(2,1)}, u32[]{:S(2)}) copy-start(bf16[768,384]{1,0:T(8,128)(2,1)} %copy-done.4) | copy-start | bytes 1769476
  146.7 12.8 %all-to-all-start.7 = ((bf16[4,4,48,384]{3,2,1,0:T(8,128)(2,1)}), bf16[4,4,48,384]{3,2,1,0:T(8,128)(2,1)}, u32[]{:S(2)}, u32[]{:S(2)}) async-start(bf16[4,4,48,384]{3,2,1,0:T(8,128)(2,1)} %broadcast_in_dim.52), calls=%async_computation.7 | async-start | bytes 1179648 | tf_op jit(solution)/shard_map/all_to_all | solution.py:19
  166.6 1.3 copy-start.2
  167.8 1.3 copy-start.3
Sparse Core Ops, SparseCore 0:
  25.4 42.0 all-gather.3
  103.3 33.1 all-gather.5

commit v6 on v5

--- a/solution.py
+++ b/solution.py
@@ -48,19 +48,43 @@
     return lax.dot_general(a, b, (((1,), (1,)), ((), ())), preferred_element_type=F32)
 
 
-def partial_kernel(place, vec, proj, sym, own_map, out):
+def map_half_kernel(after, corner_rows, tri_inv, out):
+    del after
+    out[...] = dot(corner_rows[...], tri_inv[...]).astype(BF16)
+
+
+def join_kernel(core, mine, theirs, edge_wide, own_map, proj):
+    half = mine.shape[0]
+    rows = edge_wide.shape[0]
+    low = jnp.broadcast_to(core[0] == 0, mine.shape)
+    own_map[:half] = jnp.where(low, mine[...], theirs[...])
+    own_map[half:] = jnp.where(low, theirs[...], mine[...])
+    proj[:rows] = dot(edge_wide[...], own_map[...]).astype(BF16)
+    proj[rows:] = jnp.zeros((proj.shape[0] - rows, proj.shape[1]), BF16)
+
+
+def partial_kernel(place, vec, sym, proj_in, map_in, out, proj, own_map, sem):
     rows, width = vec.shape
-    blocks = sym.shape[0]
+    blocks = proj.shape[0]
+    fetch_proj = pltpu.make_async_copy(proj_in.at[:, :rows], proj, sem.at[0])
+    fetch_map = pltpu.make_async_copy(map_in, own_map, sem.at[1])
+    fetch_proj.start()
+    fetch_map.start()
     first = lax.broadcasted_iota(jnp.int32, (width, width), 0)
     second = lax.broadcasted_iota(jnp.int32, (width, width), 1)
     zero = jnp.zeros((width, width), BF16)
     acc = jnp.zeros((rows, width), F32)
+    fetch_proj.wait()
     for k in range(blocks):
         shift = (place[0] - k) * width
-        part = proj[k, :rows]
-        acc += dot(part, jnp.where(first <= second + shift, sym[k], zero))
-        acc += dot_turned(part, jnp.where(first < second - shift, sym[k], zero))
+        block = jnp.concatenate(
+            [sym[c, y, k] for c in range(sym.shape[0]) for y in range(sym.shape[1])]
+        )
+        part = proj[k]
+        acc += dot(part, jnp.where(first <= second + shift, block, zero))
+        acc += dot_turned(part, jnp.where(first < second - shift, block, zero))
     corrected = (vec[...] - acc).astype(BF16)
+    fetch_map.wait()
     for k in range(blocks):
         share = dot_turned(corrected, own_map[k * width : (k + 1) * width])
         out[k] = share.astype(BF16)
@@ -81,7 +105,8 @@
 
 
 def finish_kernel(count, sums, vec, dedge, out, coeffs):
-    vv, vd, dd = (jnp.sum(sums[i : i + 1], axis=1, keepdims=True) for i in range(3))
+    lines = sum(sums[i] for i in range(sums.shape[0]))
+    vv, vd, dd = (jnp.sum(lines[i : i + 1], axis=1, keepdims=True) for i in range(3))
     along = (vv - vd) / count
     keep = 1.0 - along
     square = (keep * keep * vv - 2.0 * keep * vd + dd) / count
@@ -101,10 +126,13 @@
     rows_total = rows * lax.axis_size(ROW)
 
     before = lax.broadcasted_iota(jnp.int32, (blocks, 1, 1), 0) < place
-    edge, here, before = lax.optimization_barrier((edge, here, before))
+    core = lax.axis_index("core")
+    core_here = core[None]
+    edge, here, core_here, before = lax.optimization_barrier(
+        (edge, here, core_here, before)
+    )
     edge_wide = lax.all_gather(edge, "x", axis=1, tiled=True)
     half = bond // 2
-    core = lax.axis_index("core")
     corner_rows = lax.dynamic_slice_in_dim(corner, core * half, half, 0)
     edge_wide, corner_rows = lax.optimization_barrier((edge_wide, corner_rows))
     corner_wide = lax.all_gather(corner_rows, "x", axis=1, tiled=True)
@@ -115,33 +143,53 @@
     cross = cross * (1.0 / rows_total)
     for axis in ("core", "y", "zl"):
         cross = scatter_sum(cross.astype(BF16), axis)
-    cross = total(spread(cross.astype(BF16), "zh"))
+    cross = cross.astype(BF16)
+
+    mine = pl.pallas_call(
+        map_half_kernel,
+        out_shape=jax.ShapeDtypeStruct((half, width), BF16),
+        in_specs=[pl.BlockSpec(memory_space=pl.ANY), VMEM, VMEM],
+        out_specs=VMEM,
+        compiler_params=PARAMS,
+        cost_estimate=pl.CostEstimate(
+            flops=2 * half * bond * width, bytes_accessed=4 * half * bond, transcendentals=0
+        ),
+    )(cross, corner_wide, tri_inv)
+    theirs = lax.ppermute(mine, "core", [(0, 1), (1, 0)])
+    own_map, proj = pl.pallas_call(
+        join_kernel,
+        out_shape=(
+            jax.ShapeDtypeStruct((bond, width), BF16),
+            jax.ShapeDtypeStruct((width, width), BF16),
+        ),
+        in_specs=[SMEM] + [VMEM] * 3,
+        out_specs=(VMEM, VMEM),
+        compiler_params=PARAMS,
+        cost_estimate=pl.CostEstimate(
+            flops=2 * rows * bond * width, bytes_accessed=4 * half * bond, transcendentals=0
+        ),
+    )(core_here, mine, theirs, edge_wide)
+    proj_blocks = lax.all_gather(proj, "x", axis=0)
+
+    cross = total(spread(cross, "zh"))
     cross_all = spread(cross.astype(BF16), "x").reshape(-1, bond)
-
-    mine = dot(corner_wide, tri_inv).astype(BF16)
-    theirs = lax.ppermute(mine, "core", [(0, 1), (1, 0)])
-    own_map = jnp.concatenate(
-        [jnp.where(core == 0, mine, theirs), jnp.where(core == 0, theirs, mine)]
-    )
-    proj = dot(edge_wide, own_map).astype(BF16)
-
     other = dot(cross_all, own_map).astype(BF16).reshape(blocks, -1, width)
     own = swap(other, "x")
-
-    proj = jnp.concatenate([proj, own_map[: width - rows]])
-    proj_blocks = lax.all_gather(proj, "x", axis=0)
-
-    chosen = jnp.where(before, other, own)
-    for axis in ("zl", "y", "core"):
-        chosen = join_rows(chosen, axis)
+    chosen = join_rows(jnp.where(before, other, own), "zl")
+    chosen = spread(spread(chosen, "y"), "core")
 
     shares = pl.pallas_call(
         partial_kernel,
         out_shape=jax.ShapeDtypeStruct((blocks, rows, width), BF16),
-        in_specs=[SMEM] + [VMEM] * 4,
+        in_specs=[SMEM, VMEM, VMEM] + [pl.BlockSpec(memory_space=pl.ANY)] * 2,
         out_specs=VMEM,
-        compiler_params=PARAMS,
-    )(here, vector, proj_blocks, chosen, own_map)
+        scratch_shapes=[
+            pltpu.VMEM((blocks, rows, width), BF16),
+            pltpu.VMEM((bond, width), BF16),
+            pltpu.SemaphoreType.DMA((2,)),
+        ],
+        compiler_params=PARAMS,
+    )(here, vector, chosen, proj_blocks, own_map)
     shares = swap(shares, "x")
     dedge, sums = pl.pallas_call(
         edge_kernel,
@@ -153,8 +201,9 @@
         out_specs=(VMEM, VMEM),
         compiler_params=PARAMS,
     )(vector, shares)
-    for axis in ("core", "x", "y", "zl", "zh"):
+    for axis in ("core", "x", "y", "zl"):
         sums = lax.psum(sums, axis)
+    sums = spread(sums, "zh")
     return pl.pallas_call(
         functools.partial(finish_kernel, float(rows_total * bond)),
         out_shape=(

time: 237 us -> 228 us (0.962)
  blocking collectives: 112 us -> 156 us
  waiting for transfers between devices: 60.9 us -> 22 us
  starting transfers between devices: 25.5 us -> 14.1 us
  other arithmetic: 6.32 us -> 2.36 us
  matrix products: 4.73 us -> 0.81 us
  local copies, waits for them, and re-layouts: 9.18 us -> 12.5 us
  Pallas kernels: 3.14 us -> 5.54 us
    all_to_all x6 -> x10, blocking collectives: 53.2 us -> 109 us  [swap(): return lax.all_to_all(pieces, axis, split_axis=0, concat_axis=0, tiled=True)]
    all_gather x1, waiting for transfers between devices: 32.4 us -> 9.89 us  [on_device(): corner_wide = lax.all_gather(corner_rows, 'x', axis=1, tiled=True)]
    all_to_all x4 -> x1, waiting for transfers between devices: 28.5 us -> 12 us  [swap(): return lax.all_to_all(pieces, axis, split_axis=0, concat_axis=0, tiled=True)]
    psum x5 -> x4, blocking collectives: 41.8 us -> 29.7 us  [on_device(): sums = lax.psum(sums, axis)]
    all_to_all x4 -> x1, starting transfers between devices: 23.5 us -> 12.2 us  [swap(): return lax.all_to_all(pieces, axis, split_axis=0, concat_axis=0, tiled=True)]
    unnamed x16 -> x24, local copies, waits for them, and re-layouts: 2.57 us -> 9.75 us
    dot_general x3 -> x1, matrix products: 4.23 us -> 0.3 us  [dot(): return jnp.dot(a, b, preferred_element_type=F32)]
  transfers between devices with their start and end apart: 7 -> 4, of which waited for: 4 -> 2; matrix products, arithmetic and copies ran while one was open for 7% -> 2% of each run, Pallas kernels for 0% -> 0%
where the time goes in v6:
time: 228 us; the launch traced here: 227 us
  blocking collectives  156 us (68%)
  waiting for transfers between devices  22 us (10%)
  between operations  14.2 us (6%)
  starting transfers between devices  14.1 us (6%)
  local copies, waits for them, and re-layouts  12.5 us (5%)
  Pallas kernels  5.54 us (2%)
  other arithmetic  2.36 us (1%)
    all_to_all x10, blocking collectives, swap(): return lax.all_to_all(pieces, axis, split_axis=0, concat_axis=0, tiled=True)  109 us
    psum x4, blocking collectives, on_device(): sums = lax.psum(sums, axis)  29.7 us
    all_gather x1, blocking collectives, on_device(): edge_wide = lax.all_gather(edge, 'x', axis=1, tiled=True)  17.1 us
    all_to_all x1, starting transfers between devices, swap(): return lax.all_to_all(pieces, axis, split_axis=0, concat_axis=0, tiled=True)  12.2 us
    all_to_all x1, waiting for transfers between devices, swap(): return lax.all_to_all(pieces, axis, split_axis=0, concat_axis=0, tiled=True)  12 us
    all_gather x1, waiting for transfers between devices, on_device(): corner_wide = lax.all_gather(corner_rows, 'x', axis=1, tiled=True)  9.89 us
    unnamed x24, local copies, waits for them, and re-layouts  9.75 us
  transfers between devices with their start and end apart: 4, of which 2 were waited for; matrix products, arithmetic and copies ran while one was open for 2% of the time, Pallas kernels for 0%

profile of v6, /device:TPU:2, one launch (start us, length us, event | category | flops | bytes accessed | tf_op | source)
XLA Modules:
  0.0 227.3 jit_solution(2137568452097873870)
XLA Ops:
  7.3 17.1 %all_gather.12.edge_wide = bf16[256,1536]{1,0:T(8,128)(2,1)S(1)} all-gather(bf16[256,384]{1,0:T(8,128)(2,1)} %param.4), channel_id=1, replica_groups=mesh['y'=4,'zh'=4,'zl'=4,'core'=2,'x'=4] {'x'}, dimensions={1}, use_global_device_ids=true | all-gather | bytes 983040 | tf_op jit(solution)/shard_map/all_gather | solution.py:134
  25.8 4.7 %all_to_all.55 = bf16[2,192,1536]{2,1,0:T(8,128)(2,1)S(1)} all-to-all(bf16[2,192,1536]{2,1,0:T(8,128)(2,1)S(1)} %bitcast.15), channel_id=1, replica_groups=mesh['y'=4,'zh'=4,'zl'=4,'core'=2,'x'=4] {'core'}, dimensions={0} | all-to-all | bytes 2359296 | tf_op jit(solution)/shard_map/all_to_all | solution.py:19
  31.6 14.2 %all_to_all.56 = bf16[4,48,1536]{2,1,0:T(8,128)(2,1)S(1)} all-to-all(bf16[4,48,1536]{2,1,0:T(8,128)(2,1)} %bitcast.16), channel_id=1, replica_groups=mesh['y'=4,'zh'=4,'zl'=4,'core'=2,'x'=4] {'y'}, dimensions={0} | all-to-all | bytes 1179648 | tf_op jit(solution)/shard_map/all_to_all | solution.py:19
  46.0 11.6 %all_to_all.57 = bf16[4,12,1536]{2,1,0:T(8,128)(2,1)S(1)} all-to-all(bf16[4,12,1536]{2,1,0:T(8,128)(2,1)S(1)} %reshape.35), channel_id=1, replica_groups=mesh['y'=4,'zh'=4,'zl'=4,'core'=2,'x'=4] {'zl'}, dimensions={0} | all-to-all | bytes 294912 | tf_op jit(solution)/shard_map/all_to_all | solution.py:19
  57.6 9.9 %all-gather.4.cloned.1.call-done.corner_rows = bf16[768,1536]{1,0:T(8,128)(2,1)} async-done(((bf16[768,384]{1,0:T(8,128)(2,1)}), bf16[768,1536]{1,0:T(8,128)(2,1)}) %all-gather.4.cloned.1.call-update) | async-done | bytes 2359312 | tf_op jit(solution)/shard_map/all_gather | solution.py:138
  67.5 1.7 copy-done.3
  70.4 1.4 shard_map.59.mine
  72.4 1.9 collective-permute-start
  74.3 1.5 broadcast_in_dim.57
  75.8 12.2 %all-to-all-start.3 = ((bf16[4,12,1536]{2,1,0:T(8,128)(2,1)}), bf16[4,12,1536]{2,1,0:T(8,128)(2,1)}, u32[]{:S(2)}, u32[]{:S(2)}) async-start(bf16[4,12,1536]{2,1,0:T(8,128)(2,1)} %broadcast_in_dim.57), calls=%async_computation.3 | async-start | bytes 393216 | tf_op jit(solution)/shard_map/all_to_all | solution.py:19
  92.3 12.0 %all-to-all-done.3 = bf16[4,12,1536]{2,1,0:T(8,128)(2,1)} async-done(((bf16[4,12,1536]{2,1,0:T(8,128)(2,1)}), bf16[4,12,1536]{2,1,0:T(8,128)(2,1)}, u32[]{:S(2)}, u32[]{:S(2)}) %all-to-all-start.3) | async-done | bytes 147488 | tf_op jit(solution)/shard_map/all_to_all | solution.py:19
  105.3 10.4 %all_to_all.58 = bf16[4,12,1536]{2,1,0:T(8,128)(2,1)S(1)} all-to-all(bf16[4,12,1536]{2,1,0:T(8,128)(2,1)S(1)} %broadcast_in_dim.58), channel_id=1, replica_groups=mesh['y'=4,'zh'=4,'zl'=4,'core'=2,'x'=4] {'x'}, dimensions={0} | all-to-all | bytes 294912 | tf_op jit(solution)/shard_map/all_to_all | solution.py:19
  116.1 8.4 %all_to_all.59 = bf16[4,12,384]{2,1,0:T(8,128)(2,1)S(1)} all-to-all(bf16[4,12,384]{2,1,0:T(8,128)(2,1)S(1)} %reshape.37), channel_id=1, replica_groups=mesh['y'=4,'zh'=4,'zl'=4,'core'=2,'x'=4] {'x'}, dimensions={0} | all-to-all | bytes 73728 | tf_op jit(solution)/shard_map/all_to_all | solution.py:19
  124.7 11.5 %all_to_all.60 = bf16[4,4,12,384]{3,1,2,0:T(4,128)(2,1)S(1)} all-to-all(bf16[4,4,12,384]{3,1,2,0:T(4,128)(2,1)S(1)} %broadcast_in_dim.59), channel_id=1, replica_groups=mesh['y'=4,'zh'=4,'zl'=4,'core'=2,'x'=4] {'zl'}, dimensions={0} | all-to-all | bytes 294912 | tf_op jit(solution)/shard_map/all_to_all | solution.py:19
  136.2 12.5 %all_to_all.61 = bf16[4,4,48,384]{3,2,1,0:T(8,128)(2,1)S(1)} all-to-all(bf16[4,4,48,384]{3,2,1,0:T(8,128)(2,1)S(1)} %broadcast_in_dim.61), channel_id=1, replica_groups=mesh['y'=4,'zh'=4,'zl'=4,'core'=2,'x'=4] {'y'}, dimensions={0} | all-to-all | bytes 1179648 | tf_op jit(solution)/shard_map/all_to_all | solution.py:19
  148.9 5.5 %all_to_all.62.sym = bf16[2,4,4,48,384]{4,3,2,1,0:T(8,128)(2,1)} all-to-all(bf16[2,4,4,48,384]{4,3,2,1,0:T(8,128)(2,1)S(1)} %broadcast_in_dim.62), channel_id=1, replica_groups=mesh['y'=4,'zh'=4,'zl'=4,'core'=2,'x'=4] {'core'}, dimensions={0} | all-to-all | bytes 2359296 | tf_op jit(solution)/shard_map/all_to_all | solution.py:19
  154.4 1.3 copy-done.2
  156.9 2.4 %shard_map.61 = bf16[4,256,384]{2,1,0:T(8,128)(2,1)S(1)} custom-call(s32[1]{0:T(128)} %bitcast.place, f32[256,384]{1,0:T(8,128)S(1)} %copy-done.1, bf16[2,4,4,48,384]{4,3,2,1,0:T(8,128)(2,1)S(1)} %copy-done.2, bf16[4,384,384]{2,1,0:T(8,128)(2,1)S(1)} %bitcast.14, bf16[1536,384]{1,0:T(8,128)(2,1)S(1)} %get-tuple-element.18.map_in), custom_call_target="tpu_custom_call" | custom-call | tf_op jit(solution)/shard_map/pallas_call | solution.py:181
  159.4 15.3 %all_to_all.63.shares = bf16[4,256,384]{2,1,0:T(8,128)(2,1)S(1)} all-to-all(bf16[4,256,384]{2,1,0:T(8,128)(2,1)S(1)} %shard_map.61), channel_id=1, replica_groups=mesh['y'=4,'zh'=4,'zl'=4,'core'=2,'x'=4] {'x'}, dimensions={0} | all-to-all | bytes 1572864 | tf_op jit(solution)/shard_map/all_to_all | solution.py:19
  174.8 2.5 %psum.28 = f32[8,128]{1,0:T(8,128)S(1)} all-reduce(f32[8,128]{1,0:T(8,128)S(1)} %get-tuple-element.20), channel_id=1, replica_groups=mesh['y'=4,'zh'=4,'zl'=4,'core'=2,'x'=4] {'core'}, use_global_device_ids=true, to_apply=%region_4.5 | all-reduce | flops 1024 | bytes 8192 | tf_op jit(solution)/shard_map/psum | solution.py:205
  177.3 9.2 %psum.29 = f32[8,128]{1,0:T(8,128)S(1)} all-reduce(f32[8,128]{1,0:T(8,128)S(1)} %psum.28), channel_id=1, replica_groups=mesh['y'=4,'zh'=4,'zl'=4,'core'=2,'x'=4] {'x'}, use_global_device_ids=true, to_apply=%region_5.6 | all-reduce | flops 1024 | bytes 8192 | tf_op jit(solution)/shard_map/psum | solution.py:205
  186.5 8.9 %psum.30 = f32[8,128]{1,0:T(8,128)S(1)} all-reduce(f32[8,128]{1,0:T(8,128)S(1)} %psum.29), channel_id=1, replica_groups=mesh['y'=4,'zh'=4,'zl'=4,'core'=2,'x'=4] {'y'}, use_global_device_ids=true, to_apply=%region_6.7 | all-reduce | flops 1024 | bytes 8192 | tf_op jit(solution)/shard_map/psum | solution.py:205
  195.4 9.2 %psum.31 = f32[8,128]{1,0:T(8,128)S(1)} all-reduce(f32[8,128]{1,0:T(8,128)S(1)} %psum.30), channel_id=1, replica_groups=mesh['y'=4,'zh'=4,'zl'=4,'core'=2,'x'=4] {'zl'}, use_global_device_ids=true, to_apply=%region_7.8 | all-reduce | flops 1024 | bytes 8192 | tf_op jit(solution)/shard_map/psum | solution.py:205
  204.6 14.9 %all_to_all.64.sums = f32[4,8,128]{2,1,0:T(8,128)S(1)} all-to-all(f32[4,8,128]{2,1,0:T(8,128)S(1)} %broadcast_in_dim.63), channel_id=1, replica_groups=mesh['y'=4,'zh'=4,'zl'=4,'core'=2,'x'=4] {'zh'}, dimensions={0} | all-to-all | bytes 32768 | tf_op jit(solution)/shard_map/all_to_all | solution.py:19
  (50 shorter events, 13.0 us)
Async XLA Ops:
  7.2 17.2 %copy-start = (bf16[1536,384]{1,0:T(8,128)(2,1)S(1)}, bf16[1536,384]{1,0:T(8,128)(2,1)}, u32[]{:S(2)}) copy-start(bf16[1536,384]{1,0:T(8,128)(2,1)} %param.5) | copy-start | bytes 3538948
  7.2 60.3 %all-gather.4.cloned.1.call-start = ((), (), s32[]{:S(2)}) async-start(), calls=%async_computation.11 | async-start | bytes 2949120 | tf_op jit(solution)/shard_map/all_gather | solution.py:138
  7.2 18.0 %copy-start.1 = (f32[256,384]{1,0:T(8,128)S(1)}, f32[256,384]{1,0:T(8,128)}, u32[]{:S(2)}) copy-start(f32[256,384]{1,0:T(8,128)} %vec.5) | copy-start | bytes 1179652
  67.5 1.7 copy-start.3
  69.1 1.3 copy-start.7
  71.8 0.6 copy-start.10
  72.4 15.6 %copy-start.4 = (bf16[768,384]{1,0:T(8,128)(2,1)}, bf16[768,384]{1,0:T(8,128)(2,1)S(1)}, u32[]{:S(2)}) copy-start(bf16[768,384]{1,0:T(8,128)(2,1)S(1)} %shard_map.59.mine) | copy-start | bytes 1769476
  72.4 15.6 %collective-permute-start = (bf16[768,384]{1,0:T(8,128)(2,1)S(1)}, bf16[768,384]{1,0:T(8,128)(2,1)S(1)}, u32[]{:S(2)}, u32[]{:S(2)}) collective-permute-start(bf16[768,384]{1,0:T(8,128)(2,1)S(1)} %shard_map.59.mine), channel_id=1, source_target_pairs={{0,4},{4,0},{1,5},{5,1},{2,6},{6,2},{3,7},{7,3},{8,12},{12,8},{9,1... | collective-permute-start | bytes 1769480 | tf_op jit(solution)/shard_map/ppermute | solution.py:158
  75.8 28.5 %all-to-all-start.3 = ((bf16[4,12,1536]{2,1,0:T(8,128)(2,1)}), bf16[4,12,1536]{2,1,0:T(8,128)(2,1)}, u32[]{:S(2)}, u32[]{:S(2)}) async-start(bf16[4,12,1536]{2,1,0:T(8,128)(2,1)} %broadcast_in_dim.57), calls=%async_computation.3 | async-start | bytes 393216 | tf_op jit(solution)/shard_map/all_to_all | solution.py:19
  88.0 66.4 %all-gather.6.cloned.1.call-start = ((), (), s32[]{:S(2)}) async-start(), calls=%async_computation.12 | async-start | bytes 1474560 | tf_op jit(solution)/shard_map/all_gather | solution.py:172
  88.0 0.8 copy-start.8
  88.8 1.1 copy-start.5
  89.9 1.1 copy-start.9
  91.6 0.7 copy-start.11
  154.4 1.3 copy-start.2
  155.7 1.3 copy-start.6
Sparse Core Ops, SparseCore 0:
  25.4 42.0 all-gather.3
  92.4 32.5 all-gather.5

commit v7 on v4

--- a/solution.py
+++ b/solution.py
@@ -12,7 +12,8 @@
 ROW = ("y", "zh", "zl", "core")
 VMEM = pl.BlockSpec(memory_space=pltpu.VMEM)
 SMEM = pl.BlockSpec(memory_space=pltpu.SMEM)
-PARAMS = pltpu.CompilerParams(vmem_limit_bytes=48 * 1024 * 1024)
+PARAMS = pltpu.CompilerParams(vmem_limit_bytes=14 * 1024 * 1024)
+LARGE = pltpu.CompilerParams(vmem_limit_bytes=56 * 1024 * 1024)
 
 
 def swap(pieces, axis):
@@ -48,19 +49,54 @@
     return lax.dot_general(a, b, (((1,), (1,)), ((), ())), preferred_element_type=F32)
 
 
-def partial_kernel(place, vec, proj, sym, own_map, out):
+def map_kernel(corner_rows, tri_inv, edge_cols, slice_cols, own_map, proj, gram, acc, low):
+    step = pl.program_id(0)
+    rows = edge_cols.shape[0]
+    own_map[...] = dot(corner_rows[...], tri_inv[...]).astype(BF16)
+
+    @pl.when(step == 0)
+    def _():
+        acc[...] = jnp.zeros_like(acc)
+        low[...] = jnp.zeros_like(low)
+        proj[rows:] = jnp.zeros((proj.shape[0] - rows, proj.shape[1]), BF16)
+
+    acc[...] += dot(edge_cols[...], own_map[...])
+    low[...] += dot(slice_cols[...], own_map[...])
+
+    @pl.when(step == pl.num_programs(0) - 1)
+    def _():
+        proj[:rows] = acc[...].astype(BF16)
+        gram[...] = low[...].astype(BF16)
+
+
+def partial_kernel(
+    place, vec_in, sym_in, proj_in, map_in, out, vec, sym, proj, own_map, sem
+):
     rows, width = vec.shape
-    blocks = sym.shape[0]
+    blocks = proj.shape[0]
+    fetch_proj = pltpu.make_async_copy(proj_in.at[:, :rows], proj, sem.at[0])
+    fetch_sym = pltpu.make_async_copy(sym_in, sym, sem.at[1])
+    fetch_vec = pltpu.make_async_copy(vec_in, vec, sem.at[2])
+    fetch_map = pltpu.make_async_copy(map_in, own_map, sem.at[3])
+    for fetch in (fetch_proj, fetch_sym, fetch_vec, fetch_map):
+        fetch.start()
     first = lax.broadcasted_iota(jnp.int32, (width, width), 0)
     second = lax.broadcasted_iota(jnp.int32, (width, width), 1)
     zero = jnp.zeros((width, width), BF16)
     acc = jnp.zeros((rows, width), F32)
+    fetch_proj.wait()
+    fetch_sym.wait()
     for k in range(blocks):
         shift = (place[0] - k) * width
-        part = proj[k, :rows]
-        acc += dot(part, jnp.where(first <= second + shift, sym[k], zero))
-        acc += dot_turned(part, jnp.where(first < second - shift, sym[k], zero))
+        block = jnp.concatenate(
+            [sym[c, y, k] for c in range(sym.shape[0]) for y in range(sym.shape[1])]
+        )
+        part = proj[k]
+        acc += dot(part, jnp.where(first <= second + shift, block, zero))
+        acc += dot_turned(part, jnp.where(first < second - shift, block, zero))
+    fetch_vec.wait()
     corrected = (vec[...] - acc).astype(BF16)
+    fetch_map.wait()
     for k in range(blocks):
         share = dot_turned(corrected, own_map[k * width : (k + 1) * width])
         out[k] = share.astype(BF16)
@@ -81,7 +117,8 @@
 
 
 def finish_kernel(count, sums, vec, dedge, out, coeffs):
-    vv, vd, dd = (jnp.sum(sums[i : i + 1], axis=1, keepdims=True) for i in range(3))
+    lines = sum(sums[i] for i in range(sums.shape[0]))
+    vv, vd, dd = (jnp.sum(lines[i : i + 1], axis=1, keepdims=True) for i in range(3))
     along = (vv - vd) / count
     keep = 1.0 - along
     square = (keep * keep * vv - 2.0 * keep * vd + dd) / count
@@ -102,9 +139,8 @@
 
     before = lax.broadcasted_iota(jnp.int32, (blocks, 1, 1), 0) < place
     edge, here, before = lax.optimization_barrier((edge, here, before))
+    corner_wide = lax.all_gather(corner, "x", axis=1, tiled=True)
     edge_wide = lax.all_gather(edge, "x", axis=1, tiled=True)
-    edge_wide, corner = lax.optimization_barrier((edge_wide, corner))
-    corner_wide = lax.all_gather(corner, "x", axis=1, tiled=True)
     vec_low = vector.astype(BF16)
     cross = lax.dot_general(
         vec_low, edge_wide, (((0,), (0,)), ((), ())), preferred_element_type=F32
@@ -112,29 +148,61 @@
     cross = cross * (1.0 / rows_total)
     for axis in ("core", "y", "zl"):
         cross = scatter_sum(cross.astype(BF16), axis)
-    cross = total(spread(cross.astype(BF16), "zh"))
-    cross_all = spread(cross.astype(BF16), "x").reshape(-1, bond)
-
-    other = dot(dot(cross_all, corner_wide).astype(BF16), tri_inv).astype(BF16)
+    cross = total(spread(cross.astype(BF16), "zh")).astype(BF16)
+    cross_all = spread(cross, "x").reshape(-1, bond)
+
+    step = bond // 6
+    own_map, proj, other = pl.pallas_call(
+        map_kernel,
+        grid=(bond // step,),
+        out_shape=(
+            jax.ShapeDtypeStruct((bond, width), BF16),
+            jax.ShapeDtypeStruct((width, width), BF16),
+            jax.ShapeDtypeStruct((cross_all.shape[0], width), BF16),
+        ),
+        in_specs=[
+            pl.BlockSpec((step, bond), lambda i: (i, 0)),
+            pl.BlockSpec((bond, width), lambda i: (0, 0)),
+            pl.BlockSpec((rows, step), lambda i: (0, i)),
+            pl.BlockSpec((cross_all.shape[0], step), lambda i: (0, i)),
+        ],
+        out_specs=(
+            pl.BlockSpec((step, width), lambda i: (i, 0)),
+            pl.BlockSpec((width, width), lambda i: (0, 0)),
+            pl.BlockSpec((cross_all.shape[0], width), lambda i: (0, 0)),
+        ),
+        scratch_shapes=[
+            pltpu.VMEM((rows, width), F32),
+            pltpu.VMEM((cross_all.shape[0], width), F32),
+        ],
+        compiler_params=LARGE,
+        cost_estimate=pl.CostEstimate(
+            flops=2 * (bond + rows) * bond * width,
+            bytes_accessed=2 * bond * (bond + 2 * width),
+            transcendentals=0,
+        ),
+    )(corner_wide, tri_inv, edge_wide, cross_all)
+    proj_blocks = lax.all_gather(proj, "x", axis=0)
+
     other = other.reshape(blocks, -1, width)
     own = swap(other, "x")
-
-    own_map = dot(corner_wide, tri_inv).astype(BF16)
-    proj = dot(edge_wide, own_map).astype(BF16)
-    proj = jnp.concatenate([proj, own_map[: width - rows]])
-    proj_blocks = lax.all_gather(proj, "x", axis=0)
-
-    chosen = jnp.where(before, other, own)
-    for axis in ("zl", "y", "core"):
-        chosen = join_rows(chosen, axis)
+    chosen = join_rows(jnp.where(before, other, own), "zl")
+    chosen = spread(spread(chosen, "y"), "core")
 
     shares = pl.pallas_call(
         partial_kernel,
         out_shape=jax.ShapeDtypeStruct((blocks, rows, width), BF16),
-        in_specs=[SMEM] + [VMEM] * 4,
+        in_specs=[SMEM] + [pl.BlockSpec(memory_space=pl.ANY)] * 4,
         out_specs=VMEM,
-        compiler_params=PARAMS,
-    )(here, vector, proj_blocks, chosen, own_map)
+        scratch_shapes=[
+            pltpu.VMEM((rows, width), F32),
+            pltpu.VMEM(chosen.shape, BF16),
+            pltpu.VMEM((blocks, rows, width), BF16),
+            pltpu.VMEM((bond, width), BF16),
+            pltpu.SemaphoreType.DMA((4,)),
+        ],
+        compiler_params=LARGE,
+    )(here, vector, chosen, proj_blocks, own_map)
     shares = swap(shares, "x")
     dedge, sums = pl.pallas_call(
         edge_kernel,
@@ -146,8 +214,9 @@
         out_specs=(VMEM, VMEM),
         compiler_params=PARAMS,
     )(vector, shares)
-    for axis in ("core", "x", "y", "zl", "zh"):
+    for axis in ("core", "x", "y", "zl"):
         sums = lax.psum(sums, axis)
+    sums = spread(sums, "zh")
     return pl.pallas_call(
         functools.partial(finish_kernel, float(rows_total * bond)),
         out_shape=(

time: 217 us -> 213 us (0.982)
  blocking collectives: 154 us -> 180 us
  waiting for transfers between devices: 16.8 us -> 0.7 us
  starting transfers between devices: 12.4 us -> 0.08 us
  Pallas kernels: 3.14 us -> 14.2 us
  matrix products: 9.48 us -> 0.51 us
    all_to_all x9 -> x11, blocking collectives: 91.3 us -> 133 us  [swap(): return lax.all_to_all(pieces, axis, split_axis=0, concat_axis=0, tiled=True)]
    all_gather x1, waiting for transfers between devices: 16.7 us -> 0.01 us  [on_device(): corner_wide = lax.all_gather(corner, 'x', axis=1, tiled=True)]
    psum x5 -> x4, blocking collectives: 45.9 us -> 29.7 us  [on_device(): sums = lax.psum(sums, axis)]
    all_to_all x1 -> x0, starting transfers between devices: 12.4 us -> none  [swap(): return lax.all_to_all(pieces, axis, split_axis=0, concat_axis=0, tiled=True)]
    dot_general x3 -> x0, matrix products: 8.97 us -> none  [dot(): return jnp.dot(a, b, preferred_element_type=F32)]
    pallas_call x0 -> x1, Pallas kernels: none -> 8.47 us  [on_device(): pl.pallas_call(map_kernel, grid=(bond // step,), out_shape=(jax.ShapeDtyp...]
    pallas_call x1, Pallas kernels: 2.03 us -> 4.61 us  [on_device(): pl.pallas_call(partial_kernel, out_shape=jax.ShapeDtypeStruct((blocks, ro...]
    unnamed x10 -> x8, local copies, waits for them, and re-layouts: 2.97 us -> 0.51 us
  transfers between devices with their start and end apart: 3 -> 2, of which waited for: 1 -> 0; matrix products, arithmetic and copies ran while one was open for 6% -> 1% of each run, Pallas kernels for 0% -> 0%
where the time goes in v7:
time: 213 us; the launch traced here: 212 us
  blocking collectives  180 us (85%)
  Pallas kernels  14.2 us (7%)
  between operations  14.2 us (7%)
  local copies, waits for them, and re-layouts  2.3 us (1%)
    all_to_all x11, blocking collectives, swap(): return lax.all_to_all(pieces, axis, split_axis=0, concat_axis=0, tiled=True)  133 us
    psum x4, blocking collectives, on_device(): sums = lax.psum(sums, axis)  29.7 us
    all_gather x1, blocking collectives, on_device(): edge_wide = lax.all_gather(edge, 'x', axis=1, tiled=True)  16.7 us
    pallas_call x1, Pallas kernels, on_device(): pl.pallas_call(map_kernel, grid=(bond // step,), out_shape=(jax.ShapeDtyp...  8.47 us
    pallas_call x1, Pallas kernels, on_device(): pl.pallas_call(partial_kernel, out_shape=jax.ShapeDtypeStruct((blocks, ro...  4.61 us
  transfers between devices with their start and end apart: 2, of which 0 were waited for; matrix products, arithmetic and copies ran while one was open for 1% of the time, Pallas kernels for 0%

profile of v7, /device:TPU:2, one launch (start us, length us, event | category | flops | bytes accessed | tf_op | source)
XLA Modules:
  0.0 212.2 jit_solution(2207665250902752691)
XLA Ops:
  7.2 0.7 all-gather.4.cloned.1.call-update
  8.1 16.7 %all_gather.13.edge_cols = bf16[256,1536]{1,0:T(8,128)(2,1)S(1)} all-gather(bf16[256,384]{1,0:T(8,128)(2,1)S(1)} %copy-done.3), channel_id=1, replica_groups=mesh['y'=4,'zh'=4,'zl'=4,'core'=2,'x'=4] {'x'}, dimensions={1}, use_global_device_ids=true | all-gather | bytes 983040 | tf_op jit(solution)/shard_map/all_gather | solution.py:143
  24.8 0.5 fusion
  25.3 0.4 copy-done.2
  25.7 4.7 %all_to_all.55 = bf16[2,192,1536]{2,1,0:T(8,128)(2,1)S(1)} all-to-all(bf16[2,192,1536]{2,1,0:T(8,128)(2,1)S(1)} %bitcast.11), channel_id=1, replica_groups=mesh['y'=4,'zh'=4,'zl'=4,'core'=2,'x'=4] {'core'}, dimensions={0} | all-to-all | bytes 2359296 | tf_op jit(solution)/shard_map/all_to_all | solution.py:20
  30.6 13.1 %all_to_all.56 = bf16[4,48,1536]{2,1,0:T(8,128)(2,1)S(1)} all-to-all(bf16[4,48,1536]{2,1,0:T(8,128)(2,1)S(1)} %bitcast.12), channel_id=1, replica_groups=mesh['y'=4,'zh'=4,'zl'=4,'core'=2,'x'=4] {'y'}, dimensions={0} | all-to-all | bytes 1179648 | tf_op jit(solution)/shard_map/all_to_all | solution.py:20
  43.9 12.4 %all_to_all.57 = bf16[4,12,1536]{2,1,0:T(8,128)(2,1)S(1)} all-to-all(bf16[4,12,1536]{2,1,0:T(8,128)(2,1)S(1)} %reshape.35), channel_id=1, replica_groups=mesh['y'=4,'zh'=4,'zl'=4,'core'=2,'x'=4] {'zl'}, dimensions={0} | all-to-all | bytes 294912 | tf_op jit(solution)/shard_map/all_to_all | solution.py:20
  56.4 27.9 %all_to_all.58 = bf16[4,12,1536]{2,1,0:T(8,128)(2,1)S(1)} all-to-all(bf16[4,12,1536]{2,1,0:T(8,128)(2,1)S(1)} %broadcast_in_dim.29), channel_id=1, replica_groups=mesh['y'=4,'zh'=4,'zl'=4,'core'=2,'x'=4] {'zh'}, dimensions={0} | all-to-all | bytes 294912 | tf_op jit(solution)/shard_map/all_to_all | solution.py:20
  84.4 9.1 %all_to_all.59 = bf16[4,12,1536]{2,1,0:T(8,128)(2,1)S(1)} all-to-all(bf16[4,12,1536]{2,1,0:T(8,128)(2,1)S(1)} %broadcast_in_dim.54), channel_id=1, replica_groups=mesh['y'=4,'zh'=4,'zl'=4,'core'=2,'x'=4] {'x'}, dimensions={0} | all-to-all | bytes 294912 | tf_op jit(solution)/shard_map/all_to_all | solution.py:20
  93.5 0.7 reshape.36.slice_cols
  94.2 8.5 %shard_map.59 = (bf16[1536,384]{1,0:T(8,128)(2,1)}, bf16[384,384]{1,0:T(8,128)(2,1)}, bf16[48,384]{1,0:T(8,128)(2,1)}) custom-call(bf16[1536,1536]{1,0:T(8,128)(2,1)} %all-gather.4.cloned.1.call-done.corner_rows, bf16[1536,384]{1,0:T(8,128)(2,1)} %tri_inv.1, bf16[256,1536]{1,0:T(8,128)(2,1)} %copy-done.2, bf16[48,1536]{1,0:T(8,128)(2,1)} %reshape.36.slice_cols), custom_call_target="tpu_custom_call" | custom-call | flops 2113929216 | bytes 7077888 | tf_op jit(solution)/shard_map/pallas_call | solution.py:155
  102.7 0.8 reshape.37
  103.5 7.9 %all_to_all.60 = bf16[4,12,384]{2,1,0:T(8,128)(2,1)S(1)} all-to-all(bf16[4,12,384]{2,1,0:T(8,128)(2,1)S(1)} %reshape.37), channel_id=1, replica_groups=mesh['y'=4,'zh'=4,'zl'=4,'core'=2,'x'=4] {'x'}, dimensions={0} | all-to-all | bytes 73728 | tf_op jit(solution)/shard_map/all_to_all | solution.py:20
  111.5 10.2 %all_to_all.61 = bf16[4,4,12,384]{3,1,2,0:T(4,128)(2,1)S(1)} all-to-all(bf16[4,4,12,384]{3,1,2,0:T(4,128)(2,1)S(1)} %broadcast_in_dim.55), channel_id=1, replica_groups=mesh['y'=4,'zh'=4,'zl'=4,'core'=2,'x'=4] {'zl'}, dimensions={0} | all-to-all | bytes 294912 | tf_op jit(solution)/shard_map/all_to_all | solution.py:20
  121.8 10.8 %all_to_all.62 = bf16[4,4,48,384]{3,2,1,0:T(8,128)(2,1)S(1)} all-to-all(bf16[4,4,48,384]{3,2,1,0:T(8,128)(2,1)S(1)} %broadcast_in_dim.57), channel_id=1, replica_groups=mesh['y'=4,'zh'=4,'zl'=4,'core'=2,'x'=4] {'y'}, dimensions={0} | all-to-all | bytes 1179648 | tf_op jit(solution)/shard_map/all_to_all | solution.py:20
  132.8 5.5 %all_to_all.63.sym_in = bf16[2,4,4,48,384]{4,3,2,1,0:T(8,128)(2,1)} all-to-all(bf16[2,4,4,48,384]{4,3,2,1,0:T(8,128)(2,1)S(1)} %broadcast_in_dim.58), channel_id=1, replica_groups=mesh['y'=4,'zh'=4,'zl'=4,'core'=2,'x'=4] {'core'}, dimensions={0} | all-to-all | bytes 2359296 | tf_op jit(solution)/shard_map/all_to_all | solution.py:20
  138.3 4.6 %shard_map.60 = bf16[4,256,384]{2,1,0:T(8,128)(2,1)} custom-call(s32[1]{0:T(128)} %bitcast.place, f32[256,384]{1,0:T(8,128)} %vec.3, bf16[2,4,4,48,384]{4,3,2,1,0:T(8,128)(2,1)} %all_to_all.63.sym_in, bf16[4,384,384]{2,1,0:T(8,128)(2,1)} %bitcast.13, bf16[1536,384]{1,0:T(8,128)(2,1)} %get-tuple-element.15.map_in), custom_call_target="tpu_custom_call" | custom-call | tf_op jit(solution)/shard_map/pallas_call | solution.py:192
  142.9 16.5 %all_to_all.64.shares = bf16[4,256,384]{2,1,0:T(8,128)(2,1)S(1)} all-to-all(bf16[4,256,384]{2,1,0:T(8,128)(2,1)} %shard_map.60), channel_id=1, replica_groups=mesh['y'=4,'zh'=4,'zl'=4,'core'=2,'x'=4] {'x'}, dimensions={0} | all-to-all | bytes 1572864 | tf_op jit(solution)/shard_map/all_to_all | solution.py:20
  159.6 2.5 %psum.28 = f32[8,128]{1,0:T(8,128)S(1)} all-reduce(f32[8,128]{1,0:T(8,128)S(1)} %get-tuple-element.16), channel_id=1, replica_groups=mesh['y'=4,'zh'=4,'zl'=4,'core'=2,'x'=4] {'core'}, use_global_device_ids=true, to_apply=%region_4.5 | all-reduce | flops 1024 | bytes 8192 | tf_op jit(solution)/shard_map/psum | solution.py:218
  162.1 9.2 %psum.29 = f32[8,128]{1,0:T(8,128)S(1)} all-reduce(f32[8,128]{1,0:T(8,128)S(1)} %psum.28), channel_id=1, replica_groups=mesh['y'=4,'zh'=4,'zl'=4,'core'=2,'x'=4] {'x'}, use_global_device_ids=true, to_apply=%region_5.6 | all-reduce | flops 1024 | bytes 8192 | tf_op jit(solution)/shard_map/psum | solution.py:218
  171.2 8.9 %psum.30 = f32[8,128]{1,0:T(8,128)S(1)} all-reduce(f32[8,128]{1,0:T(8,128)S(1)} %psum.29), channel_id=1, replica_groups=mesh['y'=4,'zh'=4,'zl'=4,'core'=2,'x'=4] {'y'}, use_global_device_ids=true, to_apply=%region_6.7 | all-reduce | flops 1024 | bytes 8192 | tf_op jit(solution)/shard_map/psum | solution.py:218
  180.1 9.2 %psum.31 = f32[8,128]{1,0:T(8,128)S(1)} all-reduce(f32[8,128]{1,0:T(8,128)S(1)} %psum.30), channel_id=1, replica_groups=mesh['y'=4,'zh'=4,'zl'=4,'core'=2,'x'=4] {'zl'}, use_global_device_ids=true, to_apply=%region_7.8 | all-reduce | flops 1024 | bytes 8192 | tf_op jit(solution)/shard_map/psum | solution.py:218
  189.3 15.1 %all_to_all.65.sums = f32[4,8,128]{2,1,0:T(8,128)S(1)} all-to-all(f32[4,8,128]{2,1,0:T(8,128)S(1)} %broadcast_in_dim.59), channel_id=1, replica_groups=mesh['y'=4,'zh'=4,'zl'=4,'core'=2,'x'=4] {'zh'}, dimensions={0} | all-to-all | bytes 32768 | tf_op jit(solution)/shard_map/all_to_all | solution.py:20
  204.4 0.9 shard_map.62
  (28 shorter events, 1.2 us)
Async XLA Ops:
  7.2 0.9 copy-start.3
  7.2 17.6 %copy-start = (f32[256,384]{1,0:T(8,128)S(1)}, f32[256,384]{1,0:T(8,128)}, u32[]{:S(2)}) copy-start(f32[256,384]{1,0:T(8,128)} %vec.3) | copy-start | bytes 1179652
  7.2 87.0 %all-gather.4.cloned.1.call-start = ((), (), s32[]{:S(2)}) async-start(), calls=%async_computation.11 | async-start | bytes 5898240 | tf_op jit(solution)/shard_map/all_gather | solution.py:142
  7.9 130.4 %all-gather.6.cloned.1.call-start = ((), (), s32[]{:S(2)}) async-start(), calls=%async_computation.12 | async-start | bytes 1474560 | tf_op jit(solution)/shard_map/all_gather | solution.py:185
  24.8 0.9 copy-start.2
  142.9 16.5 %copy-start.1 = (f32[256,384]{1,0:T(8,128)S(1)}, f32[256,384]{1,0:T(8,128)}, u32[]{:S(2)}) copy-start(f32[256,384]{1,0:T(8,128)} %vec.3) | copy-start | bytes 1179652
Sparse Core Ops, SparseCore 0:
  10.1 64.1 all-gather.3
  102.8 21.4 all-gather.5

commit v8 on v4

--- a/solution.py
+++ b/solution.py
@@ -12,7 +12,7 @@
 ROW = ("y", "zh", "zl", "core")
 VMEM = pl.BlockSpec(memory_space=pltpu.VMEM)
 SMEM = pl.BlockSpec(memory_space=pltpu.SMEM)
-PARAMS = pltpu.CompilerParams(vmem_limit_bytes=48 * 1024 * 1024)
+PARAMS = pltpu.CompilerParams(vmem_limit_bytes=10 * 1024 * 1024)
 
 
 def swap(pieces, axis):
@@ -48,18 +48,36 @@
     return lax.dot_general(a, b, (((1,), (1,)), ((), ())), preferred_element_type=F32)
 
 
-def partial_kernel(place, vec, proj, sym, own_map, out):
+def map_kernel(corner, tri_inv, edge, slices, own_map, proj, gram):
+    bond = corner.shape[0]
+    rows = edge.shape[0]
+    step = bond // 6
+
+    @pl.loop(0, bond, step=step)
+    def _(i):
+        part = pl.ds(pl.multiple_of(i, step), step)
+        own_map[part] = dot(corner[part], tri_inv[...]).astype(BF16)
+
+    proj[:rows] = dot(edge[...], own_map[...]).astype(BF16)
+    proj[rows:] = jnp.zeros((proj.shape[0] - rows, proj.shape[1]), BF16)
+    gram[...] = dot(slices[...], own_map[...]).astype(BF16)
+
+
+def partial_kernel(place, vec, sym, proj, own_map, out):
     rows, width = vec.shape
-    blocks = sym.shape[0]
+    blocks = proj.shape[0]
     first = lax.broadcasted_iota(jnp.int32, (width, width), 0)
     second = lax.broadcasted_iota(jnp.int32, (width, width), 1)
     zero = jnp.zeros((width, width), BF16)
     acc = jnp.zeros((rows, width), F32)
     for k in range(blocks):
         shift = (place[0] - k) * width
+        block = jnp.concatenate(
+            [sym[c, y, k] for c in range(sym.shape[0]) for y in range(sym.shape[1])]
+        )
         part = proj[k, :rows]
-        acc += dot(part, jnp.where(first <= second + shift, sym[k], zero))
-        acc += dot_turned(part, jnp.where(first < second - shift, sym[k], zero))
+        acc += dot(part, jnp.where(first <= second + shift, block, zero))
+        acc += dot_turned(part, jnp.where(first < second - shift, block, zero))
     corrected = (vec[...] - acc).astype(BF16)
     for k in range(blocks):
         share = dot_turned(corrected, own_map[k * width : (k + 1) * width])
@@ -81,7 +99,8 @@
 
 
 def finish_kernel(count, sums, vec, dedge, out, coeffs):
-    vv, vd, dd = (jnp.sum(sums[i : i + 1], axis=1, keepdims=True) for i in range(3))
+    lines = sum(sums[i] for i in range(sums.shape[0]))
+    vv, vd, dd = (jnp.sum(lines[i : i + 1], axis=1, keepdims=True) for i in range(3))
     along = (vv - vd) / count
     keep = 1.0 - along
     square = (keep * keep * vv - 2.0 * keep * vd + dd) / count
@@ -102,9 +121,8 @@
 
     before = lax.broadcasted_iota(jnp.int32, (blocks, 1, 1), 0) < place
     edge, here, before = lax.optimization_barrier((edge, here, before))
+    corner_wide = lax.all_gather(corner, "x", axis=1, tiled=True)
     edge_wide = lax.all_gather(edge, "x", axis=1, tiled=True)
-    edge_wide, corner = lax.optimization_barrier((edge_wide, corner))
-    corner_wide = lax.all_gather(corner, "x", axis=1, tiled=True)
     vec_low = vector.astype(BF16)
     cross = lax.dot_general(
         vec_low, edge_wide, (((0,), (0,)), ((), ())), preferred_element_type=F32
@@ -112,21 +130,34 @@
     cross = cross * (1.0 / rows_total)
     for axis in ("core", "y", "zl"):
         cross = scatter_sum(cross.astype(BF16), axis)
-    cross = total(spread(cross.astype(BF16), "zh"))
-    cross_all = spread(cross.astype(BF16), "x").reshape(-1, bond)
-
-    other = dot(dot(cross_all, corner_wide).astype(BF16), tri_inv).astype(BF16)
+    cross = total(spread(cross.astype(BF16), "zh")).astype(BF16)
+    cross, corner_wide = lax.optimization_barrier((cross, corner_wide))
+    cross_all = spread(cross, "x").reshape(-1, bond)
+
+    own_map, proj, other = pl.pallas_call(
+        map_kernel,
+        out_shape=(
+            jax.ShapeDtypeStruct((bond, width), BF16),
+            jax.ShapeDtypeStruct((width, width), BF16),
+            jax.ShapeDtypeStruct((cross_all.shape[0], width), BF16),
+        ),
+        in_specs=[VMEM] * 4,
+        out_specs=(VMEM,) * 3,
+        compiler_params=PARAMS,
+        cost_estimate=pl.CostEstimate(
+            flops=2 * (bond + rows) * bond * width,
+            bytes_accessed=2 * bond * (bond + 2 * width),
+            transcendentals=0,
+        ),
+    )(corner_wide, tri_inv, edge_wide, cross_all)
+    proj_blocks = lax.all_gather(proj, "x", axis=0)
+
     other = other.reshape(blocks, -1, width)
     own = swap(other, "x")
-
-    own_map = dot(corner_wide, tri_inv).astype(BF16)
-    proj = dot(edge_wide, own_map).astype(BF16)
-    proj = jnp.concatenate([proj, own_map[: width - rows]])
-    proj_blocks = lax.all_gather(proj, "x", axis=0)
-
-    chosen = jnp.where(before, other, own)
-    for axis in ("zl", "y", "core"):
-        chosen = join_rows(chosen, axis)
+    chosen = join_rows(jnp.where(before, other, own), "zl")
+    chosen = spread(chosen, "y")
+    chosen, proj_blocks = lax.optimization_barrier((chosen, proj_blocks))
+    chosen = spread(chosen, "core")
 
     shares = pl.pallas_call(
         partial_kernel,
@@ -134,7 +165,7 @@
         in_specs=[SMEM] + [VMEM] * 4,
         out_specs=VMEM,
         compiler_params=PARAMS,
-    )(here, vector, proj_blocks, chosen, own_map)
+    )(here, vector, chosen, proj_blocks, own_map)
     shares = swap(shares, "x")
     dedge, sums = pl.pallas_call(
         edge_kernel,
@@ -146,8 +177,9 @@
         out_specs=(VMEM, VMEM),
         compiler_params=PARAMS,
     )(vector, shares)
-    for axis in ("core", "x", "y", "zl", "zh"):
+    for axis in ("core", "x", "y", "zl"):
         sums = lax.psum(sums, axis)
+    sums = spread(sums, "zh")
     return pl.pallas_call(
         functools.partial(finish_kernel, float(rows_total * bond)),
         out_shape=(

time: 217 us -> 211 us (0.972)
  blocking collectives: 154 us -> 182 us
  waiting for transfers between devices: 16.8 us -> 0.72 us
  starting transfers between devices: 12.4 us -> 0.08 us
  matrix products: 9.48 us -> 0.51 us
  Pallas kernels: 3.14 us -> 7.93 us
    all_to_all x9 -> x11, blocking collectives: 91.3 us -> 136 us  [swap(): return lax.all_to_all(pieces, axis, split_axis=0, concat_axis=0, tiled=True)]
    all_gather x1, waiting for transfers between devices: 16.7 us -> 0.02 us  [on_device(): corner_wide = lax.all_gather(corner, 'x', axis=1, tiled=True)]
    psum x5 -> x4, blocking collectives: 45.9 us -> 29.7 us  [on_device(): sums = lax.psum(sums, axis)]
    all_to_all x1 -> x0, starting transfers between devices: 12.4 us -> none  [swap(): return lax.all_to_all(pieces, axis, split_axis=0, concat_axis=0, tiled=True)]
    dot_general x3 -> x0, matrix products: 8.97 us -> none  [dot(): return jnp.dot(a, b, preferred_element_type=F32)]
    pallas_call x0 -> x1, Pallas kernels: none -> 4.77 us  [on_device(): pl.pallas_call(map_kernel, out_shape=(jax.ShapeDtypeStruct((bond, width),...]
  transfers between devices with their start and end apart: 3 -> 2, of which waited for: 1 -> 0; matrix products, arithmetic and copies ran while one was open for 6% -> 1% of each run, Pallas kernels for 0% -> 0%
where the time goes in v8:
time: 211 us
  blocking collectives  182 us (86%)
  between operations  14.2 us (7%)
  Pallas kernels  7.93 us (4%)
  local copies, waits for them, and re-layouts  4.08 us (2%)
    all_to_all x11, blocking collectives, swap(): return lax.all_to_all(pieces, axis, split_axis=0, concat_axis=0, tiled=True)  136 us
    psum x4, blocking collectives, on_device(): sums = lax.psum(sums, axis)  29.7 us
    all_gather x1, blocking collectives, on_device(): edge_wide = lax.all_gather(edge, 'x', axis=1, tiled=True)  16.7 us
    pallas_call x1, Pallas kernels, on_device(): pl.pallas_call(map_kernel, out_shape=(jax.ShapeDtypeStruct((bond, width),...  4.77 us
  transfers between devices with their start and end apart: 2, of which 0 were waited for; matrix products, arithmetic and copies ran while one was open for 1% of the time, Pallas kernels for 0%

profile of v8, /device:TPU:2, one launch (start us, length us, event | category | flops | bytes accessed | tf_op | source)
XLA Modules:
  0.0 210.5 jit_solution(13180116711176758328)
XLA Ops:
  7.2 0.7 all-gather.4.cloned.1.call-update
  8.1 16.7 %all_gather.12.edge = bf16[256,1536]{1,0:T(8,128)(2,1)S(1)} all-gather(bf16[256,384]{1,0:T(8,128)(2,1)S(1)} %copy-done.4), channel_id=1, replica_groups=mesh['y'=4,'zh'=4,'zl'=4,'core'=2,'x'=4] {'x'}, dimensions={1}, use_global_device_ids=true | all-gather | bytes 983040 | tf_op jit(solution)/shard_map/all_gather | solution.py:125
  24.8 0.5 fusion
  25.3 4.7 %all_to_all.55 = bf16[2,192,1536]{2,1,0:T(8,128)(2,1)S(1)} all-to-all(bf16[2,192,1536]{2,1,0:T(8,128)(2,1)S(1)} %bitcast.12), channel_id=1, replica_groups=mesh['y'=4,'zh'=4,'zl'=4,'core'=2,'x'=4] {'core'}, dimensions={0} | all-to-all | bytes 2359296 | tf_op jit(solution)/shard_map/all_to_all | solution.py:19
  30.0 0.2 reduce_sum.48
  30.3 13.1 %all_to_all.56 = bf16[4,48,1536]{2,1,0:T(8,128)(2,1)S(1)} all-to-all(bf16[4,48,1536]{2,1,0:T(8,128)(2,1)S(1)} %bitcast.13), channel_id=1, replica_groups=mesh['y'=4,'zh'=4,'zl'=4,'core'=2,'x'=4] {'y'}, dimensions={0} | all-to-all | bytes 1179648 | tf_op jit(solution)/shard_map/all_to_all | solution.py:19
  43.5 12.4 %all_to_all.57 = bf16[4,12,1536]{2,1,0:T(8,128)(2,1)S(1)} all-to-all(bf16[4,12,1536]{2,1,0:T(8,128)(2,1)S(1)} %reshape.35), channel_id=1, replica_groups=mesh['y'=4,'zh'=4,'zl'=4,'core'=2,'x'=4] {'zl'}, dimensions={0} | all-to-all | bytes 294912 | tf_op jit(solution)/shard_map/all_to_all | solution.py:19
  56.0 27.9 %all_to_all.58 = bf16[4,12,1536]{2,1,0:T(8,128)(2,1)S(1)} all-to-all(bf16[4,12,1536]{2,1,0:T(8,128)(2,1)S(1)} %broadcast_in_dim.29), channel_id=1, replica_groups=mesh['y'=4,'zh'=4,'zl'=4,'core'=2,'x'=4] {'zh'}, dimensions={0} | all-to-all | bytes 294912 | tf_op jit(solution)/shard_map/all_to_all | solution.py:19
  84.0 9.1 %all_to_all.59 = bf16[4,12,1536]{2,1,0:T(8,128)(2,1)S(1)} all-to-all(bf16[4,12,1536]{2,1,0:T(8,128)(2,1)S(1)} %broadcast_in_dim.54), channel_id=1, replica_groups=mesh['y'=4,'zh'=4,'zl'=4,'core'=2,'x'=4] {'x'}, dimensions={0} | all-to-all | bytes 294912 | tf_op jit(solution)/shard_map/all_to_all | solution.py:19
  93.2 2.3 %copy-done.2 = bf16[1536,1536]{1,0:T(8,128)(2,1)S(1)} copy-done((bf16[1536,1536]{1,0:T(8,128)(2,1)S(1)}, bf16[1536,1536]{1,0:T(8,128)(2,1)}, u32[]{:S(2)}) %copy-start.2) | copy-done | bytes 4718616
  95.5 1.3 copy-done.3
  96.8 4.8 %shard_map.59 = (bf16[1536,384]{1,0:T(8,128)(2,1)S(1)}, bf16[384,384]{1,0:T(8,128)(2,1)}, bf16[48,384]{1,0:T(8,128)(2,1)S(1)}) custom-call(bf16[1536,1536]{1,0:T(8,128)(2,1)S(1)} %copy-done.2, bf16[1536,384]{1,0:T(8,128)(2,1)S(1)} %copy-done.3, bf16[256,1536]{1,0:T(8,128)(2,1)S(1)} %all_gather.12.edge, bf16[48,1536]{1,0:T(8,128)(2,1)S(1)} %reshape.36.slices), custom_call_target="tpu_custom_call" | custom-call | flops 2113929216 | bytes 7077888 | tf_op jit(solution)/shard_map/pallas_call | solution.py:137
  101.6 7.9 %all_to_all.60 = bf16[4,12,384]{2,1,0:T(8,128)(2,1)S(1)} all-to-all(bf16[4,12,384]{2,1,0:T(8,128)(2,1)S(1)} %reshape.37), channel_id=1, replica_groups=mesh['y'=4,'zh'=4,'zl'=4,'core'=2,'x'=4] {'x'}, dimensions={0} | all-to-all | bytes 73728 | tf_op jit(solution)/shard_map/all_to_all | solution.py:19
  109.7 10.2 %all_to_all.61 = bf16[4,4,12,384]{3,1,2,0:T(4,128)(2,1)S(1)} all-to-all(bf16[4,4,12,384]{3,1,2,0:T(4,128)(2,1)S(1)} %broadcast_in_dim.55), channel_id=1, replica_groups=mesh['y'=4,'zh'=4,'zl'=4,'core'=2,'x'=4] {'zl'}, dimensions={0} | all-to-all | bytes 294912 | tf_op jit(solution)/shard_map/all_to_all | solution.py:19
  120.0 10.8 %all_to_all.62 = bf16[4,4,48,384]{3,2,1,0:T(8,128)(2,1)S(1)} all-to-all(bf16[4,4,48,384]{3,2,1,0:T(8,128)(2,1)S(1)} %broadcast_in_dim.57), channel_id=1, replica_groups=mesh['y'=4,'zh'=4,'zl'=4,'core'=2,'x'=4] {'y'}, dimensions={0} | all-to-all | bytes 1179648 | tf_op jit(solution)/shard_map/all_to_all | solution.py:19
  130.9 4.8 %all_to_all.63.sym = bf16[2,4,4,48,384]{4,3,2,1,0:T(8,128)(2,1)S(1)} all-to-all(bf16[2,4,4,48,384]{4,3,2,1,0:T(8,128)(2,1)S(1)} %broadcast_in_dim.58), channel_id=1, replica_groups=mesh['y'=4,'zh'=4,'zl'=4,'core'=2,'x'=4] {'core'}, dimensions={0} | all-to-all | bytes 2359296 | tf_op jit(solution)/shard_map/all_to_all | solution.py:19
  135.7 2.0 shard_map.60
  137.8 15.3 %all_to_all.64.shares = bf16[4,256,384]{2,1,0:T(8,128)(2,1)S(1)} all-to-all(bf16[4,256,384]{2,1,0:T(8,128)(2,1)S(1)} %shard_map.60), channel_id=1, replica_groups=mesh['y'=4,'zh'=4,'zl'=4,'core'=2,'x'=4] {'x'}, dimensions={0} | all-to-all | bytes 1572864 | tf_op jit(solution)/shard_map/all_to_all | solution.py:19
  153.2 2.5 %psum.28 = f32[8,128]{1,0:T(8,128)S(1)} all-reduce(f32[8,128]{1,0:T(8,128)S(1)} %get-tuple-element.24), channel_id=1, replica_groups=mesh['y'=4,'zh'=4,'zl'=4,'core'=2,'x'=4] {'core'}, use_global_device_ids=true, to_apply=%region_4.5 | all-reduce | flops 1024 | bytes 8192 | tf_op jit(solution)/shard_map/psum | solution.py:181
  155.7 9.2 %psum.29 = f32[8,128]{1,0:T(8,128)S(1)} all-reduce(f32[8,128]{1,0:T(8,128)S(1)} %psum.28), channel_id=1, replica_groups=mesh['y'=4,'zh'=4,'zl'=4,'core'=2,'x'=4] {'x'}, use_global_device_ids=true, to_apply=%region_5.6 | all-reduce | flops 1024 | bytes 8192 | tf_op jit(solution)/shard_map/psum | solution.py:181
  164.9 8.9 %psum.30 = f32[8,128]{1,0:T(8,128)S(1)} all-reduce(f32[8,128]{1,0:T(8,128)S(1)} %psum.29), channel_id=1, replica_groups=mesh['y'=4,'zh'=4,'zl'=4,'core'=2,'x'=4] {'y'}, use_global_device_ids=true, to_apply=%region_6.7 | all-reduce | flops 1024 | bytes 8192 | tf_op jit(solution)/shard_map/psum | solution.py:181
  173.8 9.2 %psum.31 = f32[8,128]{1,0:T(8,128)S(1)} all-reduce(f32[8,128]{1,0:T(8,128)S(1)} %psum.30), channel_id=1, replica_groups=mesh['y'=4,'zh'=4,'zl'=4,'core'=2,'x'=4] {'zl'}, use_global_device_ids=true, to_apply=%region_7.8 | all-reduce | flops 1024 | bytes 8192 | tf_op jit(solution)/shard_map/psum | solution.py:181
  183.0 19.7 %all_to_all.65.sums = f32[4,8,128]{2,1,0:T(8,128)S(1)} all-to-all(f32[4,8,128]{2,1,0:T(8,128)S(1)} %broadcast_in_dim.59), channel_id=1, replica_groups=mesh['y'=4,'zh'=4,'zl'=4,'core'=2,'x'=4] {'zh'}, dimensions={0} | all-to-all | bytes 32768 | tf_op jit(solution)/shard_map/all_to_all | solution.py:19
  202.7 0.9 shard_map.62
  (30 shorter events, 1.0 us)
Async XLA Ops:
  7.2 0.9 copy-start.4
  7.2 17.6 %copy-start = (f32[256,384]{1,0:T(8,128)S(1)}, f32[256,384]{1,0:T(8,128)}, u32[]{:S(2)}) copy-start(f32[256,384]{1,0:T(8,128)} %vec.5) | copy-start | bytes 1179652
  7.2 76.8 %all-gather.4.cloned.1.call-start = ((), (), s32[]{:S(2)}) async-start(), calls=%async_computation.11 | async-start | bytes 5898240 | tf_op jit(solution)/shard_map/all_gather | solution.py:124
  7.9 122.9 %all-gather.6.cloned.1.call-start = ((), (), s32[]{:S(2)}) async-start(), calls=%async_computation.12 | async-start | bytes 1474560 | tf_op jit(solution)/shard_map/all_gather | solution.py:153
  93.2 2.3 %copy-start.2 = (bf16[1536,1536]{1,0:T(8,128)(2,1)S(1)}, bf16[1536,1536]{1,0:T(8,128)(2,1)}, u32[]{:S(2)}) copy-start(bf16[1536,1536]{1,0:T(8,128)(2,1)} %all-gather.4.cloned.1.call-done.corner) | copy-start | bytes 14155780
  95.5 1.3 copy-start.3
  130.9 4.8 %copy-start.1 = (bf16[1536,384]{1,0:T(8,128)(2,1)S(1)}, bf16[1536,384]{1,0:T(8,128)(2,1)}, u32[]{:S(2)}) copy-start(bf16[1536,384]{1,0:T(8,128)(2,1)} %all-gather.6.cloned.1.call-done) | copy-start | bytes 3538948
Sparse Core Ops, SparseCore 0:
  10.1 64.1 all-gather.3
  101.7 21.8 all-gather.5

commit v9 on v4

--- a/solution.py
+++ b/solution.py
@@ -12,7 +12,7 @@
 ROW = ("y", "zh", "zl", "core")
 VMEM = pl.BlockSpec(memory_space=pltpu.VMEM)
 SMEM = pl.BlockSpec(memory_space=pltpu.SMEM)
-PARAMS = pltpu.CompilerParams(vmem_limit_bytes=48 * 1024 * 1024)
+PARAMS = pltpu.CompilerParams(vmem_limit_bytes=10 * 1024 * 1024)
 
 
 def swap(pieces, axis):
@@ -48,18 +48,21 @@
     return lax.dot_general(a, b, (((1,), (1,)), ((), ())), preferred_element_type=F32)
 
 
-def partial_kernel(place, vec, proj, sym, own_map, out):
+def partial_kernel(place, vec, sym, proj, own_map, out):
     rows, width = vec.shape
-    blocks = sym.shape[0]
+    blocks = proj.shape[0]
     first = lax.broadcasted_iota(jnp.int32, (width, width), 0)
     second = lax.broadcasted_iota(jnp.int32, (width, width), 1)
     zero = jnp.zeros((width, width), BF16)
     acc = jnp.zeros((rows, width), F32)
     for k in range(blocks):
         shift = (place[0] - k) * width
+        block = jnp.concatenate(
+            [sym[c, y, k] for c in range(sym.shape[0]) for y in range(sym.shape[1])]
+        )
         part = proj[k, :rows]
-        acc += dot(part, jnp.where(first <= second + shift, sym[k], zero))
-        acc += dot_turned(part, jnp.where(first < second - shift, sym[k], zero))
+        acc += dot(part, jnp.where(first <= second + shift, block, zero))
+        acc += dot_turned(part, jnp.where(first < second - shift, block, zero))
     corrected = (vec[...] - acc).astype(BF16)
     for k in range(blocks):
         share = dot_turned(corrected, own_map[k * width : (k + 1) * width])
@@ -102,9 +105,8 @@
 
     before = lax.broadcasted_iota(jnp.int32, (blocks, 1, 1), 0) < place
     edge, here, before = lax.optimization_barrier((edge, here, before))
+    corner_wide = lax.all_gather(corner, "x", axis=1, tiled=True)
     edge_wide = lax.all_gather(edge, "x", axis=1, tiled=True)
-    edge_wide, corner = lax.optimization_barrier((edge_wide, corner))
-    corner_wide = lax.all_gather(corner, "x", axis=1, tiled=True)
     vec_low = vector.astype(BF16)
     cross = lax.dot_general(
         vec_low, edge_wide, (((0,), (0,)), ((), ())), preferred_element_type=F32
@@ -112,21 +114,20 @@
     cross = cross * (1.0 / rows_total)
     for axis in ("core", "y", "zl"):
         cross = scatter_sum(cross.astype(BF16), axis)
-    cross = total(spread(cross.astype(BF16), "zh"))
-    cross_all = spread(cross.astype(BF16), "x").reshape(-1, bond)
-
-    other = dot(dot(cross_all, corner_wide).astype(BF16), tri_inv).astype(BF16)
-    other = other.reshape(blocks, -1, width)
-    own = swap(other, "x")
+    cross = total(spread(cross.astype(BF16), "zh")).astype(BF16)
+    cross_all = spread(cross, "x").reshape(-1, bond)
 
     own_map = dot(corner_wide, tri_inv).astype(BF16)
     proj = dot(edge_wide, own_map).astype(BF16)
     proj = jnp.concatenate([proj, own_map[: width - rows]])
     proj_blocks = lax.all_gather(proj, "x", axis=0)
 
-    chosen = jnp.where(before, other, own)
-    for axis in ("zl", "y", "core"):
-        chosen = join_rows(chosen, axis)
+    other = dot(cross_all, own_map).astype(BF16).reshape(blocks, -1, width)
+    own = swap(other, "x")
+    chosen = join_rows(jnp.where(before, other, own), "zl")
+    chosen = spread(chosen, "y")
+    chosen, proj_blocks = lax.optimization_barrier((chosen, proj_blocks))
+    chosen = spread(chosen, "core")
 
     shares = pl.pallas_call(
         partial_kernel,
@@ -134,7 +135,7 @@
         in_specs=[SMEM] + [VMEM] * 4,
         out_specs=VMEM,
         compiler_params=PARAMS,
-    )(here, vector, proj_blocks, chosen, own_map)
+    )(here, vector, chosen, proj_blocks, own_map)
     shares = swap(shares, "x")
     dedge, sums = pl.pallas_call(
         edge_kernel,
@@ -146,8 +147,10 @@
         out_specs=(VMEM, VMEM),
         compiler_params=PARAMS,
     )(vector, shares)
-    for axis in ("core", "x", "y", "zl", "zh"):
-        sums = lax.psum(sums, axis)
+    sums = lax.psum(sums, "core")
+    for axis in ("x", "y", "zl"):
+        sums = total(spread(sums, axis))
+    sums = lax.psum(sums, "zh")
     return pl.pallas_call(
         functools.partial(finish_kernel, float(rows_total * bond)),
         out_shape=(

time: 217 us -> 196 us (0.903)
  blocking collectives: 154 us -> 145 us
  waiting for transfers between devices: 16.8 us -> 10.3 us
  matrix products: 9.48 us -> 6.33 us
  local copies, waits for them, and re-layouts: 4.19 us -> 1.34 us
    psum x5 -> x2, blocking collectives: 45.9 us -> 16.6 us  [the longest x1 14.1 us: on_device(): sums = lax.psum(sums, 'zh')]
    all_to_all x9 -> x12, blocking collectives: 91.3 us -> 111 us  [swap(): return lax.all_to_all(pieces, axis, split_axis=0, concat_axis=0, tiled=True)]
    all_gather x1, waiting for transfers between devices: 16.7 us -> 4.02 us  [on_device(): corner_wide = lax.all_gather(corner, 'x', axis=1, tiled=True)]
    all_to_all x1, waiting for transfers between devices: 0.01 us -> 5.55 us  [swap(): return lax.all_to_all(pieces, axis, split_axis=0, concat_axis=0, tiled=True)]
    dot_general x3, matrix products: 8.97 us -> 5.82 us  [dot(): return jnp.dot(a, b, preferred_element_type=F32)]
    unnamed x10 -> x8, local copies, waits for them, and re-layouts: 2.97 us -> 0.27 us
  transfers between devices with their start and end apart: 3 -> 3, of which waited for: 1 -> 2; matrix products, arithmetic and copies ran while one was open for 6% -> 5% of each run, Pallas kernels for 0% -> 0%
where the time goes in v9:
time: 196 us; the launch traced here: 195 us
  blocking collectives  145 us (74%)
  between operations  14.2 us (7%)
  starting transfers between devices  12.4 us (6%)
  waiting for transfers between devices  10.3 us (5%)
  matrix products  6.33 us (3%)
  other arithmetic  3.14 us (2%)
  Pallas kernels  3.12 us (2%)
    all_to_all x12, blocking collectives, swap(): return lax.all_to_all(pieces, axis, split_axis=0, concat_axis=0, tiled=True)  111 us
    all_gather x1, blocking collectives, on_device(): edge_wide = lax.all_gather(edge, 'x', axis=1, tiled=True)  16.7 us
    psum x1, blocking collectives, on_device(): sums = lax.psum(sums, 'zh')  14.1 us
    all_to_all x1, starting transfers between devices, swap(): return lax.all_to_all(pieces, axis, split_axis=0, concat_axis=0, tiled=True)  12.4 us
    dot_general x3, matrix products, dot(): return jnp.dot(a, b, preferred_element_type=F32)  5.82 us
    all_to_all x1, waiting for transfers between devices, swap(): return lax.all_to_all(pieces, axis, split_axis=0, concat_axis=0, tiled=True)  5.55 us
    all_gather x1, waiting for transfers between devices, on_device(): corner_wide = lax.all_gather(corner, 'x', axis=1, tiled=True)  4.02 us
  transfers between devices with their start and end apart: 3, of which 2 were waited for; matrix products, arithmetic and copies ran while one was open for 5% of the time, Pallas kernels for 0%

profile of v9, /device:TPU:2, one launch (start us, length us, event | category | flops | bytes accessed | tf_op | source)
XLA Modules:
  0.0 195.4 jit_solution(14792130802927636567)
XLA Ops:
  8.2 16.7 %all_gather.12 = bf16[256,1536]{1,0:T(8,128)(2,1)S(1)} all-gather(bf16[256,384]{1,0:T(8,128)(2,1)S(1)} %copy-done.3), channel_id=1, replica_groups=mesh['y'=4,'zh'=4,'zl'=4,'core'=2,'x'=4] {'x'}, dimensions={1}, use_global_device_ids=true | all-gather | bytes 983040 | tf_op jit(solution)/shard_map/all_gather | solution.py:109
  25.4 4.7 %all_to_all.65 = bf16[2,192,1536]{2,1,0:T(8,128)(2,1)S(1)} all-to-all(bf16[2,192,1536]{2,1,0:T(8,128)(2,1)S(1)} %bitcast.18), channel_id=1, replica_groups=mesh['y'=4,'zh'=4,'zl'=4,'core'=2,'x'=4] {'core'}, dimensions={0} | all-to-all | bytes 2359296 | tf_op jit(solution)/shard_map/all_to_all | solution.py:19
  30.1 1.2 reduce_sum.75
  31.3 14.2 %all_to_all.66 = bf16[4,48,1536]{2,1,0:T(8,128)(2,1)S(1)} all-to-all(bf16[4,48,1536]{2,1,0:T(8,128)(2,1)} %bitcast.19), channel_id=1, replica_groups=mesh['y'=4,'zh'=4,'zl'=4,'core'=2,'x'=4] {'y'}, dimensions={0} | all-to-all | bytes 1179648 | tf_op jit(solution)/shard_map/all_to_all | solution.py:19
  45.7 11.6 %all_to_all.67 = bf16[4,12,1536]{2,1,0:T(8,128)(2,1)S(1)} all-to-all(bf16[4,12,1536]{2,1,0:T(8,128)(2,1)S(1)} %reshape.37), channel_id=1, replica_groups=mesh['y'=4,'zh'=4,'zl'=4,'core'=2,'x'=4] {'zl'}, dimensions={0} | all-to-all | bytes 294912 | tf_op jit(solution)/shard_map/all_to_all | solution.py:19
  58.0 12.4 %all-to-all-start.3 = ((bf16[4,12,1536]{2,1,0:T(8,128)(2,1)}), bf16[4,12,1536]{2,1,0:T(8,128)(2,1)}, u32[]{:S(2)}, u32[]{:S(2)}) async-start(bf16[4,12,1536]{2,1,0:T(8,128)(2,1)} %broadcast_in_dim.33), calls=%async_computation.3 | async-start | bytes 393216 | tf_op jit(solution)/shard_map/all_to_all | solution.py:19
  70.4 4.0 %all-gather.4.cloned.1.call-done = bf16[1536,1536]{1,0:T(8,128)(2,1)} async-done(((bf16[1536,384]{1,0:T(8,128)(2,1)}), bf16[1536,1536]{1,0:T(8,128)(2,1)}) %all-gather.4.cloned.1.call-update) | async-done | bytes 4718608 | tf_op jit(solution)/shard_map/all_gather | solution.py:108
  74.4 4.9 %convolution_convert_fusion.own_map = bf16[1536,384]{1,0:T(8,128)(2,1)S(1)} fusion(bf16[1536,1536]{1,0:T(8,128)(2,1)} %all-gather.4.cloned.1.call-done, bf16[1536,384]{1,0:T(8,128)(2,1)S(1)} %copy-done), kind=kOutput, calls=%fused_computation.2 | convolution fusion | flops 1812529152 | bytes 7077888 | tf_op jit(solution)/shard_map/dot_general | solution.py:44
  79.9 0.7 pad_maximum_fusion
  80.7 5.6 %all-to-all-done.3 = bf16[4,12,1536]{2,1,0:T(8,128)(2,1)} async-done(((bf16[4,12,1536]{2,1,0:T(8,128)(2,1)}), bf16[4,12,1536]{2,1,0:T(8,128)(2,1)}, u32[]{:S(2)}, u32[]{:S(2)}) %all-to-all-start.3) | async-done | bytes 147488 | tf_op jit(solution)/shard_map/all_to_all | solution.py:19
  86.3 1.0 reduce_sum.78
  87.2 9.0 %all_to_all.68 = bf16[4,12,1536]{2,1,0:T(8,128)(2,1)S(1)} all-to-all(bf16[4,12,1536]{2,1,0:T(8,128)(2,1)S(1)} %broadcast_in_dim.34), channel_id=1, replica_groups=mesh['y'=4,'zh'=4,'zl'=4,'core'=2,'x'=4] {'x'}, dimensions={0} | all-to-all | bytes 294912 | tf_op jit(solution)/shard_map/all_to_all | solution.py:19
  96.6 8.4 %all_to_all.69 = bf16[4,12,384]{2,1,0:T(8,128)(2,1)S(1)} all-to-all(bf16[4,12,384]{2,1,0:T(8,128)(2,1)S(1)} %reshape.39), channel_id=1, replica_groups=mesh['y'=4,'zh'=4,'zl'=4,'core'=2,'x'=4] {'x'}, dimensions={0} | all-to-all | bytes 73728 | tf_op jit(solution)/shard_map/all_to_all | solution.py:19
  105.2 9.0 %all_to_all.70 = bf16[4,4,12,384]{3,1,2,0:T(4,128)(2,1)S(1)} all-to-all(bf16[4,4,12,384]{3,1,2,0:T(4,128)(2,1)S(1)} %broadcast_in_dim.35), channel_id=1, replica_groups=mesh['y'=4,'zh'=4,'zl'=4,'core'=2,'x'=4] {'zl'}, dimensions={0} | all-to-all | bytes 294912 | tf_op jit(solution)/shard_map/all_to_all | solution.py:19
  114.3 10.8 %all_to_all.71 = bf16[4,4,48,384]{3,2,1,0:T(8,128)(2,1)S(1)} all-to-all(bf16[4,4,48,384]{3,2,1,0:T(8,128)(2,1)S(1)} %broadcast_in_dim.37), channel_id=1, replica_groups=mesh['y'=4,'zh'=4,'zl'=4,'core'=2,'x'=4] {'y'}, dimensions={0} | all-to-all | bytes 1179648 | tf_op jit(solution)/shard_map/all_to_all | solution.py:19
  125.3 4.8 %all_to_all.72.sym = bf16[2,4,4,48,384]{4,3,2,1,0:T(8,128)(2,1)S(1)} all-to-all(bf16[2,4,4,48,384]{4,3,2,1,0:T(8,128)(2,1)S(1)} %broadcast_in_dim.70), channel_id=1, replica_groups=mesh['y'=4,'zh'=4,'zl'=4,'core'=2,'x'=4] {'core'}, dimensions={0} | all-to-all | bytes 2359296 | tf_op jit(solution)/shard_map/all_to_all | solution.py:19
  130.1 2.0 %shard_map.59 = bf16[4,256,384]{2,1,0:T(8,128)(2,1)S(1)} custom-call(s32[1]{0:T(128)} %bitcast.place, f32[256,384]{1,0:T(8,128)S(1)} %copy-done.1, bf16[2,4,4,48,384]{4,3,2,1,0:T(8,128)(2,1)S(1)} %all_to_all.72.sym, bf16[4,384,384]{2,1,0:T(8,128)(2,1)S(1)} %bitcast.17, bf16[1536,384]{1,0:T(8,128)(2,1)S(1)} %convolution_convert_fusion.own_map), custom_call_target="tpu_custom_call" | custom-call | tf_op jit(solution)/shard_map/pallas_call | solution.py:132
  132.1 15.3 %all_to_all.73.shares = bf16[4,256,384]{2,1,0:T(8,128)(2,1)S(1)} all-to-all(bf16[4,256,384]{2,1,0:T(8,128)(2,1)S(1)} %shard_map.59), channel_id=1, replica_groups=mesh['y'=4,'zh'=4,'zl'=4,'core'=2,'x'=4] {'x'}, dimensions={0} | all-to-all | bytes 1572864 | tf_op jit(solution)/shard_map/all_to_all | solution.py:19
  147.6 2.5 %psum.14 = f32[8,128]{1,0:T(8,128)S(1)} all-reduce(f32[8,128]{1,0:T(8,128)S(1)} %get-tuple-element.14), channel_id=1, replica_groups=mesh['y'=4,'zh'=4,'zl'=4,'core'=2,'x'=4] {'core'}, use_global_device_ids=true, to_apply=%region_4.5 | all-reduce | flops 1024 | bytes 8192 | tf_op jit(solution)/shard_map/psum | solution.py:150
  150.1 7.7 %all_to_all.74 = f32[4,8,128]{2,1,0:T(8,128)S(1)} all-to-all(f32[4,8,128]{2,1,0:T(8,128)S(1)} %broadcast_in_dim.71), channel_id=1, replica_groups=mesh['y'=4,'zh'=4,'zl'=4,'core'=2,'x'=4] {'x'}, dimensions={0} | all-to-all | bytes 32768 | tf_op jit(solution)/shard_map/all_to_all | solution.py:19
  157.8 7.7 %all_to_all.75 = f32[4,8,128]{2,1,0:T(8,128)S(1)} all-to-all(f32[4,8,128]{2,1,0:T(8,128)S(1)} %broadcast_in_dim.72), channel_id=1, replica_groups=mesh['y'=4,'zh'=4,'zl'=4,'core'=2,'x'=4] {'y'}, dimensions={0} | all-to-all | bytes 32768 | tf_op jit(solution)/shard_map/all_to_all | solution.py:19
  165.5 8.0 %all_to_all.76 = f32[4,8,128]{2,1,0:T(8,128)S(1)} all-to-all(f32[4,8,128]{2,1,0:T(8,128)S(1)} %broadcast_in_dim.73), channel_id=1, replica_groups=mesh['y'=4,'zh'=4,'zl'=4,'core'=2,'x'=4] {'zl'}, dimensions={0} | all-to-all | bytes 32768 | tf_op jit(solution)/shard_map/all_to_all | solution.py:19
  173.5 14.1 %psum.15.sums = f32[8,128]{1,0:T(8,128)S(1)} all-reduce(f32[8,128]{1,0:T(8,128)S(1)} %reduce_sum.81), channel_id=1, replica_groups=mesh['y'=4,'zh'=4,'zl'=4,'core'=2,'x'=4] {'zh'}, use_global_device_ids=true, to_apply=%region_8.9 | all-reduce | flops 1024 | bytes 8192 | tf_op jit(solution)/shard_map/psum | solution.py:153
  187.6 0.9 shard_map.61
  (38 shorter events, 3.9 us)
Async XLA Ops:
  7.2 67.2 %copy-start = (bf16[1536,384]{1,0:T(8,128)(2,1)S(1)}, bf16[1536,384]{1,0:T(8,128)(2,1)}, u32[]{:S(2)}) copy-start(bf16[1536,384]{1,0:T(8,128)(2,1)} %param.6) | copy-start | bytes 3538948
  7.2 1.0 copy-start.3
  7.2 17.7 %copy-start.1 = (f32[256,384]{1,0:T(8,128)S(1)}, f32[256,384]{1,0:T(8,128)}, u32[]{:S(2)}) copy-start(f32[256,384]{1,0:T(8,128)} %vec.5) | copy-start | bytes 1179652
  7.2 67.2 %all-gather.4.cloned.1.call-start = ((), (), s32[]{:S(2)}) async-start(), calls=%async_computation.13 | async-start | bytes 5898240 | tf_op jit(solution)/shard_map/all_gather | solution.py:108
  58.0 28.3 %all-to-all-start.3 = ((bf16[4,12,1536]{2,1,0:T(8,128)(2,1)}), bf16[4,12,1536]{2,1,0:T(8,128)(2,1)}, u32[]{:S(2)}, u32[]{:S(2)}) async-start(bf16[4,12,1536]{2,1,0:T(8,128)(2,1)} %broadcast_in_dim.33), calls=%async_computation.3 | async-start | bytes 393216 | tf_op jit(solution)/shard_map/all_to_all | solution.py:19
  70.4 54.8 %all-gather.6.cloned.1.call-start = ((), (), s32[]{:S(2)}) async-start(), calls=%async_computation.14 | async-start | bytes 1474560 | tf_op jit(solution)/shard_map/all_gather | solution.py:123
  125.2 4.8 %copy-start.2 = (bf16[1536,384]{1,0:T(8,128)(2,1)S(1)}, bf16[1536,384]{1,0:T(8,128)(2,1)}, u32[]{:S(2)}) copy-start(bf16[1536,384]{1,0:T(8,128)(2,1)} %all-gather.6.cloned.1.call-done) | copy-start | bytes 3538948
Sparse Core Ops, SparseCore 0:
  10.2 64.1 all-gather.3
  80.8 32.2 all-gather.5

commit v10 on v9

--- a/solution.py
+++ b/solution.py
@@ -46,6 +46,16 @@
 
 def dot_turned(a, b):
     return lax.dot_general(a, b, (((1,), (1,)), ((), ())), preferred_element_type=F32)
+
+
+def add_kernel(pieces, out):
+    out[...] = sum(pieces[i].astype(F32) for i in range(pieces.shape[0])).astype(BF16)
+
+
+def proj_kernel(edge, own_map, out):
+    rows = edge.shape[0]
+    out[:rows] = dot(edge[...], own_map[...]).astype(BF16)
+    out[rows:] = jnp.zeros((out.shape[0] - rows, out.shape[1]), BF16)
 
 
 def partial_kernel(place, vec, sym, proj, own_map, out):
@@ -112,14 +122,32 @@
         vec_low, edge_wide, (((0,), (0,)), ((), ())), preferred_element_type=F32
     )
     cross = cross * (1.0 / rows_total)
-    for axis in ("core", "y", "zl"):
+    pair = swap(cross.astype(BF16).reshape(2, -1, bond), "core")
+    cross = pl.pallas_call(
+        add_kernel,
+        out_shape=jax.ShapeDtypeStruct(pair.shape[1:], BF16),
+        in_specs=[VMEM],
+        out_specs=VMEM,
+        compiler_params=PARAMS,
+    )(pair)
+    for axis in ("y", "zl"):
         cross = scatter_sum(cross.astype(BF16), axis)
     cross = total(spread(cross.astype(BF16), "zh")).astype(BF16)
     cross_all = spread(cross, "x").reshape(-1, bond)
 
     own_map = dot(corner_wide, tri_inv).astype(BF16)
-    proj = dot(edge_wide, own_map).astype(BF16)
-    proj = jnp.concatenate([proj, own_map[: width - rows]])
+    proj = pl.pallas_call(
+        proj_kernel,
+        out_shape=jax.ShapeDtypeStruct((width, width), BF16),
+        in_specs=[VMEM, VMEM],
+        out_specs=VMEM,
+        compiler_params=PARAMS,
+        cost_estimate=pl.CostEstimate(
+            flops=2 * rows * bond * width,
+            bytes_accessed=2 * bond * (rows + width),
+            transcendentals=0,
+        ),
+    )(edge_wide, own_map)
     proj_blocks = lax.all_gather(proj, "x", axis=0)
 
     other = dot(cross_all, own_map).astype(BF16).reshape(blocks, -1, width)

time: 196 us -> 196 us (level)
    dot_general x3 -> x2, matrix products: 5.82 us -> 5.25 us  [dot(): return jnp.dot(a, b, preferred_element_type=F32)]
  transfers between devices with their start and end apart: 3 -> 3, of which waited for: 2 -> 2; matrix products, arithmetic and copies ran while one was open for 5% -> 4% of each run, Pallas kernels for 0% -> 0%
where the time goes in v10:
time: 196 us; the launch traced here: 195 us
  blocking collectives  146 us (74%)
  between operations  14.2 us (7%)
  starting transfers between devices  12.4 us (6%)
  waiting for transfers between devices  10.3 us (5%)
  matrix products  5.78 us (3%)
  Pallas kernels  3.84 us (2%)
  local copies, waits for them, and re-layouts  2.04 us (1%)
    all_to_all x12, blocking collectives, swap(): return lax.all_to_all(pieces, axis, split_axis=0, concat_axis=0, tiled=True)  111 us
    all_gather x1, blocking collectives, on_device(): edge_wide = lax.all_gather(edge, 'x', axis=1, tiled=True)  16.7 us
    psum x1, blocking collectives, on_device(): sums = lax.psum(sums, 'zh')  15.8 us
    all_to_all x1, starting transfers between devices, swap(): return lax.all_to_all(pieces, axis, split_axis=0, concat_axis=0, tiled=True)  12.4 us
    dot_general x2, matrix products, dot(): return jnp.dot(a, b, preferred_element_type=F32)  5.25 us
    all_gather x1, waiting for transfers between devices, on_device(): corner_wide = lax.all_gather(corner, 'x', axis=1, tiled=True)  5.25 us
    all_to_all x1, waiting for transfers between devices, swap(): return lax.all_to_all(pieces, axis, split_axis=0, concat_axis=0, tiled=True)  4.37 us
  transfers between devices with their start and end apart: 3, of which 2 were waited for; matrix products, arithmetic and copies ran while one was open for 4% of the time, Pallas kernels for 0%

profile of v10, /device:TPU:2, one launch (start us, length us, event | category | flops | bytes accessed | tf_op | source)
XLA Modules:
  0.0 195.4 jit_solution(10508466592019214624)
XLA Ops:
  8.2 16.7 %all_gather.12.edge = bf16[256,1536]{1,0:T(8,128)(2,1)S(1)} all-gather(bf16[256,384]{1,0:T(8,128)(2,1)S(1)} %copy-done.4), channel_id=1, replica_groups=mesh['y'=4,'zh'=4,'zl'=4,'core'=2,'x'=4] {'x'}, dimensions={1}, use_global_device_ids=true | all-gather | bytes 983040 | tf_op jit(solution)/shard_map/all_gather | solution.py:119
  25.5 4.7 %all_to_all.65.pieces = bf16[2,192,1536]{2,1,0:T(8,128)(2,1)S(1)} all-to-all(bf16[2,192,1536]{2,1,0:T(8,128)(2,1)S(1)} %bitcast.17), channel_id=1, replica_groups=mesh['y'=4,'zh'=4,'zl'=4,'core'=2,'x'=4] {'core'}, dimensions={0} | all-to-all | bytes 2359296 | tf_op jit(solution)/shard_map/all_to_all | solution.py:19
  30.3 13.1 %all_to_all.66 = bf16[4,48,1536]{2,1,0:T(8,128)(2,1)S(1)} all-to-all(bf16[4,48,1536]{2,1,0:T(8,128)(2,1)S(1)} %bitcast.15), channel_id=1, replica_groups=mesh['y'=4,'zh'=4,'zl'=4,'core'=2,'x'=4] {'y'}, dimensions={0} | all-to-all | bytes 1179648 | tf_op jit(solution)/shard_map/all_to_all | solution.py:19
  43.6 12.4 %all_to_all.67 = bf16[4,12,1536]{2,1,0:T(8,128)(2,1)S(1)} all-to-all(bf16[4,12,1536]{2,1,0:T(8,128)(2,1)S(1)} %reshape.37), channel_id=1, replica_groups=mesh['y'=4,'zh'=4,'zl'=4,'core'=2,'x'=4] {'zl'}, dimensions={0} | all-to-all | bytes 294912 | tf_op jit(solution)/shard_map/all_to_all | solution.py:19
  56.0 0.7 broadcast_in_dim.33
  56.7 12.4 %all-to-all-start.3 = ((bf16[4,12,1536]{2,1,0:T(8,128)(2,1)}), bf16[4,12,1536]{2,1,0:T(8,128)(2,1)}, u32[]{:S(2)}, u32[]{:S(2)}) async-start(bf16[4,12,1536]{2,1,0:T(8,128)(2,1)} %broadcast_in_dim.33), calls=%async_computation.3 | async-start | bytes 393216 | tf_op jit(solution)/shard_map/all_to_all | solution.py:19
  69.1 5.2 %all-gather.4.cloned.1.call-done = bf16[1536,1536]{1,0:T(8,128)(2,1)} async-done(((bf16[1536,384]{1,0:T(8,128)(2,1)}), bf16[1536,1536]{1,0:T(8,128)(2,1)}) %all-gather.4.cloned.1.call-update) | async-done | bytes 4718608 | tf_op jit(solution)/shard_map/all_gather | solution.py:118
  74.4 5.0 %convolution_convert_fusion.own_map = bf16[1536,384]{1,0:T(8,128)(2,1)S(1)} fusion(bf16[1536,1536]{1,0:T(8,128)(2,1)} %all-gather.4.cloned.1.call-done, bf16[1536,384]{1,0:T(8,128)(2,1)S(1)} %copy-done), kind=kOutput, calls=%fused_computation.2 | convolution fusion | flops 1812529152 | bytes 7077888 | tf_op jit(solution)/shard_map/dot_general | solution.py:44
  79.9 0.7 copy-done.2
  80.7 4.4 %all-to-all-done.3 = bf16[4,12,1536]{2,1,0:T(8,128)(2,1)} async-done(((bf16[4,12,1536]{2,1,0:T(8,128)(2,1)}), bf16[4,12,1536]{2,1,0:T(8,128)(2,1)}, u32[]{:S(2)}, u32[]{:S(2)}) %all-to-all-start.3) | async-done | bytes 147488 | tf_op jit(solution)/shard_map/all_to_all | solution.py:19
  85.0 1.0 reduce_sum.65
  86.0 9.0 %all_to_all.68 = bf16[4,12,1536]{2,1,0:T(8,128)(2,1)S(1)} all-to-all(bf16[4,12,1536]{2,1,0:T(8,128)(2,1)S(1)} %broadcast_in_dim.34), channel_id=1, replica_groups=mesh['y'=4,'zh'=4,'zl'=4,'core'=2,'x'=4] {'x'}, dimensions={0} | all-to-all | bytes 294912 | tf_op jit(solution)/shard_map/all_to_all | solution.py:19
  95.4 8.1 %all_to_all.69 = bf16[4,12,384]{2,1,0:T(8,128)(2,1)S(1)} all-to-all(bf16[4,12,384]{2,1,0:T(8,128)(2,1)S(1)} %reshape.39), channel_id=1, replica_groups=mesh['y'=4,'zh'=4,'zl'=4,'core'=2,'x'=4] {'x'}, dimensions={0} | all-to-all | bytes 73728 | tf_op jit(solution)/shard_map/all_to_all | solution.py:19
  103.6 9.0 %all_to_all.70 = bf16[4,4,12,384]{3,1,2,0:T(4,128)(2,1)S(1)} all-to-all(bf16[4,4,12,384]{3,1,2,0:T(4,128)(2,1)S(1)} %broadcast_in_dim.35), channel_id=1, replica_groups=mesh['y'=4,'zh'=4,'zl'=4,'core'=2,'x'=4] {'zl'}, dimensions={0} | all-to-all | bytes 294912 | tf_op jit(solution)/shard_map/all_to_all | solution.py:19
  112.7 10.8 %all_to_all.71 = bf16[4,4,48,384]{3,2,1,0:T(8,128)(2,1)S(1)} all-to-all(bf16[4,4,48,384]{3,2,1,0:T(8,128)(2,1)S(1)} %broadcast_in_dim.37), channel_id=1, replica_groups=mesh['y'=4,'zh'=4,'zl'=4,'core'=2,'x'=4] {'y'}, dimensions={0} | all-to-all | bytes 1179648 | tf_op jit(solution)/shard_map/all_to_all | solution.py:19
  123.7 4.8 %all_to_all.72.sym = bf16[2,4,4,48,384]{4,3,2,1,0:T(8,128)(2,1)S(1)} all-to-all(bf16[2,4,4,48,384]{4,3,2,1,0:T(8,128)(2,1)S(1)} %broadcast_in_dim.70), channel_id=1, replica_groups=mesh['y'=4,'zh'=4,'zl'=4,'core'=2,'x'=4] {'core'}, dimensions={0} | all-to-all | bytes 2359296 | tf_op jit(solution)/shard_map/all_to_all | solution.py:19
  128.5 2.0 %shard_map.61 = bf16[4,256,384]{2,1,0:T(8,128)(2,1)S(1)} custom-call(s32[1]{0:T(128)} %bitcast.place, f32[256,384]{1,0:T(8,128)S(1)} %copy-done.1, bf16[2,4,4,48,384]{4,3,2,1,0:T(8,128)(2,1)S(1)} %all_to_all.72.sym, bf16[4,384,384]{2,1,0:T(8,128)(2,1)S(1)} %bitcast.16, bf16[1536,384]{1,0:T(8,128)(2,1)S(1)} %convolution_convert_fusion.own_map), custom_call_target="tpu_custom_call" | custom-call | tf_op jit(solution)/shard_map/pallas_call | solution.py:160
  130.5 15.2 %all_to_all.73.shares = bf16[4,256,384]{2,1,0:T(8,128)(2,1)S(1)} all-to-all(bf16[4,256,384]{2,1,0:T(8,128)(2,1)S(1)} %shard_map.61), channel_id=1, replica_groups=mesh['y'=4,'zh'=4,'zl'=4,'core'=2,'x'=4] {'x'}, dimensions={0} | all-to-all | bytes 1572864 | tf_op jit(solution)/shard_map/all_to_all | solution.py:19
  145.9 2.5 %psum.14 = f32[8,128]{1,0:T(8,128)S(1)} all-reduce(f32[8,128]{1,0:T(8,128)S(1)} %get-tuple-element.14), channel_id=1, replica_groups=mesh['y'=4,'zh'=4,'zl'=4,'core'=2,'x'=4] {'core'}, use_global_device_ids=true, to_apply=%region_3.4 | all-reduce | flops 1024 | bytes 8192 | tf_op jit(solution)/shard_map/psum | solution.py:178
  148.4 7.7 %all_to_all.74 = f32[4,8,128]{2,1,0:T(8,128)S(1)} all-to-all(f32[4,8,128]{2,1,0:T(8,128)S(1)} %broadcast_in_dim.71), channel_id=1, replica_groups=mesh['y'=4,'zh'=4,'zl'=4,'core'=2,'x'=4] {'x'}, dimensions={0} | all-to-all | bytes 32768 | tf_op jit(solution)/shard_map/all_to_all | solution.py:19
  156.1 7.7 %all_to_all.75 = f32[4,8,128]{2,1,0:T(8,128)S(1)} all-to-all(f32[4,8,128]{2,1,0:T(8,128)S(1)} %broadcast_in_dim.72), channel_id=1, replica_groups=mesh['y'=4,'zh'=4,'zl'=4,'core'=2,'x'=4] {'y'}, dimensions={0} | all-to-all | bytes 32768 | tf_op jit(solution)/shard_map/all_to_all | solution.py:19
  163.8 8.0 %all_to_all.76 = f32[4,8,128]{2,1,0:T(8,128)S(1)} all-to-all(f32[4,8,128]{2,1,0:T(8,128)S(1)} %broadcast_in_dim.73), channel_id=1, replica_groups=mesh['y'=4,'zh'=4,'zl'=4,'core'=2,'x'=4] {'zl'}, dimensions={0} | all-to-all | bytes 32768 | tf_op jit(solution)/shard_map/all_to_all | solution.py:19
  171.8 15.8 %psum.15.sums = f32[8,128]{1,0:T(8,128)S(1)} all-reduce(f32[8,128]{1,0:T(8,128)S(1)} %reduce_sum.68), channel_id=1, replica_groups=mesh['y'=4,'zh'=4,'zl'=4,'core'=2,'x'=4] {'zh'}, use_global_device_ids=true, to_apply=%region_7.8 | all-reduce | flops 1024 | bytes 8192 | tf_op jit(solution)/shard_map/psum | solution.py:181
  187.6 0.9 shard_map.63
  (38 shorter events, 3.3 us)
Async XLA Ops:
  7.2 67.2 %copy-start = (bf16[1536,384]{1,0:T(8,128)(2,1)S(1)}, bf16[1536,384]{1,0:T(8,128)(2,1)}, u32[]{:S(2)}) copy-start(bf16[1536,384]{1,0:T(8,128)(2,1)} %param.6) | copy-start | bytes 3538948
  7.2 1.0 copy-start.4
  7.2 17.7 %copy-start.1 = (f32[256,384]{1,0:T(8,128)S(1)}, f32[256,384]{1,0:T(8,128)}, u32[]{:S(2)}) copy-start(f32[256,384]{1,0:T(8,128)} %vec.5) | copy-start | bytes 1179652
  7.2 67.2 %all-gather.4.cloned.1.call-start = ((), (), s32[]{:S(2)}) async-start(), calls=%async_computation.13 | async-start | bytes 5898240 | tf_op jit(solution)/shard_map/all_gather | solution.py:118
  56.7 28.3 %all-to-all-start.3 = ((bf16[4,12,1536]{2,1,0:T(8,128)(2,1)}), bf16[4,12,1536]{2,1,0:T(8,128)(2,1)}, u32[]{:S(2)}, u32[]{:S(2)}) async-start(bf16[4,12,1536]{2,1,0:T(8,128)(2,1)} %broadcast_in_dim.33), calls=%async_computation.3 | async-start | bytes 393216 | tf_op jit(solution)/shard_map/all_to_all | solution.py:19
  69.1 54.4 %all-gather.6.cloned.1.call-start = ((), (), s32[]{:S(2)}) async-start(), calls=%async_computation.14 | async-start | bytes 1474560 | tf_op jit(solution)/shard_map/all_gather | solution.py:151
  79.9 0.7 copy-start.2
  123.7 4.8 %copy-start.3 = (bf16[1536,384]{1,0:T(8,128)(2,1)S(1)}, bf16[1536,384]{1,0:T(8,128)(2,1)}, u32[]{:S(2)}) copy-start(bf16[1536,384]{1,0:T(8,128)(2,1)} %all-gather.6.cloned.1.call-done) | copy-start | bytes 3538948
Sparse Core Ops, SparseCore 0:
  10.2 64.1 all-gather.3
  80.8 32.2 all-gather.5

commit v11 on v10

--- a/solution.py
+++ b/solution.py
@@ -94,7 +94,8 @@
 
 
 def finish_kernel(count, sums, vec, dedge, out, coeffs):
-    vv, vd, dd = (jnp.sum(sums[i : i + 1], axis=1, keepdims=True) for i in range(3))
+    lines = sum(sums[i] for i in range(sums.shape[0]))
+    vv, vd, dd = (jnp.sum(lines[i : i + 1], axis=1, keepdims=True) for i in range(3))
     along = (vv - vd) / count
     keep = 1.0 - along
     square = (keep * keep * vv - 2.0 * keep * vd + dd) / count
@@ -175,10 +176,8 @@
         out_specs=(VMEM, VMEM),
         compiler_params=PARAMS,
     )(vector, shares)
-    sums = lax.psum(sums, "core")
-    for axis in ("x", "y", "zl"):
-        sums = total(spread(sums, axis))
-    sums = lax.psum(sums, "zh")
+    sums = total(spread(sums, ("y", "core", "x")))
+    sums = spread(sums, ("zh", "zl"))
     return pl.pallas_call(
         functools.partial(finish_kernel, float(rows_total * bond)),
         out_shape=(

time: 196 us -> 188 us (0.959)
  the two profiles are of different devices: /device:TPU:2 before, /device:TPU:1 now
where the time goes in v11:
time: 188 us
  blocking collectives  139 us (74%)
  between operations  14.2 us (8%)
  starting transfers between devices  11.5 us (6%)
  waiting for transfers between devices  9.57 us (5%)
  matrix products  5.77 us (3%)
  Pallas kernels  3.87 us (2%)
  local copies, waits for them, and re-layouts  2.05 us (1%)
    all_to_all x11, blocking collectives, swap(): return lax.all_to_all(pieces, axis, split_axis=0, concat_axis=0, tiled=True)  126 us
    all_gather x1, blocking collectives, on_device(): edge_wide = lax.all_gather(edge, 'x', axis=1, tiled=True)  12.9 us
    all_to_all x1, starting transfers between devices, swap(): return lax.all_to_all(pieces, axis, split_axis=0, concat_axis=0, tiled=True)  11.5 us
    all_gather x1, waiting for transfers between devices, on_device(): corner_wide = lax.all_gather(corner, 'x', axis=1, tiled=True)  8.87 us
    dot_general x2, matrix products, dot(): return jnp.dot(a, b, preferred_element_type=F32)  5.25 us
  transfers between devices with their start and end apart: 3, of which 1 were waited for; matrix products, arithmetic and copies ran while one was open for 4% of the time, Pallas kernels for 0%

profile of v11, /device:TPU:1, one launch (start us, length us, event | category | flops | bytes accessed | tf_op | source)
XLA Modules:
  0.0 187.7 jit_solution(15140048701556033607)
XLA Ops:
  7.2 0.7 all-gather.4.cloned.1.call-update
  8.2 12.9 %all_gather.12.edge = bf16[256,1536]{1,0:T(8,128)(2,1)S(1)} all-gather(bf16[256,384]{1,0:T(8,128)(2,1)S(1)} %copy-done.4), channel_id=1, replica_groups=mesh['y'=4,'zh'=4,'zl'=4,'core'=2,'x'=4] {'x'}, dimensions={1}, use_global_device_ids=true | all-gather | bytes 983040 | tf_op jit(solution)/shard_map/all_gather | solution.py:120
  21.1 0.5 fusion
  21.7 12.4 %all_to_all.60.pieces = bf16[2,192,1536]{2,1,0:T(8,128)(2,1)S(1)} all-to-all(bf16[2,192,1536]{2,1,0:T(8,128)(2,1)S(1)} %bitcast.17), channel_id=1, replica_groups=mesh['y'=4,'zh'=4,'zl'=4,'core'=2,'x'=4] {'core'}, dimensions={0} | all-to-all | bytes 2359296 | tf_op jit(solution)/shard_map/all_to_all | solution.py:19
  34.2 12.1 %all_to_all.61 = bf16[4,48,1536]{2,1,0:T(8,128)(2,1)S(1)} all-to-all(bf16[4,48,1536]{2,1,0:T(8,128)(2,1)S(1)} %bitcast.15), channel_id=1, replica_groups=mesh['y'=4,'zh'=4,'zl'=4,'core'=2,'x'=4] {'y'}, dimensions={0} | all-to-all | bytes 1179648 | tf_op jit(solution)/shard_map/all_to_all | solution.py:19
  46.4 8.2 %all_to_all.62 = bf16[4,12,1536]{2,1,0:T(8,128)(2,1)S(1)} all-to-all(bf16[4,12,1536]{2,1,0:T(8,128)(2,1)S(1)} %reshape.36), channel_id=1, replica_groups=mesh['y'=4,'zh'=4,'zl'=4,'core'=2,'x'=4] {'zl'}, dimensions={0} | all-to-all | bytes 294912 | tf_op jit(solution)/shard_map/all_to_all | solution.py:19
  54.7 0.7 broadcast_in_dim.31
  55.4 11.5 %all-to-all-start.3 = ((bf16[4,12,1536]{2,1,0:T(8,128)(2,1)}), bf16[4,12,1536]{2,1,0:T(8,128)(2,1)}, u32[]{:S(2)}, u32[]{:S(2)}) async-start(bf16[4,12,1536]{2,1,0:T(8,128)(2,1)} %broadcast_in_dim.31), calls=%async_computation.3 | async-start | bytes 393216 | tf_op jit(solution)/shard_map/all_to_all | solution.py:19
  66.9 8.9 %all-gather.4.cloned.1.call-done = bf16[1536,1536]{1,0:T(8,128)(2,1)} async-done(((bf16[1536,384]{1,0:T(8,128)(2,1)}), bf16[1536,1536]{1,0:T(8,128)(2,1)}) %all-gather.4.cloned.1.call-update) | async-done | bytes 4718608 | tf_op jit(solution)/shard_map/all_gather | solution.py:119
  75.7 4.9 %convolution_convert_fusion.own_map = bf16[1536,384]{1,0:T(8,128)(2,1)S(1)} fusion(bf16[1536,1536]{1,0:T(8,128)(2,1)} %all-gather.4.cloned.1.call-done, bf16[1536,384]{1,0:T(8,128)(2,1)S(1)} %copy-done), kind=kOutput, calls=%fused_computation.2 | convolution fusion | flops 1812529152 | bytes 7077888 | tf_op jit(solution)/shard_map/dot_general | solution.py:44
  80.7 0.6 shard_map.60
  81.3 0.7 copy-done.2
  82.0 1.0 reduce_sum.47
  83.0 8.2 %all_to_all.63 = bf16[4,12,1536]{2,1,0:T(8,128)(2,1)S(1)} all-to-all(bf16[4,12,1536]{2,1,0:T(8,128)(2,1)S(1)} %broadcast_in_dim.32), channel_id=1, replica_groups=mesh['y'=4,'zh'=4,'zl'=4,'core'=2,'x'=4] {'x'}, dimensions={0} | all-to-all | bytes 294912 | tf_op jit(solution)/shard_map/all_to_all | solution.py:19
  91.2 0.3 convolution_convert_fusion.1
  91.5 6.7 %all_to_all.64 = bf16[4,12,384]{2,1,0:T(8,128)(2,1)S(1)} all-to-all(bf16[4,12,384]{2,1,0:T(8,128)(2,1)S(1)} %reshape.38), channel_id=1, replica_groups=mesh['y'=4,'zh'=4,'zl'=4,'core'=2,'x'=4] {'x'}, dimensions={0} | all-to-all | bytes 73728 | tf_op jit(solution)/shard_map/all_to_all | solution.py:19
  98.4 10.0 %all_to_all.65 = bf16[4,4,12,384]{3,1,2,0:T(4,128)(2,1)S(1)} all-to-all(bf16[4,4,12,384]{3,1,2,0:T(4,128)(2,1)S(1)} %broadcast_in_dim.33), channel_id=1, replica_groups=mesh['y'=4,'zh'=4,'zl'=4,'core'=2,'x'=4] {'zl'}, dimensions={0} | all-to-all | bytes 294912 | tf_op jit(solution)/shard_map/all_to_all | solution.py:19
  108.5 11.1 %all_to_all.66 = bf16[4,4,48,384]{3,2,1,0:T(8,128)(2,1)S(1)} all-to-all(bf16[4,4,48,384]{3,2,1,0:T(8,128)(2,1)S(1)} %broadcast_in_dim.63), channel_id=1, replica_groups=mesh['y'=4,'zh'=4,'zl'=4,'core'=2,'x'=4] {'y'}, dimensions={0} | all-to-all | bytes 1179648 | tf_op jit(solution)/shard_map/all_to_all | solution.py:19
  119.7 10.8 %all_to_all.67.sym = bf16[2,4,4,48,384]{4,3,2,1,0:T(8,128)(2,1)S(1)} all-to-all(bf16[2,4,4,48,384]{4,3,2,1,0:T(8,128)(2,1)S(1)} %broadcast_in_dim.64), channel_id=1, replica_groups=mesh['y'=4,'zh'=4,'zl'=4,'core'=2,'x'=4] {'core'}, dimensions={0} | all-to-all | bytes 2359296 | tf_op jit(solution)/shard_map/all_to_all | solution.py:19
  130.5 2.0 %shard_map.61 = bf16[4,256,384]{2,1,0:T(8,128)(2,1)S(1)} custom-call(s32[1]{0:T(128)} %bitcast.place, f32[256,384]{1,0:T(8,128)S(1)} %copy-done.1, bf16[2,4,4,48,384]{4,3,2,1,0:T(8,128)(2,1)S(1)} %all_to_all.67.sym, bf16[4,384,384]{2,1,0:T(8,128)(2,1)S(1)} %bitcast.16, bf16[1536,384]{1,0:T(8,128)(2,1)S(1)} %convolution_convert_fusion.own_map), custom_call_target="tpu_custom_call" | custom-call | tf_op jit(solution)/shard_map/pallas_call | solution.py:161
  132.5 14.4 %all_to_all.68.shares = bf16[4,256,384]{2,1,0:T(8,128)(2,1)S(1)} all-to-all(bf16[4,256,384]{2,1,0:T(8,128)(2,1)S(1)} %shard_map.61), channel_id=1, replica_groups=mesh['y'=4,'zh'=4,'zl'=4,'core'=2,'x'=4] {'x'}, dimensions={0} | all-to-all | bytes 1572864 | tf_op jit(solution)/shard_map/all_to_all | solution.py:19
  147.2 11.8 %all_to_all.69 = f32[32,8,128]{2,1,0:T(8,128)S(1)} all-to-all(f32[32,8,128]{2,1,0:T(8,128)S(1)} %broadcast_in_dim.65), channel_id=1, replica_groups=mesh['y'=4,'zh'=4,'zl'=4,'core'=2,'x'=4] {'y','core','x'}, dimensions={0} | all-to-all | bytes 262144 | tf_op jit(solution)/shard_map/all_to_all | solution.py:19
  159.1 20.8 %all_to_all.70.sums = f32[16,8,128]{2,1,0:T(8,128)S(1)} all-to-all(f32[16,8,128]{2,1,0:T(8,128)S(1)} %broadcast_in_dim.66), channel_id=1, replica_groups=mesh['y'=4,'zh'=4,'zl'=4,'core'=2,'x'=4] {'zh','zl'}, dimensions={0} | all-to-all | bytes 131072 | tf_op jit(solution)/shard_map/all_to_all | solution.py:19
  179.8 1.0 shard_map.63
  (32 shorter events, 1.3 us)
Async XLA Ops:
  7.2 68.6 %copy-start = (bf16[1536,384]{1,0:T(8,128)(2,1)S(1)}, bf16[1536,384]{1,0:T(8,128)(2,1)}, u32[]{:S(2)}) copy-start(bf16[1536,384]{1,0:T(8,128)(2,1)} %param.6) | copy-start | bytes 3538948
  7.2 1.0 copy-start.4
  7.2 13.9 %copy-start.1 = (f32[256,384]{1,0:T(8,128)S(1)}, f32[256,384]{1,0:T(8,128)}, u32[]{:S(2)}) copy-start(f32[256,384]{1,0:T(8,128)} %vec.5) | copy-start | bytes 1179652
  7.2 68.5 %all-gather.4.cloned.1.call-start = ((), (), s32[]{:S(2)}) async-start(), calls=%async_computation.12 | async-start | bytes 5898240 | tf_op jit(solution)/shard_map/all_gather | solution.py:119
  55.4 26.7 %all-to-all-start.3 = ((bf16[4,12,1536]{2,1,0:T(8,128)(2,1)}), bf16[4,12,1536]{2,1,0:T(8,128)(2,1)}, u32[]{:S(2)}, u32[]{:S(2)}) async-start(bf16[4,12,1536]{2,1,0:T(8,128)(2,1)} %broadcast_in_dim.31), calls=%async_computation.3 | async-start | bytes 393216 | tf_op jit(solution)/shard_map/all_to_all | solution.py:19
  66.9 52.7 %all-gather.6.cloned.1.call-start = ((), (), s32[]{:S(2)}) async-start(), calls=%async_computation.13 | async-start | bytes 1474560 | tf_op jit(solution)/shard_map/all_gather | solution.py:152
  81.3 0.7 copy-start.2
  119.7 10.8 %copy-start.3 = (bf16[1536,384]{1,0:T(8,128)(2,1)S(1)}, bf16[1536,384]{1,0:T(8,128)(2,1)}, u32[]{:S(2)}) copy-start(bf16[1536,384]{1,0:T(8,128)(2,1)} %all-gather.6.cloned.1.call-done) | copy-start | bytes 3538948
Sparse Core Ops, SparseCore 0:
  10.2 65.5 all-gather.3
  82.1 31.8 all-gather.5

commit v12 on v11

--- a/solution.py
+++ b/solution.py
@@ -13,6 +13,7 @@
 VMEM = pl.BlockSpec(memory_space=pltpu.VMEM)
 SMEM = pl.BlockSpec(memory_space=pltpu.SMEM)
 PARAMS = pltpu.CompilerParams(vmem_limit_bytes=10 * 1024 * 1024)
+LARGE = pltpu.CompilerParams(vmem_limit_bytes=56 * 1024 * 1024)
 
 
 def swap(pieces, axis):
@@ -48,14 +49,35 @@
     return lax.dot_general(a, b, (((1,), (1,)), ((), ())), preferred_element_type=F32)
 
 
+def cross_kernel(scale, vec, edge, out):
+    width = vec.shape[1]
+    turned = vec[...].T.astype(BF16)
+    for k in range(edge.shape[0]):
+        out[:, k * width : (k + 1) * width] = (dot(turned, edge[k]) * scale).astype(BF16)
+
+
 def add_kernel(pieces, out):
     out[...] = sum(pieces[i].astype(F32) for i in range(pieces.shape[0])).astype(BF16)
 
 
-def proj_kernel(edge, own_map, out):
-    rows = edge.shape[0]
-    out[:rows] = dot(edge[...], own_map[...]).astype(BF16)
-    out[rows:] = jnp.zeros((out.shape[0] - rows, out.shape[1]), BF16)
+def map_kernel(corner, tri_inv, edge, own_map, proj, acc):
+    step = pl.program_id(0)
+    blocks, _, width = corner.shape
+    rows = edge.shape[1]
+
+    @pl.when(step == 0)
+    def _():
+        acc[...] = jnp.zeros_like(acc)
+        proj[rows:] = jnp.zeros((proj.shape[0] - rows, proj.shape[1]), BF16)
+
+    own_map[...] = sum(
+        dot(corner[k], tri_inv[k * width : (k + 1) * width]) for k in range(blocks)
+    ).astype(BF16)
+    acc[...] += dot(edge[0], own_map[...])
+
+    @pl.when(step == pl.num_programs(0) - 1)
+    def _():
+        proj[:rows] = acc[...].astype(BF16)
 
 
 def partial_kernel(place, vec, sym, proj, own_map, out):
@@ -116,14 +138,16 @@
 
     before = lax.broadcasted_iota(jnp.int32, (blocks, 1, 1), 0) < place
     edge, here, before = lax.optimization_barrier((edge, here, before))
-    corner_wide = lax.all_gather(corner, "x", axis=1, tiled=True)
-    edge_wide = lax.all_gather(edge, "x", axis=1, tiled=True)
-    vec_low = vector.astype(BF16)
-    cross = lax.dot_general(
-        vec_low, edge_wide, (((0,), (0,)), ((), ())), preferred_element_type=F32
-    )
-    cross = cross * (1.0 / rows_total)
-    pair = swap(cross.astype(BF16).reshape(2, -1, bond), "core")
+    corner_blocks = lax.all_gather(corner, "x", axis=0)
+    edge_blocks = spread(edge, "x")
+    cross = pl.pallas_call(
+        functools.partial(cross_kernel, 1.0 / rows_total),
+        out_shape=jax.ShapeDtypeStruct((width, bond), BF16),
+        in_specs=[VMEM, VMEM],
+        out_specs=VMEM,
+        compiler_params=PARAMS,
+    )(vector, edge_blocks)
+    pair = swap(cross.reshape(2, -1, bond), "core")
     cross = pl.pallas_call(
         add_kernel,
         out_shape=jax.ShapeDtypeStruct(pair.shape[1:], BF16),
@@ -136,19 +160,30 @@
     cross = total(spread(cross.astype(BF16), "zh")).astype(BF16)
     cross_all = spread(cross, "x").reshape(-1, bond)
 
-    own_map = dot(corner_wide, tri_inv).astype(BF16)
-    proj = pl.pallas_call(
-        proj_kernel,
-        out_shape=jax.ShapeDtypeStruct((width, width), BF16),
-        in_specs=[VMEM, VMEM],
-        out_specs=VMEM,
-        compiler_params=PARAMS,
+    own_map, proj = pl.pallas_call(
+        map_kernel,
+        grid=(blocks,),
+        out_shape=(
+            jax.ShapeDtypeStruct((bond, width), BF16),
+            jax.ShapeDtypeStruct((width, width), BF16),
+        ),
+        in_specs=[
+            pl.BlockSpec((blocks, width, width), lambda i: (0, i, 0)),
+            pl.BlockSpec((bond, width), lambda i: (0, 0)),
+            pl.BlockSpec((1, rows, width), lambda i: (i, 0, 0)),
+        ],
+        out_specs=(
+            pl.BlockSpec((width, width), lambda i: (i, 0)),
+            pl.BlockSpec((width, width), lambda i: (0, 0)),
+        ),
+        scratch_shapes=[pltpu.VMEM((rows, width), F32)],
+        compiler_params=LARGE,
         cost_estimate=pl.CostEstimate(
-            flops=2 * rows * bond * width,
-            bytes_accessed=2 * bond * (rows + width),
+            flops=2 * (bond + rows) * bond * width,
+            bytes_accessed=2 * bond * (bond + 2 * width),
             transcendentals=0,
         ),
-    )(edge_wide, own_map)
+    )(corner_blocks, tri_inv, edge_blocks)
     proj_blocks = lax.all_gather(proj, "x", axis=0)
 
     other = dot(cross_all, own_map).astype(BF16).reshape(blocks, -1, width)

time: 188 us -> 189 us (level)
  Pallas kernels: 3.87 us -> 11.8 us
  matrix products: 5.77 us -> 0.3 us
  waiting for transfers between devices: 9.57 us -> 7.07 us
  blocking collectives: 139 us -> 141 us
    all_to_all x11 -> x12, blocking collectives: 126 us -> 141 us  [swap(): return lax.all_to_all(pieces, axis, split_axis=0, concat_axis=0, tiled=True)]
    all_gather x1 -> x0, blocking collectives: 12.9 us -> none  [on_device(): edge_wide = lax.all_gather(edge, 'x', axis=1, tiled=True)]
    pallas_call x1 -> x2, Pallas kernels: 0.57 us -> 8.51 us  [the longest x1 7.89 us: on_device(): pl.pallas_call(map_kernel, grid=(blocks,), out_shape=(jax.ShapeDtypeStruc...]
    dot_general x2 -> x1, matrix products: 5.25 us -> 0.3 us  [dot(): return jnp.dot(a, b, preferred_element_type=F32)]
    all_gather x1, waiting for transfers between devices: 8.87 us -> 6.37 us  [on_device(): corner_blocks = lax.all_gather(corner, 'x', axis=0)]
  transfers between devices with their start and end apart: 3 -> 3, of which waited for: 1 -> 1; matrix products, arithmetic and copies ran while one was open for 4% -> 1% of each run, Pallas kernels for 0% -> 5%
where the time goes in v12:
time: 189 us; the launch traced here: 188 us
  blocking collectives  141 us (75%)
  between operations  14.2 us (8%)
  starting transfers between devices  12.1 us (6%)
  Pallas kernels  11.8 us (6%)
  waiting for transfers between devices  7.07 us (4%)
    all_to_all x12, blocking collectives, swap(): return lax.all_to_all(pieces, axis, split_axis=0, concat_axis=0, tiled=True)  141 us
    all_to_all x1, starting transfers between devices, swap(): return lax.all_to_all(pieces, axis, split_axis=0, concat_axis=0, tiled=True)  12.1 us
    pallas_call x1, Pallas kernels, on_device(): pl.pallas_call(map_kernel, grid=(blocks,), out_shape=(jax.ShapeDtypeStruc...  7.89 us
    all_gather x1, waiting for transfers between devices, on_device(): corner_blocks = lax.all_gather(corner, 'x', axis=0)  6.37 us
  transfers between devices with their start and end apart: 3, of which 1 were waited for; matrix products, arithmetic and copies ran while one was open for 1% of the time, Pallas kernels for 5%

profile of v12, /device:TPU:1, one launch (start us, length us, event | category | flops | bytes accessed | tf_op | source)
XLA Modules:
  0.0 188.5 jit_solution(9622716160440001397)
XLA Ops:
  7.2 0.7 all-gather.5.cloned.1.call-update
  7.9 0.2 copy-done.4
  8.2 13.1 %all_to_all.65.edge = bf16[4,256,384]{2,1,0:T(8,128)(2,1)S(1)} all-to-all(bf16[4,256,384]{2,1,0:T(8,128)(2,1)S(1)} %broadcast_in_dim.33), channel_id=1, replica_groups=mesh['y'=4,'zh'=4,'zl'=4,'core'=2,'x'=4] {'x'}, dimensions={0} | all-to-all | bytes 1572864 | tf_op jit(solution)/shard_map/all_to_all | solution.py:20
  21.3 0.6 shard_map.59
  21.9 0.3 copy-done.2
  22.2 10.1 %all_to_all.66.pieces = bf16[2,192,1536]{2,1,0:T(8,128)(2,1)S(1)} all-to-all(bf16[2,192,1536]{2,1,0:T(8,128)(2,1)S(1)} %bitcast.11), channel_id=1, replica_groups=mesh['y'=4,'zh'=4,'zl'=4,'core'=2,'x'=4] {'core'}, dimensions={0} | all-to-all | bytes 2359296 | tf_op jit(solution)/shard_map/all_to_all | solution.py:20
  32.4 12.7 %all_to_all.67 = bf16[4,48,1536]{2,1,0:T(8,128)(2,1)S(1)} all-to-all(bf16[4,48,1536]{2,1,0:T(8,128)(2,1)S(1)} %bitcast.12), channel_id=1, replica_groups=mesh['y'=4,'zh'=4,'zl'=4,'core'=2,'x'=4] {'y'}, dimensions={0} | all-to-all | bytes 1179648 | tf_op jit(solution)/shard_map/all_to_all | solution.py:20
  45.2 11.3 %all_to_all.68 = bf16[4,12,1536]{2,1,0:T(8,128)(2,1)S(1)} all-to-all(bf16[4,12,1536]{2,1,0:T(8,128)(2,1)S(1)} %reshape.37), channel_id=1, replica_groups=mesh['y'=4,'zh'=4,'zl'=4,'core'=2,'x'=4] {'zl'}, dimensions={0} | all-to-all | bytes 294912 | tf_op jit(solution)/shard_map/all_to_all | solution.py:20
  56.6 0.7 broadcast_in_dim.34
  57.2 12.1 %all-to-all-start.4 = ((bf16[4,12,1536]{2,1,0:T(8,128)(2,1)}), bf16[4,12,1536]{2,1,0:T(8,128)(2,1)S(1)}, u32[]{:S(2)}, u32[]{:S(2)}) async-start(bf16[4,12,1536]{2,1,0:T(8,128)(2,1)} %broadcast_in_dim.34), calls=%async_computation.4 | async-start | bytes 393216 | tf_op jit(solution)/shard_map/all_to_all | solution.py:20
  69.3 6.4 %all-gather.5.cloned.1.call-done = bf16[6144,384]{1,0:T(8,128)(2,1)} async-done(((bf16[1536,384]{1,0:T(8,128)(2,1)}), bf16[6144,384]{1,0:T(8,128)(2,1)}) %all-gather.5.cloned.1.call-update) | async-done | bytes 4718608 | tf_op jit(solution)/shard_map/all_gather | solution.py:141
  75.7 7.9 %shard_map.61 = (bf16[1536,384]{1,0:T(8,128)(2,1)}, bf16[384,384]{1,0:T(8,128)(2,1)}) custom-call(bf16[4,1536,384]{2,1,0:T(8,128)(2,1)} %bitcast.16, bf16[1536,384]{1,0:T(8,128)(2,1)} %tri_inv.1, bf16[4,256,384]{2,1,0:T(8,128)(2,1)} %copy-done.2), custom_call_target="tpu_custom_call" | custom-call | flops 2113929216 | bytes 7077888 | tf_op jit(solution)/shard_map/pallas_call | solution.py:163
  83.7 8.2 %all_to_all.69 = bf16[4,12,1536]{2,1,0:T(8,128)(2,1)S(1)} all-to-all(bf16[4,12,1536]{2,1,0:T(8,128)(2,1)S(1)} %broadcast_in_dim.35), channel_id=1, replica_groups=mesh['y'=4,'zh'=4,'zl'=4,'core'=2,'x'=4] {'x'}, dimensions={0} | all-to-all | bytes 294912 | tf_op jit(solution)/shard_map/all_to_all | solution.py:20
  92.0 0.3 convolution_convert_fusion
  92.3 6.7 %all_to_all.70 = bf16[4,12,384]{2,1,0:T(8,128)(2,1)S(1)} all-to-all(bf16[4,12,384]{2,1,0:T(8,128)(2,1)S(1)} %reshape.39), channel_id=1, replica_groups=mesh['y'=4,'zh'=4,'zl'=4,'core'=2,'x'=4] {'x'}, dimensions={0} | all-to-all | bytes 73728 | tf_op jit(solution)/shard_map/all_to_all | solution.py:20
  99.2 10.0 %all_to_all.71 = bf16[4,4,12,384]{3,1,2,0:T(4,128)(2,1)S(1)} all-to-all(bf16[4,4,12,384]{3,1,2,0:T(4,128)(2,1)S(1)} %broadcast_in_dim.36), channel_id=1, replica_groups=mesh['y'=4,'zh'=4,'zl'=4,'core'=2,'x'=4] {'zl'}, dimensions={0} | all-to-all | bytes 294912 | tf_op jit(solution)/shard_map/all_to_all | solution.py:20
  109.3 11.1 %all_to_all.72 = bf16[4,4,48,384]{3,2,1,0:T(8,128)(2,1)S(1)} all-to-all(bf16[4,4,48,384]{3,2,1,0:T(8,128)(2,1)S(1)} %broadcast_in_dim.70), channel_id=1, replica_groups=mesh['y'=4,'zh'=4,'zl'=4,'core'=2,'x'=4] {'y'}, dimensions={0} | all-to-all | bytes 1179648 | tf_op jit(solution)/shard_map/all_to_all | solution.py:20
  120.5 10.4 %all_to_all.73.sym = bf16[2,4,4,48,384]{4,3,2,1,0:T(8,128)(2,1)S(1)} all-to-all(bf16[2,4,4,48,384]{4,3,2,1,0:T(8,128)(2,1)S(1)} %broadcast_in_dim.71), channel_id=1, replica_groups=mesh['y'=4,'zh'=4,'zl'=4,'core'=2,'x'=4] {'core'}, dimensions={0} | all-to-all | bytes 2359296 | tf_op jit(solution)/shard_map/all_to_all | solution.py:20
  130.9 2.0 %shard_map.62 = bf16[4,256,384]{2,1,0:T(8,128)(2,1)S(1)} custom-call(s32[1]{0:T(128)} %bitcast.place, f32[256,384]{1,0:T(8,128)S(1)} %copy-done, bf16[2,4,4,48,384]{4,3,2,1,0:T(8,128)(2,1)S(1)} %all_to_all.73.sym, bf16[4,384,384]{2,1,0:T(8,128)(2,1)S(1)} %bitcast.13, bf16[1536,384]{1,0:T(8,128)(2,1)S(1)} %copy-done.1), custom_call_target="tpu_custom_call" | custom-call | tf_op jit(solution)/shard_map/pallas_call | solution.py:196
  133.0 14.4 %all_to_all.74.shares = bf16[4,256,384]{2,1,0:T(8,128)(2,1)S(1)} all-to-all(bf16[4,256,384]{2,1,0:T(8,128)(2,1)S(1)} %shard_map.62), channel_id=1, replica_groups=mesh['y'=4,'zh'=4,'zl'=4,'core'=2,'x'=4] {'x'}, dimensions={0} | all-to-all | bytes 1572864 | tf_op jit(solution)/shard_map/all_to_all | solution.py:20
  147.4 0.2 shard_map.63
  147.6 11.8 %all_to_all.75 = f32[32,8,128]{2,1,0:T(8,128)S(1)} all-to-all(f32[32,8,128]{2,1,0:T(8,128)S(1)} %broadcast_in_dim.72), channel_id=1, replica_groups=mesh['y'=4,'zh'=4,'zl'=4,'core'=2,'x'=4] {'y','core','x'}, dimensions={0} | all-to-all | bytes 262144 | tf_op jit(solution)/shard_map/all_to_all | solution.py:20
  159.5 21.2 %all_to_all.76.sums = f32[16,8,128]{2,1,0:T(8,128)S(1)} all-to-all(f32[16,8,128]{2,1,0:T(8,128)S(1)} %broadcast_in_dim.73), channel_id=1, replica_groups=mesh['y'=4,'zh'=4,'zl'=4,'core'=2,'x'=4] {'zh','zl'}, dimensions={0} | all-to-all | bytes 131072 | tf_op jit(solution)/shard_map/all_to_all | solution.py:20
  180.6 1.0 shard_map.64
  (32 shorter events, 0.9 us)
Async XLA Ops:
  7.2 0.9 copy-start.4
  7.2 68.5 %all-gather.5.cloned.1.call-start = ((), (), s32[]{:S(2)}) async-start(), calls=%async_computation.13 | async-start | bytes 5898240 | tf_op jit(solution)/shard_map/all_gather | solution.py:141
  8.1 13.2 %copy-start = (f32[256,384]{1,0:T(8,128)S(1)}, f32[256,384]{1,0:T(8,128)}, u32[]{:S(2)}) copy-start(f32[256,384]{1,0:T(8,128)} %vec.7) | copy-start | bytes 1179652
  21.3 0.9 copy-start.2
  57.2 26.4 %all-to-all-start.4 = ((bf16[4,12,1536]{2,1,0:T(8,128)(2,1)}), bf16[4,12,1536]{2,1,0:T(8,128)(2,1)S(1)}, u32[]{:S(2)}, u32[]{:S(2)}) async-start(bf16[4,12,1536]{2,1,0:T(8,128)(2,1)} %broadcast_in_dim.34), calls=%async_computation.4 | async-start | bytes 393216 | tf_op jit(solution)/shard_map/all_to_all | solution.py:20
  69.3 51.0 %all-gather.7.cloned.1.call-start = ((), (), s32[]{:S(2)}) async-start(), calls=%async_computation.14 | async-start | bytes 1474560 | tf_op jit(solution)/shard_map/all_gather | solution.py:187
  83.6 8.4 %copy-start.1 = (bf16[1536,384]{1,0:T(8,128)(2,1)S(1)}, bf16[1536,384]{1,0:T(8,128)(2,1)}, u32[]{:S(2)}) copy-start(bf16[1536,384]{1,0:T(8,128)(2,1)} %get-tuple-element.14.own_map) | copy-start | bytes 3538948
  120.5 10.4 %copy-start.3 = (bf16[1536,384]{1,0:T(8,128)(2,1)S(1)}, bf16[1536,384]{1,0:T(8,128)(2,1)}, u32[]{:S(2)}) copy-start(bf16[1536,384]{1,0:T(8,128)(2,1)} %all-gather.7.cloned.1.call-done) | copy-start | bytes 3538948
Sparse Core Ops, SparseCore 0:
  10.1 65.5 all-gather.4
  83.8 31.5 all-gather.6

commit v13 on v11

--- a/solution.py
+++ b/solution.py
@@ -13,6 +13,7 @@
 VMEM = pl.BlockSpec(memory_space=pltpu.VMEM)
 SMEM = pl.BlockSpec(memory_space=pltpu.SMEM)
 PARAMS = pltpu.CompilerParams(vmem_limit_bytes=10 * 1024 * 1024)
+LARGE = pltpu.CompilerParams(vmem_limit_bytes=56 * 1024 * 1024)
 
 
 def swap(pieces, axis):
@@ -140,9 +141,13 @@
     proj = pl.pallas_call(
         proj_kernel,
         out_shape=jax.ShapeDtypeStruct((width, width), BF16),
-        in_specs=[VMEM, VMEM],
-        out_specs=VMEM,
-        compiler_params=PARAMS,
+        grid=(1,),
+        in_specs=[
+            pl.BlockSpec((rows, bond), lambda i: (0, 0)),
+            pl.BlockSpec((bond, width), lambda i: (0, 0)),
+        ],
+        out_specs=pl.BlockSpec((width, width), lambda i: (0, 0)),
+        compiler_params=LARGE,
         cost_estimate=pl.CostEstimate(
             flops=2 * rows * bond * width,
             bytes_accessed=2 * bond * (rows + width),

time: 188 us -> 190 us (1.011)
  Pallas kernels: 3.87 us -> 6.1 us
    pallas_call x1, Pallas kernels: 0.57 us -> 2.8 us  [on_device(): pl.pallas_call(proj_kernel, out_shape=jax.ShapeDtypeStruct((width, width)...]
  transfers between devices with their start and end apart: 3 -> 3, of which waited for: 1 -> 1; matrix products, arithmetic and copies ran while one was open for 4% -> 4% of each run, Pallas kernels for 0% -> 2%
where the time goes in v13:
time: 190 us; the launch traced here: 189 us
  blocking collectives  140 us (74%)
  between operations  14.2 us (7%)
  starting transfers between devices  11.5 us (6%)
  waiting for transfers between devices  9.23 us (5%)
  matrix products  6.82 us (4%)
  Pallas kernels  6.1 us (3%)
    all_to_all x11, blocking collectives, swap(): return lax.all_to_all(pieces, axis, split_axis=0, concat_axis=0, tiled=True)  127 us
    all_gather x1, blocking collectives, on_device(): edge_wide = lax.all_gather(edge, 'x', axis=1, tiled=True)  12.9 us
    all_to_all x1, starting transfers between devices, swap(): return lax.all_to_all(pieces, axis, split_axis=0, concat_axis=0, tiled=True)  11.5 us
    all_gather x1, waiting for transfers between devices, on_device(): corner_wide = lax.all_gather(corner, 'x', axis=1, tiled=True)  8.53 us
    dot_general x2, matrix products, dot(): return jnp.dot(a, b, preferred_element_type=F32)  6.31 us
  transfers between devices with their start and end apart: 3, of which 1 were waited for; matrix products, arithmetic and copies ran while one was open for 4% of the time, Pallas kernels for 2%

profile of v13, /device:TPU:1, one launch (start us, length us, event | category | flops | bytes accessed | tf_op | source)
XLA Modules:
  0.0 189.4 jit_solution(14858169550662244467)
XLA Ops:
  7.2 0.7 all-gather.4.cloned.1.call-update
  8.0 0.3 copy-done.5
  8.2 12.9 %all_gather.12.edge = bf16[256,1536]{1,0:T(8,128)(2,1)S(1)} all-gather(bf16[256,384]{1,0:T(8,128)(2,1)S(1)} %copy-done.5), channel_id=1, replica_groups=mesh['y'=4,'zh'=4,'zl'=4,'core'=2,'x'=4] {'x'}, dimensions={1}, use_global_device_ids=true | all-gather | bytes 983040 | tf_op jit(solution)/shard_map/all_gather | solution.py:121
  21.1 0.5 fusion
  21.6 0.4 copy-done.4
  22.0 12.4 %all_to_all.60.pieces = bf16[2,192,1536]{2,1,0:T(8,128)(2,1)S(1)} all-to-all(bf16[2,192,1536]{2,1,0:T(8,128)(2,1)S(1)} %bitcast.17), channel_id=1, replica_groups=mesh['y'=4,'zh'=4,'zl'=4,'core'=2,'x'=4] {'core'}, dimensions={0} | all-to-all | bytes 2359296 | tf_op jit(solution)/shard_map/all_to_all | solution.py:20
  34.6 12.1 %all_to_all.61 = bf16[4,48,1536]{2,1,0:T(8,128)(2,1)S(1)} all-to-all(bf16[4,48,1536]{2,1,0:T(8,128)(2,1)S(1)} %bitcast.15), channel_id=1, replica_groups=mesh['y'=4,'zh'=4,'zl'=4,'core'=2,'x'=4] {'y'}, dimensions={0} | all-to-all | bytes 1179648 | tf_op jit(solution)/shard_map/all_to_all | solution.py:20
  46.8 8.2 %all_to_all.62 = bf16[4,12,1536]{2,1,0:T(8,128)(2,1)S(1)} all-to-all(bf16[4,12,1536]{2,1,0:T(8,128)(2,1)S(1)} %reshape.36), channel_id=1, replica_groups=mesh['y'=4,'zh'=4,'zl'=4,'core'=2,'x'=4] {'zl'}, dimensions={0} | all-to-all | bytes 294912 | tf_op jit(solution)/shard_map/all_to_all | solution.py:20
  55.0 0.7 broadcast_in_dim.31
  55.7 11.5 %all-to-all-start.3 = ((bf16[4,12,1536]{2,1,0:T(8,128)(2,1)}), bf16[4,12,1536]{2,1,0:T(8,128)(2,1)S(1)}, u32[]{:S(2)}, u32[]{:S(2)}) async-start(bf16[4,12,1536]{2,1,0:T(8,128)(2,1)} %broadcast_in_dim.31), calls=%async_computation.3 | async-start | bytes 393216 | tf_op jit(solution)/shard_map/all_to_all | solution.py:20
  67.2 8.5 %all-gather.4.cloned.1.call-done = bf16[1536,1536]{1,0:T(8,128)(2,1)} async-done(((bf16[1536,384]{1,0:T(8,128)(2,1)}), bf16[1536,1536]{1,0:T(8,128)(2,1)}) %all-gather.4.cloned.1.call-update) | async-done | bytes 4718608 | tf_op jit(solution)/shard_map/all_gather | solution.py:120
  75.7 6.0 %convolution_convert_fusion.own_map = bf16[1536,384]{1,0:T(8,128)(2,1)} fusion(bf16[1536,1536]{1,0:T(8,128)(2,1)} %all-gather.4.cloned.1.call-done, bf16[1536,384]{1,0:T(8,128)(2,1)S(1)} %copy-done), kind=kOutput, calls=%fused_computation.2 | convolution fusion | flops 1812529152 | bytes 7077888 | tf_op jit(solution)/shard_map/dot_general | solution.py:45
  81.7 2.8 %shard_map.60 = bf16[384,384]{1,0:T(8,128)(2,1)} custom-call(bf16[256,1536]{1,0:T(8,128)(2,1)} %copy-done.4, bf16[1536,384]{1,0:T(8,128)(2,1)} %convolution_convert_fusion.own_map), custom_call_target="tpu_custom_call" | custom-call | flops 301989888 | bytes 1966080 | tf_op jit(solution)/shard_map/pallas_call | solution.py:141
  84.6 8.3 %all_to_all.63 = bf16[4,12,1536]{2,1,0:T(8,128)(2,1)S(1)} all-to-all(bf16[4,12,1536]{2,1,0:T(8,128)(2,1)S(1)} %broadcast_in_dim.32), channel_id=1, replica_groups=mesh['y'=4,'zh'=4,'zl'=4,'core'=2,'x'=4] {'x'}, dimensions={0} | all-to-all | bytes 294912 | tf_op jit(solution)/shard_map/all_to_all | solution.py:20
  93.0 0.3 convolution_convert_fusion.1
  93.3 6.7 %all_to_all.64 = bf16[4,12,384]{2,1,0:T(8,128)(2,1)S(1)} all-to-all(bf16[4,12,384]{2,1,0:T(8,128)(2,1)S(1)} %reshape.38), channel_id=1, replica_groups=mesh['y'=4,'zh'=4,'zl'=4,'core'=2,'x'=4] {'x'}, dimensions={0} | all-to-all | bytes 73728 | tf_op jit(solution)/shard_map/all_to_all | solution.py:20
  100.2 10.0 %all_to_all.65 = bf16[4,4,12,384]{3,1,2,0:T(4,128)(2,1)S(1)} all-to-all(bf16[4,4,12,384]{3,1,2,0:T(4,128)(2,1)S(1)} %broadcast_in_dim.33), channel_id=1, replica_groups=mesh['y'=4,'zh'=4,'zl'=4,'core'=2,'x'=4] {'zl'}, dimensions={0} | all-to-all | bytes 294912 | tf_op jit(solution)/shard_map/all_to_all | solution.py:20
  110.3 11.1 %all_to_all.66 = bf16[4,4,48,384]{3,2,1,0:T(8,128)(2,1)S(1)} all-to-all(bf16[4,4,48,384]{3,2,1,0:T(8,128)(2,1)S(1)} %broadcast_in_dim.63), channel_id=1, replica_groups=mesh['y'=4,'zh'=4,'zl'=4,'core'=2,'x'=4] {'y'}, dimensions={0} | all-to-all | bytes 1179648 | tf_op jit(solution)/shard_map/all_to_all | solution.py:20
  121.5 10.4 %all_to_all.67.sym = bf16[2,4,4,48,384]{4,3,2,1,0:T(8,128)(2,1)S(1)} all-to-all(bf16[2,4,4,48,384]{4,3,2,1,0:T(8,128)(2,1)S(1)} %broadcast_in_dim.64), channel_id=1, replica_groups=mesh['y'=4,'zh'=4,'zl'=4,'core'=2,'x'=4] {'core'}, dimensions={0} | all-to-all | bytes 2359296 | tf_op jit(solution)/shard_map/all_to_all | solution.py:20
  131.9 2.0 %shard_map.61 = bf16[4,256,384]{2,1,0:T(8,128)(2,1)S(1)} custom-call(s32[1]{0:T(128)} %bitcast.place, f32[256,384]{1,0:T(8,128)S(1)} %copy-done.2, bf16[2,4,4,48,384]{4,3,2,1,0:T(8,128)(2,1)S(1)} %all_to_all.67.sym, bf16[4,384,384]{2,1,0:T(8,128)(2,1)S(1)} %bitcast.16, bf16[1536,384]{1,0:T(8,128)(2,1)S(1)} %copy-done.1), custom_call_target="tpu_custom_call" | custom-call | tf_op jit(solution)/shard_map/pallas_call | solution.py:166
  133.9 14.4 %all_to_all.68.shares = bf16[4,256,384]{2,1,0:T(8,128)(2,1)S(1)} all-to-all(bf16[4,256,384]{2,1,0:T(8,128)(2,1)S(1)} %shard_map.61), channel_id=1, replica_groups=mesh['y'=4,'zh'=4,'zl'=4,'core'=2,'x'=4] {'x'}, dimensions={0} | all-to-all | bytes 1572864 | tf_op jit(solution)/shard_map/all_to_all | solution.py:20
  148.6 11.8 %all_to_all.69 = f32[32,8,128]{2,1,0:T(8,128)S(1)} all-to-all(f32[32,8,128]{2,1,0:T(8,128)S(1)} %broadcast_in_dim.65), channel_id=1, replica_groups=mesh['y'=4,'zh'=4,'zl'=4,'core'=2,'x'=4] {'y','core','x'}, dimensions={0} | all-to-all | bytes 262144 | tf_op jit(solution)/shard_map/all_to_all | solution.py:20
  160.5 21.1 %all_to_all.70.sums = f32[16,8,128]{2,1,0:T(8,128)S(1)} all-to-all(f32[16,8,128]{2,1,0:T(8,128)S(1)} %broadcast_in_dim.66), channel_id=1, replica_groups=mesh['y'=4,'zh'=4,'zl'=4,'core'=2,'x'=4] {'zh','zl'}, dimensions={0} | all-to-all | bytes 131072 | tf_op jit(solution)/shard_map/all_to_all | solution.py:20
  181.6 1.0 shard_map.63
  (34 shorter events, 1.1 us)
Async XLA Ops:
  7.2 68.6 %copy-start = (bf16[1536,384]{1,0:T(8,128)(2,1)S(1)}, bf16[1536,384]{1,0:T(8,128)(2,1)}, u32[]{:S(2)}) copy-start(bf16[1536,384]{1,0:T(8,128)(2,1)} %param.6) | copy-start | bytes 3538948
  7.2 1.0 copy-start.5
  7.2 13.9 %copy-start.2 = (f32[256,384]{1,0:T(8,128)S(1)}, f32[256,384]{1,0:T(8,128)}, u32[]{:S(2)}) copy-start(f32[256,384]{1,0:T(8,128)} %vec.5) | copy-start | bytes 1179652
  7.2 68.5 %all-gather.4.cloned.1.call-start = ((), (), s32[]{:S(2)}) async-start(), calls=%async_computation.12 | async-start | bytes 5898240 | tf_op jit(solution)/shard_map/all_gather | solution.py:120
  21.1 0.9 copy-start.4
  55.7 28.9 %all-to-all-start.3 = ((bf16[4,12,1536]{2,1,0:T(8,128)(2,1)}), bf16[4,12,1536]{2,1,0:T(8,128)(2,1)S(1)}, u32[]{:S(2)}, u32[]{:S(2)}) async-start(bf16[4,12,1536]{2,1,0:T(8,128)(2,1)} %broadcast_in_dim.31), calls=%async_computation.3 | async-start | bytes 393216 | tf_op jit(solution)/shard_map/all_to_all | solution.py:20
  67.2 54.2 %all-gather.6.cloned.1.call-start = ((), (), s32[]{:S(2)}) async-start(), calls=%async_computation.13 | async-start | bytes 1474560 | tf_op jit(solution)/shard_map/all_gather | solution.py:157
  84.5 8.4 %copy-start.1 = (bf16[1536,384]{1,0:T(8,128)(2,1)S(1)}, bf16[1536,384]{1,0:T(8,128)(2,1)}, u32[]{:S(2)}) copy-start(bf16[1536,384]{1,0:T(8,128)(2,1)} %convolution_convert_fusion.own_map) | copy-start | bytes 3538948
  121.5 10.4 %copy-start.3 = (bf16[1536,384]{1,0:T(8,128)(2,1)S(1)}, bf16[1536,384]{1,0:T(8,128)(2,1)}, u32[]{:S(2)}) copy-start(bf16[1536,384]{1,0:T(8,128)(2,1)} %all-gather.6.cloned.1.call-done) | copy-start | bytes 3538948
Sparse Core Ops, SparseCore 0:
  10.2 65.5 all-gather.3
  84.7 31.6 all-gather.5

commit v14 on v11

--- a/solution.py
+++ b/solution.py
@@ -176,8 +176,8 @@
         out_specs=(VMEM, VMEM),
         compiler_params=PARAMS,
     )(vector, shares)
-    sums = total(spread(sums, ("y", "core", "x")))
-    sums = spread(sums, ("zh", "zl"))
+    sums = total(spread(sums, ("zh", "zl")))
+    sums = spread(sums, ("y", "core", "x"))
     return pl.pallas_call(
         functools.partial(finish_kernel, float(rows_total * bond)),
         out_shape=(

time: 188 us -> 190 us (1.011)
  blocking collectives: 139 us -> 141 us
where the time goes in v14:
time: 190 us; the launch traced here: 189 us
  blocking collectives  141 us (74%)
  between operations  14.2 us (7%)
  starting transfers between devices  11.5 us (6%)
  waiting for transfers between devices  9.57 us (5%)
  matrix products  5.77 us (3%)
  Pallas kernels  3.89 us (2%)
  local copies, waits for them, and re-layouts  2.05 us (1%)
    all_to_all x11, blocking collectives, swap(): return lax.all_to_all(pieces, axis, split_axis=0, concat_axis=0, tiled=True)  128 us
    all_gather x1, blocking collectives, on_device(): edge_wide = lax.all_gather(edge, 'x', axis=1, tiled=True)  12.9 us
    all_to_all x1, starting transfers between devices, swap(): return lax.all_to_all(pieces, axis, split_axis=0, concat_axis=0, tiled=True)  11.5 us
    all_gather x1, waiting for transfers between devices, on_device(): corner_wide = lax.all_gather(corner, 'x', axis=1, tiled=True)  8.87 us
    dot_general x2, matrix products, dot(): return jnp.dot(a, b, preferred_element_type=F32)  5.25 us
  transfers between devices with their start and end apart: 3, of which 1 were waited for; matrix products, arithmetic and copies ran while one was open for 4% of the time, Pallas kernels for 0%

profile of v14, /device:TPU:1, one launch (start us, length us, event | category | flops | bytes accessed | tf_op | source)
XLA Modules:
  0.0 189.2 jit_solution(6930783400481554487)
XLA Ops:
  7.2 0.7 all-gather.4.cloned.1.call-update
  8.2 12.9 %all_gather.12.edge = bf16[256,1536]{1,0:T(8,128)(2,1)S(1)} all-gather(bf16[256,384]{1,0:T(8,128)(2,1)S(1)} %copy-done.4), channel_id=1, replica_groups=mesh['y'=4,'zh'=4,'zl'=4,'core'=2,'x'=4] {'x'}, dimensions={1}, use_global_device_ids=true | all-gather | bytes 983040 | tf_op jit(solution)/shard_map/all_gather | solution.py:120
  21.1 0.5 fusion
  21.7 12.4 %all_to_all.60.pieces = bf16[2,192,1536]{2,1,0:T(8,128)(2,1)S(1)} all-to-all(bf16[2,192,1536]{2,1,0:T(8,128)(2,1)S(1)} %bitcast.17), channel_id=1, replica_groups=mesh['y'=4,'zh'=4,'zl'=4,'core'=2,'x'=4] {'core'}, dimensions={0} | all-to-all | bytes 2359296 | tf_op jit(solution)/shard_map/all_to_all | solution.py:19
  34.2 12.1 %all_to_all.61 = bf16[4,48,1536]{2,1,0:T(8,128)(2,1)S(1)} all-to-all(bf16[4,48,1536]{2,1,0:T(8,128)(2,1)S(1)} %bitcast.15), channel_id=1, replica_groups=mesh['y'=4,'zh'=4,'zl'=4,'core'=2,'x'=4] {'y'}, dimensions={0} | all-to-all | bytes 1179648 | tf_op jit(solution)/shard_map/all_to_all | solution.py:19
  46.4 8.2 %all_to_all.62 = bf16[4,12,1536]{2,1,0:T(8,128)(2,1)S(1)} all-to-all(bf16[4,12,1536]{2,1,0:T(8,128)(2,1)S(1)} %reshape.36), channel_id=1, replica_groups=mesh['y'=4,'zh'=4,'zl'=4,'core'=2,'x'=4] {'zl'}, dimensions={0} | all-to-all | bytes 294912 | tf_op jit(solution)/shard_map/all_to_all | solution.py:19
  54.7 0.7 broadcast_in_dim.31
  55.4 11.5 %all-to-all-start.3 = ((bf16[4,12,1536]{2,1,0:T(8,128)(2,1)}), bf16[4,12,1536]{2,1,0:T(8,128)(2,1)}, u32[]{:S(2)}, u32[]{:S(2)}) async-start(bf16[4,12,1536]{2,1,0:T(8,128)(2,1)} %broadcast_in_dim.31), calls=%async_computation.3 | async-start | bytes 393216 | tf_op jit(solution)/shard_map/all_to_all | solution.py:19
  66.9 8.9 %all-gather.4.cloned.1.call-done = bf16[1536,1536]{1,0:T(8,128)(2,1)} async-done(((bf16[1536,384]{1,0:T(8,128)(2,1)}), bf16[1536,1536]{1,0:T(8,128)(2,1)}) %all-gather.4.cloned.1.call-update) | async-done | bytes 4718608 | tf_op jit(solution)/shard_map/all_gather | solution.py:119
  75.7 4.9 %convolution_convert_fusion.own_map = bf16[1536,384]{1,0:T(8,128)(2,1)S(1)} fusion(bf16[1536,1536]{1,0:T(8,128)(2,1)} %all-gather.4.cloned.1.call-done, bf16[1536,384]{1,0:T(8,128)(2,1)S(1)} %copy-done), kind=kOutput, calls=%fused_computation.2 | convolution fusion | flops 1812529152 | bytes 7077888 | tf_op jit(solution)/shard_map/dot_general | solution.py:44
  80.7 0.6 shard_map.60
  81.3 0.7 copy-done.2
  82.0 1.0 reduce_sum.47
  83.0 8.2 %all_to_all.63 = bf16[4,12,1536]{2,1,0:T(8,128)(2,1)S(1)} all-to-all(bf16[4,12,1536]{2,1,0:T(8,128)(2,1)S(1)} %broadcast_in_dim.32), channel_id=1, replica_groups=mesh['y'=4,'zh'=4,'zl'=4,'core'=2,'x'=4] {'x'}, dimensions={0} | all-to-all | bytes 294912 | tf_op jit(solution)/shard_map/all_to_all | solution.py:19
  91.2 0.3 convolution_convert_fusion.1
  91.5 6.7 %all_to_all.64 = bf16[4,12,384]{2,1,0:T(8,128)(2,1)S(1)} all-to-all(bf16[4,12,384]{2,1,0:T(8,128)(2,1)S(1)} %reshape.38), channel_id=1, replica_groups=mesh['y'=4,'zh'=4,'zl'=4,'core'=2,'x'=4] {'x'}, dimensions={0} | all-to-all | bytes 73728 | tf_op jit(solution)/shard_map/all_to_all | solution.py:19
  98.4 10.0 %all_to_all.65 = bf16[4,4,12,384]{3,1,2,0:T(4,128)(2,1)S(1)} all-to-all(bf16[4,4,12,384]{3,1,2,0:T(4,128)(2,1)S(1)} %broadcast_in_dim.33), channel_id=1, replica_groups=mesh['y'=4,'zh'=4,'zl'=4,'core'=2,'x'=4] {'zl'}, dimensions={0} | all-to-all | bytes 294912 | tf_op jit(solution)/shard_map/all_to_all | solution.py:19
  108.5 11.1 %all_to_all.66 = bf16[4,4,48,384]{3,2,1,0:T(8,128)(2,1)S(1)} all-to-all(bf16[4,4,48,384]{3,2,1,0:T(8,128)(2,1)S(1)} %broadcast_in_dim.63), channel_id=1, replica_groups=mesh['y'=4,'zh'=4,'zl'=4,'core'=2,'x'=4] {'y'}, dimensions={0} | all-to-all | bytes 1179648 | tf_op jit(solution)/shard_map/all_to_all | solution.py:19
  119.7 10.8 %all_to_all.67.sym = bf16[2,4,4,48,384]{4,3,2,1,0:T(8,128)(2,1)S(1)} all-to-all(bf16[2,4,4,48,384]{4,3,2,1,0:T(8,128)(2,1)S(1)} %broadcast_in_dim.64), channel_id=1, replica_groups=mesh['y'=4,'zh'=4,'zl'=4,'core'=2,'x'=4] {'core'}, dimensions={0} | all-to-all | bytes 2359296 | tf_op jit(solution)/shard_map/all_to_all | solution.py:19
  130.5 2.0 %shard_map.61 = bf16[4,256,384]{2,1,0:T(8,128)(2,1)S(1)} custom-call(s32[1]{0:T(128)} %bitcast.place, f32[256,384]{1,0:T(8,128)S(1)} %copy-done.1, bf16[2,4,4,48,384]{4,3,2,1,0:T(8,128)(2,1)S(1)} %all_to_all.67.sym, bf16[4,384,384]{2,1,0:T(8,128)(2,1)S(1)} %bitcast.16, bf16[1536,384]{1,0:T(8,128)(2,1)S(1)} %convolution_convert_fusion.own_map), custom_call_target="tpu_custom_call" | custom-call | tf_op jit(solution)/shard_map/pallas_call | solution.py:161
  132.5 14.4 %all_to_all.68.shares = bf16[4,256,384]{2,1,0:T(8,128)(2,1)S(1)} all-to-all(bf16[4,256,384]{2,1,0:T(8,128)(2,1)S(1)} %shard_map.61), channel_id=1, replica_groups=mesh['y'=4,'zh'=4,'zl'=4,'core'=2,'x'=4] {'x'}, dimensions={0} | all-to-all | bytes 1572864 | tf_op jit(solution)/shard_map/all_to_all | solution.py:19
  147.2 20.9 %all_to_all.69 = f32[16,8,128]{2,1,0:T(8,128)S(1)} all-to-all(f32[16,8,128]{2,1,0:T(8,128)S(1)} %broadcast_in_dim.65), channel_id=1, replica_groups=mesh['y'=4,'zh'=4,'zl'=4,'core'=2,'x'=4] {'zh','zl'}, dimensions={0} | all-to-all | bytes 131072 | tf_op jit(solution)/shard_map/all_to_all | solution.py:19
  168.1 13.2 %all_to_all.70.sums = f32[32,8,128]{2,1,0:T(8,128)S(1)} all-to-all(f32[32,8,128]{2,1,0:T(8,128)S(1)} %broadcast_in_dim.66), channel_id=1, replica_groups=mesh['y'=4,'zh'=4,'zl'=4,'core'=2,'x'=4] {'y','core','x'}, dimensions={0} | all-to-all | bytes 262144 | tf_op jit(solution)/shard_map/all_to_all | solution.py:19
  181.3 1.0 shard_map.63
  (32 shorter events, 1.3 us)
Async XLA Ops:
  7.2 68.6 %copy-start = (bf16[1536,384]{1,0:T(8,128)(2,1)S(1)}, bf16[1536,384]{1,0:T(8,128)(2,1)}, u32[]{:S(2)}) copy-start(bf16[1536,384]{1,0:T(8,128)(2,1)} %param.6) | copy-start | bytes 3538948
  7.2 1.0 copy-start.4
  7.2 13.9 %copy-start.1 = (f32[256,384]{1,0:T(8,128)S(1)}, f32[256,384]{1,0:T(8,128)}, u32[]{:S(2)}) copy-start(f32[256,384]{1,0:T(8,128)} %vec.5) | copy-start | bytes 1179652
  7.2 68.5 %all-gather.4.cloned.1.call-start = ((), (), s32[]{:S(2)}) async-start(), calls=%async_computation.12 | async-start | bytes 5898240 | tf_op jit(solution)/shard_map/all_gather | solution.py:119
  55.4 26.7 %all-to-all-start.3 = ((bf16[4,12,1536]{2,1,0:T(8,128)(2,1)}), bf16[4,12,1536]{2,1,0:T(8,128)(2,1)}, u32[]{:S(2)}, u32[]{:S(2)}) async-start(bf16[4,12,1536]{2,1,0:T(8,128)(2,1)} %broadcast_in_dim.31), calls=%async_computation.3 | async-start | bytes 393216 | tf_op jit(solution)/shard_map/all_to_all | solution.py:19
  66.9 52.7 %all-gather.6.cloned.1.call-start = ((), (), s32[]{:S(2)}) async-start(), calls=%async_computation.13 | async-start | bytes 1474560 | tf_op jit(solution)/shard_map/all_gather | solution.py:152
  81.3 0.7 copy-start.2
  119.7 10.8 %copy-start.3 = (bf16[1536,384]{1,0:T(8,128)(2,1)S(1)}, bf16[1536,384]{1,0:T(8,128)(2,1)}, u32[]{:S(2)}) copy-start(bf16[1536,384]{1,0:T(8,128)(2,1)} %all-gather.6.cloned.1.call-done) | copy-start | bytes 3538948
Sparse Core Ops, SparseCore 0:
  10.2 65.5 all-gather.3
  82.1 31.8 all-gather.5
